TPU v7x, 32 devices: a whole 2x2x4 slice. The times are simulated.
32 devices in a mesh: seq: 8 (over z, y), batch: 4 (over x, core).
Axes of the slice: x: 2, y: 2, z: 4, core: 2. Of those that a mesh axis runs over, the one named last changes fastest.
Arguments:
- hidden: bfloat16 [4, 1024, 2048], P('batch', 'seq'), may hold values from -6 to 6
- segments: int32 [4, 1024], P('batch', 'seq'), may hold values from 0 to 3, as said below
- routes: int32 [4, 1024, 8], P('batch', 'seq'), may hold values from 0 to 63, all different within a row; in each aligned block of 128 rows (0 to 127, 128 to 255, ..., all dimensions but the last counted through in order) at most 32 rows name the same one
- w_in: bfloat16 [2048, 6144], P(('seq', 'batch')), may hold values from -0.125 to 0.125
- w_out: bfloat16 [2048, 2048], P(('seq', 'batch')), may hold values from -2 to 2
- w_router: bfloat16 [2048, 64], P(('seq', 'batch')), may hold values from -0.0625 to 0.0625
- gains: bfloat16 [4, 2048], P(None, ('seq', 'batch')), may hold values from 0.5 to 1.5
- w_expert: bfloat16 [64, 3, 2048, 1024], P('seq', None, None, 'batch')
- cotangent: bfloat16 [4, 1024, 2048], P('batch', 'seq'), may hold values from -6 to 6
Outputs:
- output: bfloat16 [4, 1024, 2048], P('batch', 'seq')
- input_grad: float32 [4, 1024, 2048], P('batch', 'seq')
- w_in_grad: float32 [2048, 6144], P(('seq', 'batch'))
- w_out_grad: float32 [2048, 2048], P(('seq', 'batch'))
- w_router_grad: float32 [2048, 64], P(('seq', 'batch'))
- gains_grad: float32 [4, 2048], P(None, ('seq', 'batch'))
- w_expert_grad: float32 [64, 3, 2048, 1024], P('seq', None, None, 'batch')
Inputs may be any that keep to these rules, and one draw needn't show every extreme that they name: `segments`: ids never fall along a sequence and start at 0; in one sequence, chosen by the seed, all are 0; every other sequence ends at 3. `routes`: in the 128 rows of one device (aligned blocks) no expert is named more than 32 times, and in some device's rows some expert is named exactly 32 times.
All inputs are finite; a program needn't handle non-finite values.
Results may differ from a plain program's by a relative error of at most 0.025.
Values may be sent and summed in bfloat16 or wider, within the bound.
A program may use at most 448 MiB of HBM per device.

v0:
```python
import jax
import jax.numpy as jnp
from jax import lax
from jax.sharding import PartitionSpec as P

HEADS = 16
CAP = 32


epsilon = 1e-05


def rms_scale(values):
    return lax.rsqrt(jnp.mean(values * values, axis=-1, keepdims=True) + epsilon)


def rotate_half(values):
    half = values.shape[-1] // 2
    return jnp.concatenate([-values[..., half:], values[..., :half]], axis=-1)


def rope_tables(positions, head_size):
    steps = jnp.arange(head_size // 2, dtype=jnp.float32)
    freqs = jnp.exp(steps * (-2.0 * jnp.log(10000.0) / head_size))
    angles = positions.astype(jnp.float32)[:, None] * freqs[None, :]
    angles = jnp.concatenate([angles, angles], axis=-1)
    return (jnp.cos(angles)[:, None, :], jnp.sin(angles)[:, None, :])


def norm_back(grad_out, normal, scale, gain):
    scaled = grad_out * gain
    return scale * (scaled - normal * jnp.mean(scaled * normal, axis=-1, keepdims=True))


def local(hidden, segments, routes, w_in, w_out, w_router, gains, w_expert, cotangent):
    rows = hidden.shape[1]
    width = hidden.shape[2]
    heads = HEADS
    head_size = width // heads
    scale = head_size ** (-0.5)
    top = routes.shape[2]
    capacity = CAP
    seq_count = lax.axis_size("seq")
    place = lax.axis_index("seq")
    local_experts = w_expert.shape[0]
    expert_count = local_experts * seq_count
    in_all, out_all, router_all, gains_all = (
        lax.all_gather(w_in, ("seq", "batch"), axis=0, tiled=True),
        lax.all_gather(w_out, ("seq", "batch"), axis=0, tiled=True),
        lax.all_gather(w_router, ("seq", "batch"), axis=0, tiled=True),
        lax.all_gather(gains.T, ("seq", "batch"), axis=0, tiled=True),
    )
    gains_wide = gains_all.astype(jnp.float32)
    attn_gain = gains_wide[:, 0]
    query_gain = gains_wide[:, 1]
    key_gain = gains_wide[:, 2]
    ffn_gain = gains_wide[:, 3]
    inputs = hidden[0].astype(jnp.float32)
    first_scale = rms_scale(inputs)
    first_normal = inputs * first_scale
    normed = (first_normal * attn_gain).astype(jnp.bfloat16)
    projected = jnp.dot(normed, in_all, preferred_element_type=jnp.float32)
    query_raw = projected[:, :width]
    key_raw = projected[:, width : 2 * width]
    value_raw = projected[:, 2 * width :]
    query_scale = rms_scale(query_raw)
    query_normal = query_raw * query_scale
    key_scale = rms_scale(key_raw)
    key_normal = key_raw * key_scale
    positions = place * rows + jnp.arange(rows, dtype=jnp.int32)
    cosine, sine = rope_tables(positions, head_size)
    query_pre = (query_normal * query_gain).reshape(rows, heads, head_size)
    key_pre = (key_normal * key_gain).reshape(rows, heads, head_size)
    query_heads = (query_pre * cosine + rotate_half(query_pre) * sine).astype(jnp.bfloat16)
    key_flat = (
        (key_pre * cosine + rotate_half(key_pre) * sine).astype(jnp.bfloat16).reshape(rows, width)
    )
    value_flat = value_raw.astype(jnp.bfloat16)
    segment_values = segments[0].astype(jnp.bfloat16)
    running_top = jnp.full((heads, rows), -1e30, jnp.float32)
    piece_key = lax.all_gather(key_flat, "seq", axis=0, tiled=True)
    piece_value = lax.all_gather(value_flat, "seq", axis=0, tiled=True)
    piece_segment = lax.all_gather(segment_values, "seq", axis=0, tiled=True)
    count = piece_key.shape[0]
    key_three = piece_key.reshape(count, heads, head_size)
    value_three = piece_value.reshape(count, heads, head_size)
    scores = (
        jnp.einsum("qhd,khd->hqk", query_heads, key_three, preferred_element_type=jnp.float32)
        * scale
    )
    key_positions = jnp.arange(count, dtype=jnp.int32)
    allowed = (key_positions[None, :] <= positions[:, None]) & (
        piece_segment[None, :] == segment_values[:, None]
    )
    scores = jnp.where(allowed[None], scores, -jnp.inf)
    new_top = jnp.maximum(running_top, jnp.max(scores, axis=-1))
    weights = jnp.exp(scores - new_top[..., None])
    new_total = jnp.sum(weights, axis=-1)
    new_acc = jnp.einsum(
        "hqk,khd->hqd",
        weights.astype(jnp.bfloat16),
        value_three,
        preferred_element_type=jnp.float32,
    )
    attended = new_acc / new_total[..., None]
    log_total = new_top + jnp.log(new_total)
    attended_rows = jnp.transpose(attended, (1, 0, 2))
    attn_low = attended_rows.reshape(rows, width).astype(jnp.bfloat16)
    middle = inputs + jnp.dot(attn_low, out_all, preferred_element_type=jnp.float32)
    second_scale = rms_scale(middle)
    second_normal = middle * second_scale
    ffn_in = (second_normal * ffn_gain).astype(jnp.bfloat16)
    logits = jnp.dot(ffn_in, router_all, preferred_element_type=jnp.float32)
    router = jax.nn.softmax(logits, axis=-1)
    chosen = routes[0]
    expert_hot = chosen[..., None] == jnp.arange(expert_count, dtype=jnp.int32)
    gates = jnp.sum(jnp.where(expert_hot, router[:, None, :], 0.0), axis=-1)
    pair_expert = chosen.reshape(rows * top)
    pair_hot = (pair_expert[:, None] == jnp.arange(expert_count, dtype=jnp.int32)[None, :]).astype(
        jnp.int32
    )
    rank = jnp.cumsum(pair_hot, axis=0, dtype=jnp.int32) - pair_hot
    slot = jnp.sum(rank * pair_hot, axis=1)
    target = pair_expert * capacity + slot
    source = (
        jnp.full((expert_count * capacity,), rows * top, jnp.int32)
        .at[target]
        .set(jnp.arange(rows * top, dtype=jnp.int32))
    )
    padded_in = jnp.concatenate([ffn_in, jnp.zeros((1, width), jnp.bfloat16)], axis=0)
    send_rows = padded_in[source // top].reshape(seq_count, local_experts, capacity, width)
    full_expert = lax.all_gather(w_expert, "batch", axis=3, tiled=True)
    slot_rows = lax.all_to_all(send_rows, "seq", split_axis=0, concat_axis=0, tiled=True)
    gate = jnp.einsum(
        "secd,edf->secf", slot_rows, full_expert[:, 0], preferred_element_type=jnp.float32
    )
    up_part = jnp.einsum(
        "secd,edf->secf", slot_rows, full_expert[:, 1], preferred_element_type=jnp.float32
    )
    act = (jax.nn.silu(gate) * up_part).astype(jnp.bfloat16)
    result = jnp.einsum(
        "secf,edf->secd", act, full_expert[:, 2], preferred_element_type=jnp.float32
    )
    owner_out = result.astype(jnp.bfloat16)
    home_out = lax.all_to_all(owner_out, "seq", split_axis=0, concat_axis=0, tiled=True).reshape(
        expert_count * capacity, width
    )
    picked = home_out[target].reshape(rows, top, width).astype(jnp.float32)
    mixture = jnp.sum(gates[..., None] * picked, axis=1)
    output = middle + mixture
    grad_out = cotangent[0].astype(jnp.float32)
    gate_grad = jnp.sum(grad_out[:, None, :] * picked, axis=-1)
    pair_grad = (
        (gates[..., None] * grad_out[:, None, :]).astype(jnp.bfloat16).reshape(rows * top, width)
    )
    pair_grad = jnp.concatenate([pair_grad, jnp.zeros((1, width), jnp.bfloat16)], axis=0)
    send_grad = pair_grad[source].reshape(seq_count, local_experts, capacity, width)
    owner_grad = lax.all_to_all(send_grad, "seq", split_axis=0, concat_axis=0, tiled=True)
    weights_back = lax.all_gather(w_expert, "batch", axis=3, tiled=True)
    act_grad = jnp.einsum(
        "secd,edf->secf", owner_grad, weights_back[:, 2], preferred_element_type=jnp.float32
    )
    sigma = jax.nn.sigmoid(gate)
    silu_gate = gate * sigma
    gate_low = (act_grad * up_part * sigma * (1.0 + gate * (1.0 - sigma))).astype(jnp.bfloat16)
    up_low = (act_grad * silu_gate).astype(jnp.bfloat16)
    act_low = (jax.nn.silu(gate) * up_part).astype(jnp.bfloat16)
    expert_grad = jnp.stack(
        [
            jnp.einsum("secd,secf->edf", slot_rows, gate_low, preferred_element_type=jnp.float32),
            jnp.einsum("secd,secf->edf", slot_rows, up_low, preferred_element_type=jnp.float32),
            jnp.einsum("secd,secf->edf", owner_grad, act_low, preferred_element_type=jnp.float32),
        ],
        axis=1,
    )
    owner_input_grad = (
        jnp.einsum(
            "secf,edf->secd", gate_low, weights_back[:, 0], preferred_element_type=jnp.float32
        )
        + jnp.einsum(
            "secf,edf->secd", up_low, weights_back[:, 1], preferred_element_type=jnp.float32
        )
    ).astype(jnp.bfloat16)
    home_input_grad = lax.all_to_all(
        owner_input_grad, "seq", split_axis=0, concat_axis=0, tiled=True
    ).reshape(expert_count * capacity, width)
    expert_shard_grad = lax.psum_scatter(
        expert_grad.astype(jnp.bfloat16), "batch", scatter_dimension=3, tiled=True
    ).astype(jnp.float32)
    prob_grad = jnp.sum(jnp.where(expert_hot, gate_grad[..., None], 0.0), axis=1)
    logit_grad = router * (prob_grad - jnp.sum(router * prob_grad, axis=-1, keepdims=True))
    logit_low = logit_grad.astype(jnp.bfloat16)
    router_grad = jnp.einsum("td,te->de", ffn_in, logit_low, preferred_element_type=jnp.float32)
    ffn_in_grad = jnp.sum(
        home_input_grad[target].reshape(rows, top, width).astype(jnp.float32), axis=1
    )
    ffn_in_grad = ffn_in_grad + jnp.einsum(
        "te,de->td", logit_low, router_all, preferred_element_type=jnp.float32
    )
    ffn_gain_grad = jnp.sum(ffn_in_grad * second_normal, axis=0)
    middle_grad = grad_out + norm_back(ffn_in_grad, second_normal, second_scale, ffn_gain)
    middle_low = middle_grad.astype(jnp.bfloat16)
    out_weight_grad = jnp.einsum(
        "tc,td->cd", attn_low, middle_low, preferred_element_type=jnp.float32
    )
    attn_grad = jnp.einsum(
        "td,cd->tc", middle_low, out_all, preferred_element_type=jnp.float32
    ).astype(jnp.bfloat16)
    grad_heads = attn_grad.reshape(rows, heads, head_size)
    delta = jnp.transpose(jnp.sum(grad_heads.astype(jnp.float32) * attended_rows, axis=-1), (1, 0))
    all_key, all_value, all_segment = (
        lax.all_gather(key_flat, "seq", axis=0, tiled=True),
        lax.all_gather(value_flat, "seq", axis=0, tiled=True),
        lax.all_gather(segment_values, "seq", axis=0, tiled=True),
    )
    length = all_key.shape[0]
    block = min(512, length)
    block_count = length // block
    key_blocks = all_key.reshape(block_count, block, heads, head_size)
    value_blocks = all_value.reshape(block_count, block, heads, head_size)
    segment_blocks = all_segment.reshape(block_count, block)
    starts = jnp.arange(block_count, dtype=jnp.int32) * block

    def key_block_step(query_grad, item):
        key_three, value_three, block_segment, start = item
        scores = (
            jnp.einsum("qhd,khd->hqk", query_heads, key_three, preferred_element_type=jnp.float32)
            * scale
        )
        key_positions = start + jnp.arange(block, dtype=jnp.int32)
        allowed = (key_positions[None, :] <= positions[:, None]) & (
            block_segment[None, :] == segment_values[:, None]
        )
        probs_block = jnp.exp(jnp.where(allowed[None], scores, -jnp.inf) - log_total[..., None])
        prob_grad_block = jnp.einsum(
            "qhd,khd->hqk", grad_heads, value_three, preferred_element_type=jnp.float32
        )
        score_grad = (probs_block * (prob_grad_block - delta[..., None])).astype(jnp.bfloat16)
        query_grad = (
            query_grad
            + jnp.einsum("hqk,khd->qhd", score_grad, key_three, preferred_element_type=jnp.float32)
            * scale
        )
        key_grad = (
            jnp.einsum("hqk,qhd->khd", score_grad, query_heads, preferred_element_type=jnp.float32)
            * scale
        )
        value_grad = jnp.einsum(
            "hqk,qhd->khd",
            probs_block.astype(jnp.bfloat16),
            grad_heads,
            preferred_element_type=jnp.float32,
        )
        return (
            query_grad,
            jnp.concatenate(
                [key_grad.reshape(block, width), value_grad.reshape(block, width)], axis=1
            ),
        )

    query_grad, pair_terms = lax.scan(
        key_block_step,
        jnp.zeros((rows, heads, head_size), jnp.float32),
        (key_blocks, value_blocks, segment_blocks, starts),
    )
    kv_grad = lax.psum_scatter(
        pair_terms.reshape(length, 2 * width).astype(jnp.bfloat16),
        "seq",
        scatter_dimension=0,
        tiled=True,
    ).astype(jnp.float32)
    key_grad_own = kv_grad[:, :width].reshape(rows, heads, head_size)
    value_grad_own = kv_grad[:, width:]
    query_norm_grad = (query_grad * cosine - rotate_half(query_grad * sine)).reshape(rows, width)
    key_norm_grad = (key_grad_own * cosine - rotate_half(key_grad_own * sine)).reshape(rows, width)
    query_gain_grad = jnp.sum(query_norm_grad * query_normal, axis=0)
    key_gain_grad = jnp.sum(key_norm_grad * key_normal, axis=0)
    query_raw_grad = norm_back(query_norm_grad, query_normal, query_scale, query_gain)
    key_raw_grad = norm_back(key_norm_grad, key_normal, key_scale, key_gain)
    projected_grad = jnp.concatenate([query_raw_grad, key_raw_grad, value_grad_own], axis=1).astype(
        jnp.bfloat16
    )
    in_weight_grad = jnp.einsum(
        "td,tc->dc", normed, projected_grad, preferred_element_type=jnp.float32
    )
    normed_grad = jnp.einsum(
        "tc,dc->td", projected_grad, in_all, preferred_element_type=jnp.float32
    )
    attn_gain_grad = jnp.sum(normed_grad * first_normal, axis=0)
    input_grad = middle_grad + norm_back(normed_grad, first_normal, first_scale, attn_gain)
    gains_grad = jnp.stack([attn_gain_grad, query_gain_grad, key_gain_grad, ffn_gain_grad], axis=1)
    in_shard, out_shard, router_shard, gains_shard = (
        lax.psum_scatter(in_weight_grad, ("seq", "batch"), scatter_dimension=0, tiled=True),
        lax.psum_scatter(out_weight_grad, ("seq", "batch"), scatter_dimension=0, tiled=True),
        lax.psum_scatter(router_grad, ("seq", "batch"), scatter_dimension=0, tiled=True),
        lax.psum_scatter(gains_grad, ("seq", "batch"), scatter_dimension=0, tiled=True),
    )
    return (
        output.astype(jnp.bfloat16)[None],
        input_grad[None],
        in_shard,
        out_shard,
        router_shard,
        gains_shard.T,
        expert_shard_grad,
    )


def solution(mesh):
    placed = (
        P("batch", "seq", None),
        P("batch", "seq"),
        P("batch", "seq", None),
        P(("seq", "batch"), None),
        P(("seq", "batch"), None),
        P(("seq", "batch"), None),
        P(None, ("seq", "batch")),
        P("seq", None, None, "batch"),
        P("batch", "seq", None),
    )
    return jax.shard_map(
        local,
        mesh=mesh,
        in_specs=placed,
        out_specs=(
            P("batch", "seq", None),
            P("batch", "seq", None),
            P(("seq", "batch"), None),
            P(("seq", "batch"), None),
            P(("seq", "batch"), None),
            P(None, ("seq", "batch")),
            P("seq", None, None, "batch"),
        ),
        check_vma=False,
    )
```

profile of v0, /device:TPU:0, one launch (start us, length us, event | category | flops | bytes accessed | tf_op | source)
XLA Modules:
  0.0 3345.3 jit_solution(13950185177062536765)
XLA Ops:
  7.9 43.7 %all-gather.1 = bf16[32,64,4]{1,2,0:T(4,128)(2,1)S(1)} all-gather(bf16[1,64,4]{1,2,0:T(4,128)(2,1)} %bitcast.345), channel_id=1, replica_groups=mesh['seq'=8,'batch'=4] {'seq','batch'}, dimensions={0}, use_global_device_ids=true | all-gather | bytes 16896 | tf_op jit(solution)/shard_map/all_gather | solution.py:51
  53.1 115.2 %all-gather.8.cloned.1.call-done = bf16[2048,6144]{1,0:T(8,128)(2,1)} async-done(((bf16[64,6144]{1,0:T(8,128)(2,1)}), bf16[2048,6144]{1,0:T(8,128)(2,1)}) %all-gather.8.cloned.1.call-update) | async-done | bytes 25165840 | tf_op jit(solution)/shard_map/all_gather | solution.py:48
  168.3 10.2 fusion.94
  201.5 20.6 copy.238
  223.3 18.0 reduce-window.6
  241.7 18.4 all-gather
  260.4 4.5 scatter_custom_fusion
  265.2 6.5 copy.270
  271.7 54.1 %all-gather.10.cloned.1.call-done = bf16[1024,2048]{1,0:T(8,128)(2,1)} async-done(((bf16[128,2048]{1,0:T(8,128)(2,1)}), bf16[1024,2048]{1,0:T(8,128)(2,1)}) %all-gather.10.cloned.1.call-update) | async-done | bytes 4194320 | tf_op jit(solution)/shard_map/all_gather | solution.py:81
  325.8 4.0 fusion.43
  332.1 3.6 fusion.112
  335.7 68.7 %all-gather.14.cloned.1.call-done = bf16[2048,2048]{1,0:T(8,128)(2,1)} async-done(((bf16[64,2048]{1,0:T(8,128)(2,1)}), bf16[2048,2048]{1,0:T(8,128)(2,1)}) %all-gather.14.cloned.1.call-update) | async-done | bytes 8388624 | tf_op jit(solution)/shard_map/all_gather | solution.py:49
  404.4 4.7 multiply_reduce_fusion.7
  410.3 11.0 gather_fusion
  421.4 5.5 all-to-all-start
  426.9 199.0 %all_gather.34 = bf16[2048,64]{1,0:T(8,128)(2,1)S(1)} all-gather(bf16[64,64]{1,0:T(8,128)(2,1)S(1)} %copy-done.62), channel_id=1, replica_groups=mesh['seq'=8,'batch'=4] {'seq','batch'}, dimensions={0}, use_global_device_ids=true | all-gather | bytes 270336 | tf_op jit(solution)/shard_map/all_gather | solution.py:50
  630.8 19.1 gather_fusion.2
  649.9 17.3 all-to-all-start.2
  667.2 339.1 %all-gather.16.cloned.1.call-done = bf16[8,3,2048,1024]{3,2,0,1:T(8,128)(2,1)} async-done(((bf16[8,3,2048,256]{3,2,0,1:T(8,128)(2,1)}), bf16[8,3,2048,1024]{3,2,0,1:T(8,128)(2,1)}) %all-gather.16.cloned.1.call-update) | async-done | bytes 100663312 | tf_op jit(solution)/shard_map/all_gather | solution.py:132
  1006.3 19.4 fusion.24
  1025.7 19.4 fusion.26
  1045.1 25.1 fusion.35
  1070.2 20.3 fusion.23
  1090.4 22.7 fusion.31
  1113.1 8.4 copy.244
  1121.5 6.6 all-to-all-start.3
  1128.1 18.4 convert_bitcast_fusion
  1146.4 8.3 copy.241
  1154.8 156.9 %all-to-all-done.3 = bf16[8,8,32,2048]{3,2,1,0:T(8,128)(2,1)} async-done(((bf16[8,8,32,2048]{3,2,1,0:T(8,128)(2,1)}), bf16[8,8,32,2048]{3,2,1,0:T(8,128)(2,1)}, u32[]{:S(2)}, u32[]{:S(2)}) %all-to-all-start.3) | async-done | bytes 8388640 | tf_op jit(solution)/shard_map/all_to_all | solution.py:184
  1311.7 4.9 all-to-all-start.1
  1316.8 5.8 copy.282
  1322.6 3.4 copy.283
  1326.0 13.5 gather_fusion.3
  1339.4 6.0 convert_reduce_fusion
  1345.5 153.8 %all-to-all-done.1 = bf16[8,8,32,2048]{3,2,1,0:T(8,128)(2,1)} async-done(((bf16[8,8,32,2048]{3,2,1,0:T(8,128)(2,1)}), bf16[8,8,32,2048]{3,2,1,0:T(8,128)(2,1)}, u32[]{:S(2)}, u32[]{:S(2)}) %all-to-all-start.1) | async-done | bytes 8388640 | tf_op jit(solution)/shard_map/all_to_all | solution.py:145
  1499.4 13.4 gather_fusion.1
  1512.8 5.9 fusion.30
  1524.7 6.3 convolution_convert_fusion
  1532.7 51.9 %while.13 = (s32[]{:T(128)}, f32[128,16,128]{0,2,1:T(8,128)}, bf16[2,512,4096]{1,2,0:T(8,128)(2,1)}, bf16[2,512,16,128]{3,2,1,0:T(8,128)(2,1)}, s32[2]{0:T(128)S...) while((s32[]{:T(128)}, f32[128,16,128]{0,2,1:T(8,128)}, ...), condition=%wide.region_21.22_spmd.clone, body=%wide.region_20.21_spmd.clone.sunk | while | flops 1364263552 | bytes 79921648 | solution.py:261
  1532.9 2.9 constant_dynamic-slice_fusion.3
  1538.6 3.0 fusion.162
  1541.5 4.2 fusion.163
  1545.7 4.9 fusion.164
  1554.1 4.5 fusion.165
  1564.3 3.0 fusion.162
  1567.2 4.4 fusion.163
  1571.7 4.9 fusion.164
  1580.0 4.5 fusion.165
  1584.5 11.4 copy.250
  1596.0 18.5 fusion.22
  1614.6 18.5 fusion.21
  1633.0 18.2 fusion.20
  1651.2 92.0 %reduce-scatter.9.cloned.1.call-done = bf16[128,4096]{1,0:T(8,128)(2,1)} async-done(((bf16[1024,4096]{1,0:T(8,128)(2,1)}), bf16[128,4096]{1,0:T(8,128)(2,1)}) %reduce-scatter.9.cloned.1.call-update) | async-done | bytes 1048592 | tf_op jit(solution)/shard_map/reduce_scatter | solution.py:266
  1755.7 3.3 multiply_reduce_fusion.2
  1761.7 14.6 fusion.73
  1777.8 66.1 %pad_maximum_fusion = bf16[8,3,2048,1024]{3,2,0,1:T(8,128)(2,1)} fusion(bf16[8,1,2048,1024]{3,2,0,1:T(8,128)(2,1)} %fusion.22, bf16[8,1,2048,1024]{3,2,0,1:T(8,128)(2,1)} %fusion.21, bf16[8,1,2048,1024]{3,2,0,1:T(8,128)(2,1)} %fusion.20), kind=kLoop, calls=%fused_computation.35 | loop fusion | flops 100663296 | bytes 201326592 | tf_op jit(solution)/shard_map/stack | solution.py:168
  1846.4 8.1 fusion.89
  1856.0 19.6 fusion.82
  1878.2 33.6 %reduce-scatter.19.cloned.1.call-done = f32[64,4]{1,0:T(8,128)} async-done(((f32[2048,4]{1,0:T(8,128)}), f32[64,4]{1,0:T(8,128)}) %reduce-scatter.19.cloned.1.call-update) | async-done | bytes 1040
  1913.1 665.8 %reduce-scatter.17.cloned.1.call-done = bf16[8,3,2048,256]{3,2,0,1:T(8,128)(2,1)} async-done(((bf16[8,3,2048,1024]{3,2,0,1:T(8,128)(2,1)}), bf16[8,3,2048,256]{3,2,0,1:T(8,128)(2,1)}) %reduce-scatter.17.cloned.1.call-update) | async-done | bytes 25165840 | tf_op jit(solution)/shard_map/reduce_scatter | solution.py:187
  2579.0 27.2 copy.256
  2606.1 110.6 %reduce-scatter.15.cloned.1.call-done = f32[64,64]{1,0:T(8,128)} async-done(((f32[2048,64]{1,0:T(8,128)}), f32[64,64]{1,0:T(8,128)}) %reduce-scatter.15.cloned.1.call-update) | async-done | bytes 16400 | tf_op jit(solution)/shard_map/reduce_scatter | solution.py:295
  2716.7 181.5 %reduce-scatter.13.cloned.1.call-done = f32[64,2048]{1,0:T(8,128)} async-done(((f32[2048,2048]{1,0:T(8,128)}), f32[64,2048]{1,0:T(8,128)}) %reduce-scatter.13.cloned.1.call-update) | async-done | bytes 524304 | tf_op jit(solution)/shard_map/reduce_scatter | solution.py:294
  2898.3 440.3 %reduce-scatter.11.cloned.1.call-done = f32[64,6144]{1,0:T(8,128)} async-done(((f32[2048,6144]{1,0:T(8,128)}), f32[64,6144]{1,0:T(8,128)}) %reduce-scatter.11.cloned.1.call-update) | async-done | bytes 1572880 | tf_op jit(solution)/shard_map/reduce_scatter | solution.py:293
  (290 shorter events, 82.3 us)
Async XLA Ops:
  7.2 161.2 %all-gather.8.cloned.1.call-start = ((), (), s32[]{:S(2)}) async-start(), calls=%async_computation.10 | async-start | bytes 25952256 | tf_op jit(solution)/shard_map/all_gather | solution.py:48
  7.9 257.2 %all-gather.12.cloned.1.call-start = ((), (), s32[]{:S(2)}) async-start(), calls=%async_computation.12 | async-start | bytes 4718592 | tf_op jit(solution)/shard_map/all_gather | solution.py:82
  53.0 125.5 %copy-start.56 = (f32[128]{0:T(128)}, f32[128]{0:T(128)S(1)}, u32[]{:S(2)}) copy-start(f32[128]{0:T(128)S(1)} %add_rsqrt_fusion.3) | copy-start | bytes 1540
  53.1 125.5 %copy-start.39 = (f32[2048,1]{0,1:T(1,128)}, f32[2048,1]{0,1:T(1,128)S(1)}, u32[]{:S(2)}) copy-start(f32[2048,1]{0,1:T(1,128)S(1)} %get-tuple-element.311) | copy-start | bytes 24580
  53.1 130.8 %copy-start.43 = (f32[2048,1]{0,1:T(1,128)}, f32[2048,1]{0,1:T(1,128)S(1)}, u32[]{:S(2)}) copy-start(f32[2048,1]{0,1:T(1,128)S(1)} %get-tuple-element.309) | copy-start | bytes 24580
  53.1 130.8 %copy-start.45 = (f32[2048,1]{0,1:T(1,128)}, f32[2048,1]{0,1:T(1,128)S(1)}, u32[]{:S(2)}) copy-start(f32[2048,1]{0,1:T(1,128)S(1)} %get-tuple-element.310) | copy-start | bytes 24580
  53.1 356.1 %copy-start.47 = (f32[2048,1]{0,1:T(1,128)}, f32[2048,1]{0,1:T(1,128)S(1)}, u32[]{:S(2)}) copy-start(f32[2048,1]{0,1:T(1,128)S(1)} %get-tuple-element.308) | copy-start | bytes 24580
  178.6 13.3 copy-start.5
  179.6 146.2 %all-gather.10.cloned.1.call-start = ((), (), s32[]{:S(2)}) async-start(), calls=%async_computation.11 | async-start | bytes 4718592 | tf_op jit(solution)/shard_map/all_gather | solution.py:81
  180.0 13.4 copy-start.30
  180.0 13.4 copy-start.35
  195.9 129.9 %copy-start.2 = (bf16[128,16,128]{0,2,1:T(8,128)(2,1)}, bf16[128,16,128]{0,2,1:T(8,128)(2,1)S(1)}, u32[]{:S(2)}) copy-start(bf16[128,16,128]{0,2,1:T(8,128)(2,1)S(1)} %get-tuple-element.420) | copy-start | bytes 1572868
  200.8 203.6 %all-gather.14.cloned.1.call-start = ((), (), s32[]{:S(2)}) async-start(), calls=%async_computation.13 | async-start | bytes 8650752 | tf_op jit(solution)/shard_map/all_gather | solution.py:49
  201.4 804.9 %all-gather.16.cloned.1.call-start = ((), (), s32[]{:S(2)}) async-start(), calls=%async_computation.14 | async-start | bytes 125829120 | tf_op jit(solution)/shard_map/all_gather | solution.py:132
  222.1 19.6 copy-start.75
  241.7 88.1 %copy-start.58 = (bf16[128]{0:T(256)(128)(2,1)}, bf16[128]{0:T(256)(128)(2,1)S(1)}, u32[]{:S(2)}) copy-start(bf16[128]{0:T(256)(128)(2,1)S(1)} %get-tuple-element.419) | copy-start | bytes 772
  260.1 69.7 %copy-start.60 = (bf16[1024]{0:T(1024)(128)(2,1)}, bf16[1024]{0:T(1024)(128)(2,1)S(1)}, u32[]{:S(2)}) copy-start(bf16[1024]{0:T(1024)(128)(2,1)S(1)} %reduce.5) | copy-start | bytes 6148
  260.4 69.5 %copy-start.63 = (s32[1024,1]{0,1:T(1,128)}, s32[1024,1]{0,1:T(1,128)S(1)}, u32[]{:S(2)}) copy-start(s32[1024,1]{0,1:T(1,128)S(1)} %compare_select_fusion) | copy-start | bytes 12292
  332.1 72.3 %copy-start.12 = (bf16[1,128,2048]{2,1,0:T(8,128)(2,1)S(1)}, bf16[1,128,2048]{2,1,0:T(8,128)(2,1)}, u32[]{:S(2)}) copy-start(bf16[1,128,2048]{2,1,0:T(8,128)(2,1)} %param.11) | copy-start | bytes 1572868
  335.7 73.4 %copy-start.22 = (bf16[128,16,128]{0,2,1:T(8,128)(2,1)}, bf16[128,16,128]{0,2,1:T(8,128)(2,1)S(1)}, u32[]{:S(2)}) copy-start(bf16[128,16,128]{0,2,1:T(8,128)(2,1)S(1)} %get-tuple-element.320) | copy-start | bytes 1572868
  409.2 12.2 copy-start.73
  410.3 215.7 %copy-start.18 = (bf16[128,2048]{1,0:T(8,128)(2,1)}, bf16[128,2048]{1,0:T(8,128)(2,1)S(1)}, u32[]{:S(2)}) copy-start(bf16[128,2048]{1,0:T(8,128)(2,1)S(1)} %multiply_convert_fusion.2) | copy-start | bytes 1572868
  421.4 204.5 %copy-start.28 = (bf16[1,128,2048]{2,1,0:T(8,128)(2,1)S(1)}, bf16[1,128,2048]{2,1,0:T(8,128)(2,1)}, u32[]{:S(2)}) copy-start(bf16[1,128,2048]{2,1,0:T(8,128)(2,1)} %param.19) | copy-start | bytes 1572868
  421.4 228.5 %all-to-all-start = ((bf16[8,8,32,2048]{3,2,1,0:T(8,128)(2,1)}), bf16[8,8,32,2048]{3,2,1,0:T(8,128)(2,1)}, u32[]{:S(2)}, u32[]{:S(2)}) async-start(bf16[8,8,32,2048]{3,2,1,0:T(8,128)(2,1)} %bitcast.301), calls=%async_computation | async-start | bytes 16777216 | tf_op jit(solution)/shard_map/all_to_all | solution.py:133
  626.0 23.8 copy-start.16
  626.7 23.2 copy-start.65
  627.3 22.6 copy-start.67
  627.5 22.4 copy-start.37
  649.9 395.2 %all-to-all-start.2 = ((bf16[8,8,32,2048]{3,2,1,0:T(8,128)(2,1)}), bf16[8,8,32,2048]{3,2,1,0:T(8,128)(2,1)}, u32[]{:S(2)}, u32[]{:S(2)}) async-start(bf16[8,8,32,2048]{3,2,1,0:T(8,128)(2,1)} %bitcast.302), calls=%async_computation.2 | async-start | bytes 16777216 | tf_op jit(solution)/shard_map/all_to_all | solution.py:158
  1121.5 190.1 %all-to-all-start.3 = ((bf16[8,8,32,2048]{3,2,1,0:T(8,128)(2,1)}), bf16[8,8,32,2048]{3,2,1,0:T(8,128)(2,1)}, u32[]{:S(2)}, u32[]{:S(2)}) async-start(bf16[8,8,32,2048]{3,2,1,0:T(8,128)(2,1)} %copy.244), calls=%async_computation.3 | async-start | bytes 16777216 | tf_op jit(solution)/shard_map/all_to_all | solution.py:184
  1154.8 161.9 %copy-start.61 = (bf16[1024]{0:T(1024)(128)(2,1)S(1)}, bf16[1024]{0:T(1024)(128)(2,1)}, u32[]{:S(2)}) copy-start(bf16[1024]{0:T(1024)(128)(2,1)} %copy-done.60) | copy-start | bytes 6148
  1154.8 162.0 %copy-start.64 = (s32[1024,1]{0,1:T(1,128)S(1)}, s32[1024,1]{0,1:T(1,128)}, u32[]{:S(2)}) copy-start(s32[1024,1]{0,1:T(1,128)} %copy-done.63) | copy-start | bytes 12292
  1311.7 187.6 %all-to-all-start.1 = ((bf16[8,8,32,2048]{3,2,1,0:T(8,128)(2,1)}), bf16[8,8,32,2048]{3,2,1,0:T(8,128)(2,1)}, u32[]{:S(2)}, u32[]{:S(2)}) async-start(bf16[8,8,32,2048]{3,2,1,0:T(8,128)(2,1)} %copy.241), calls=%async_computation.1 | async-start | bytes 16777216 | tf_op jit(solution)/shard_map/all_to_all | solution.py:145
  1316.6 426.6 %reduce-scatter.9.cloned.1.call-start = ((), (), s32[]{:S(2)}) async-start(), calls=%async_computation.15 | async-start | bytes 9437184 | tf_op jit(solution)/shard_map/reduce_scatter | solution.py:266
  1499.3 13.5 copy-start.17
  1499.3 13.5 copy-start.38
  1499.3 19.5 copy-start.52
  1499.3 19.5 copy-start.34
  1499.3 19.5 copy-start.66
  1499.3 19.5 copy-start.68
  1499.3 19.6 copy-start.11
  1499.3 19.6 copy-start.21
  1499.3 19.6 copy-start.48
  1499.4 19.6 copy-start.74
  1521.3 11.3 copy-start.3
  1521.3 11.3 copy-start.59
  1567.2 9.4 copy-start
  1596.0 315.7 %reduce-scatter.19.cloned.1.call-start = ((), (), s32[]{:S(2)}) async-start(), calls=%async_computation.20 | async-start | bytes 1081344
  1596.0 18.5 copy-start.76
  1633.0 112.7 %copy-start.4 = (f32[128,16,128]{0,2,1:T(8,128)S(1)}, f32[128,16,128]{0,2,1:T(8,128)}, u32[]{:S(2)}) copy-start(f32[128,16,128]{0,2,1:T(8,128)} %get-tuple-element.75) | copy-start | bytes 3145732
  1633.0 112.7 %copy-start.36 = (f32[128,128]{0,1:T(8,128)S(1)}, f32[128,128]{0,1:T(8,128)}, u32[]{:S(2)}) copy-start(f32[128,128]{0,1:T(8,128)} %copy-done.35) | copy-start | bytes 196612
  1651.2 95.8 %copy-start.31 = (f32[128,128]{0,1:T(8,128)S(1)}, f32[128,128]{0,1:T(8,128)}, u32[]{:S(2)}) copy-start(f32[128,128]{0,1:T(8,128)} %copy-done.30) | copy-start | bytes 196612
  1745.8 10.0 copy-start.44
  1745.8 9.9 copy-start.46
  1745.8 9.9 copy-start.70
  1745.8 9.9 copy-start.72
  1748.1 10.9 copy-start.6
  1752.1 9.6 copy-start.40
  1752.1 9.6 copy-start.57
  1761.7 14.6 copy-start.53
  1777.8 801.2 %reduce-scatter.17.cloned.1.call-start = ((), (), s32[]{:S(2)}) async-start(), calls=%async_computation.19 | async-start | bytes 125829120 | tf_op jit(solution)/shard_map/reduce_scatter | solution.py:187
  1844.0 872.7 %reduce-scatter.15.cloned.1.call-start = ((), (), s32[]{:S(2)}) async-start(), calls=%async_computation.18 | async-start | bytes 1081344 | tf_op jit(solution)/shard_map/reduce_scatter | solution.py:295
  1846.3 1051.9 %reduce-scatter.13.cloned.1.call-start = ((), (), s32[]{:S(2)}) async-start(), calls=%async_computation.17 | async-start | bytes 17301504 | tf_op jit(solution)/shard_map/reduce_scatter | solution.py:294
  1854.5 1484.1 %reduce-scatter.11.cloned.1.call-start = ((), (), s32[]{:S(2)}) async-start(), calls=%async_computation.16 | async-start | bytes 51904512 | tf_op jit(solution)/shard_map/reduce_scatter | solution.py:293
  (30 other events, 99.8 us)
Sparse Core Ops, SparseCore 0:
  10.9 157.4 all-gather.7
  179.7 71.6 all-gather.11
  254.1 71.7 all-gather.9
  328.5 75.8 all-gather.13
  406.4 599.8 all-gather.15
  1596.1 147.1 reduce-scatter.8
  1777.9 133.7 reduce-scatter.18
  1914.3 664.6 reduce-scatter.16
  2581.9 134.7 reduce-scatter.14
  2719.5 178.7 reduce-scatter.12
  2905.3 433.2 reduce-scatter.10
where the time goes:
time: 3350 us
  waiting for transfers between devices  2410 us (72%)
  matrix products  283 us (8%)
  blocking collectives  261 us (8%)
  local copies, waits for them, and re-layouts  198 us (6%)
  other arithmetic  139 us (4%)
  starting transfers between devices  34.7 us (1%)
    reduce_scatter x1, waiting for transfers between devices, local(): lax.psum_scatter(expert_grad.astype(jnp.bfloat16), 'batch', scatter_dimen...  666 us
    reduce_scatter x1, waiting for transfers between devices, local(): lax.psum_scatter(in_weight_grad, ('seq', 'batch'), scatter_dimension=0, t...  440 us
    all_gather x1, waiting for transfers between devices, local(): full_expert = lax.all_gather(w_expert, 'batch', axis=3, tiled=True)  339 us
    all_gather x1, blocking collectives, local(): lax.all_gather(w_router, ('seq', 'batch'), axis=0, tiled=True)  199 us
    reduce_scatter x1, waiting for transfers between devices, local(): lax.psum_scatter(out_weight_grad, ('seq', 'batch'), scatter_dimension=0,...  182 us
    all_to_all x1, waiting for transfers between devices, local(): lax.all_to_all(owner_input_grad, 'seq', split_axis=0, concat_axis=0, tile...  157 us
    all_to_all x1, waiting for transfers between devices, local(): lax.all_to_all(owner_out, 'seq', split_axis=0, concat_axis=0, tiled=True)  154 us
    all_gather x1, waiting for transfers between devices, local(): lax.all_gather(w_in, ('seq', 'batch'), axis=0, tiled=True)  115 us
  transfers between devices with their start and end apart: 15, of which 12 were waited for; matrix products, arithmetic and copies ran while one was open for 12% of the time, Pallas kernels for 0%

commit v1 on v0

v1 whole, which is shorter than its diff:
```python
import jax
import jax.numpy as jnp
from jax import lax
from jax.sharding import PartitionSpec as P

HEADS = 16
CAP = 32
epsilon = 1e-05
BOTH = ("seq", "batch")
f32 = jnp.float32
bf16 = jnp.bfloat16


def rms_scale(values):
    return lax.rsqrt(jnp.mean(values * values, axis=-1, keepdims=True) + epsilon)


def rotate_half(values):
    half = values.shape[-1] // 2
    return jnp.concatenate([-values[..., half:], values[..., :half]], axis=-1)


def rope_tables(positions, head_size):
    steps = jnp.arange(head_size // 2, dtype=f32)
    freqs = jnp.exp(steps * (-2.0 * jnp.log(10000.0) / head_size))
    angles = positions.astype(f32)[:, None] * freqs[None, :]
    angles = jnp.concatenate([angles, angles], axis=-1)
    return (jnp.cos(angles)[:, None, :], jnp.sin(angles)[:, None, :])


def norm_back(grad_out, normal, scale, gain):
    scaled = grad_out * gain
    return scale * (scaled - normal * jnp.mean(scaled * normal, axis=-1, keepdims=True))


def dot(a, b, dims):
    return lax.dot_general(a, b, (dims, ((), ())), preferred_element_type=f32)


class HeadsAttention:
    def __init__(self, hidden, segment_all, w_in, w_out, gains_all):
        seq = lax.axis_size("seq")
        batch = lax.axis_size("batch")
        place = lax.axis_index("seq")
        self.rows = hidden.shape[0]
        width = hidden.shape[1]
        self.width = width
        self.hs = width // HEADS
        self.hl = HEADS // seq
        cols = self.hl * self.hs
        self.cols = cols
        own = w_in.shape[0]
        hidden_all = lax.all_gather(hidden, "seq", axis=0, tiled=True)
        length = hidden_all.shape[0]
        self.length = length
        parts = w_in.reshape(own, 3, seq, cols)
        parts = lax.all_to_all(parts, "seq", split_axis=2, concat_axis=2, tiled=True)
        parts = jnp.transpose(parts, (2, 0, 1, 3)).reshape(seq, own, 3 * cols)
        self.w_cols = lax.all_gather(parts, "batch", axis=1, tiled=True).reshape(width, 3 * cols)
        self.w_rows = lax.all_gather(w_out, "batch", axis=0, tiled=True)
        inputs = hidden_all.astype(f32)
        normed = (inputs * rms_scale(inputs) * gains_all[0]).astype(bf16)
        self.normed = normed
        projected = jnp.dot(normed, self.w_cols, preferred_element_type=f32)
        query_raw = projected[:, :cols]
        key_raw = projected[:, cols : 2 * cols]
        squares = jnp.stack([jnp.sum(query_raw * query_raw, -1), jnp.sum(key_raw * key_raw, -1)], 0)
        scales = lax.rsqrt(lax.psum(squares, "seq") / width + epsilon)
        self.query_scale = scales[0][:, None]
        self.key_scale = scales[1][:, None]
        self.query_normal = query_raw * self.query_scale
        self.key_normal = key_raw * self.key_scale
        mine = lax.dynamic_slice_in_dim(gains_all, place * cols, cols, 1)
        self.query_gain, self.key_gain = mine[1], mine[2]
        positions = jnp.arange(length, dtype=jnp.int32)
        self.cosine, self.sine = rope_tables(positions, self.hs)
        shape = (length, self.hl, self.hs)

        def rot(u):
            u = u.reshape(shape)
            return (u * self.cosine + rotate_half(u) * self.sine).astype(bf16)

        self.query = rot(self.query_normal * self.query_gain)
        self.key = rot(self.key_normal * self.key_gain)
        self.value = projected[:, 2 * cols :].astype(bf16).reshape(shape)
        self.allowed = (positions[None, :] <= positions[:, None]) & (
            segment_all[None, :] == segment_all[:, None]
        )
        scores = self.scores()
        top = jnp.max(scores, axis=-1, keepdims=True)
        weights = jnp.exp(scores - top)
        total = jnp.sum(weights, axis=-1, keepdims=True)
        acc = jnp.einsum("hqk,khd->hqd", weights.astype(bf16), self.value, preferred_element_type=f32)
        self.log_total = top + jnp.log(total)
        self.attended = jnp.transpose(acc / total, (1, 0, 2))
        self.attn_low = self.attended.reshape(length, cols).astype(bf16)
        partial = jnp.dot(self.attn_low, self.w_rows, preferred_element_type=f32).astype(bf16)
        self.mixed = lax.psum_scatter(partial, "seq", scatter_dimension=0, tiled=True).astype(f32)

    def scores(self):
        scale = self.hs ** (-0.5)
        scores = jnp.einsum("qhd,khd->hqk", self.query, self.key, preferred_element_type=f32) * scale
        return jnp.where(self.allowed[None], scores, -jnp.inf)

    def back(self, middle_low):
        seq = lax.axis_size("seq")
        batch = lax.axis_size("batch")
        length, cols, width = self.length, self.cols, self.width
        scale = self.hs ** (-0.5)
        shape = (length, self.hl, self.hs)
        grad_all = lax.all_gather(middle_low, "seq", axis=0, tiled=True)
        out_grad = dot(self.attn_low, grad_all, ((0,), (0,))).astype(bf16)
        out_shard = lax.psum_scatter(out_grad, "batch", scatter_dimension=0, tiled=True).astype(f32)
        attn_grad = dot(grad_all, self.w_rows, ((1,), (1,))).astype(bf16).reshape(shape)
        delta = jnp.sum(attn_grad.astype(f32) * self.attended, axis=-1)
        probs = jnp.exp(self.scores() - self.log_total)
        prob_grad = jnp.einsum("qhd,khd->hqk", attn_grad, self.value, preferred_element_type=f32)
        score_grad = (probs * (prob_grad - delta.T[..., None])).astype(bf16)
        query_grad = jnp.einsum("hqk,khd->qhd", score_grad, self.key, preferred_element_type=f32) * scale
        key_grad = jnp.einsum("hqk,qhd->khd", score_grad, self.query, preferred_element_type=f32) * scale
        value_grad = jnp.einsum("hqk,qhd->khd", probs.astype(bf16), attn_grad, preferred_element_type=f32)

        def rot_back(u):
            return (u * self.cosine - rotate_half(u * self.sine)).reshape(length, cols)

        query_norm_grad = rot_back(query_grad)
        key_norm_grad = rot_back(key_grad)
        query_gain_grad = jnp.sum(query_norm_grad * self.query_normal, axis=0)
        key_gain_grad = jnp.sum(key_norm_grad * self.key_normal, axis=0)
        query_scaled = query_norm_grad * self.query_gain
        key_scaled = key_norm_grad * self.key_gain
        means = lax.psum(
            jnp.stack([jnp.sum(query_scaled * self.query_normal, -1), jnp.sum(key_scaled * self.key_normal, -1)], 0),
            "seq",
        ) / width
        query_raw_grad = self.query_scale * (query_scaled - self.query_normal * means[0][:, None])
        key_raw_grad = self.key_scale * (key_scaled - self.key_normal * means[1][:, None])
        projected_grad = jnp.concatenate(
            [query_raw_grad, key_raw_grad, value_grad.reshape(length, cols)], axis=1
        ).astype(bf16)
        partial = dot(projected_grad, self.w_cols, ((1,), (1,))).astype(bf16)
        normed_grad = lax.psum_scatter(partial, "seq", scatter_dimension=0, tiled=True).astype(f32)
        in_grad = dot(self.normed, projected_grad, ((0,), (0,))).astype(bf16)
        own = width // (seq * batch)
        in_grad = lax.psum_scatter(
            in_grad.reshape(seq, batch * own, 3 * cols), "batch", scatter_dimension=1, tiled=True
        )
        in_grad = lax.all_to_all(in_grad, "seq", split_axis=0, concat_axis=0, tiled=True)
        in_shard = jnp.transpose(in_grad.reshape(seq, own, 3, cols), (1, 2, 0, 3)).reshape(own, 3 * width)
        pair = lax.psum_scatter(
            jnp.stack([query_gain_grad, key_gain_grad], 1), "batch", scatter_dimension=0, tiled=True
        )
        return normed_grad, in_shard.astype(f32), out_shard, pair


class TokensAttention:
    def __init__(self, hidden, segment_all, w_in, w_out, gains_all):
        place = lax.axis_index("seq")
        rows, width = hidden.shape
        self.rows, self.width = rows, width
        self.hs = width // HEADS
        self.sources = w_in, w_out
        self.gather_weights(w_in, w_out)
        inputs = hidden.astype(f32)
        self.normed = (inputs * rms_scale(inputs) * gains_all[0]).astype(bf16)
        projected = jnp.dot(self.normed, self.in_all, preferred_element_type=f32)
        query_raw = projected[:, :width]
        key_raw = projected[:, width : 2 * width]
        self.query_scale = rms_scale(query_raw)
        self.query_normal = query_raw * self.query_scale
        self.key_scale = rms_scale(key_raw)
        self.key_normal = key_raw * self.key_scale
        self.query_gain, self.key_gain = gains_all[1], gains_all[2]
        self.positions = place * rows + jnp.arange(rows, dtype=jnp.int32)
        self.cosine, self.sine = rope_tables(self.positions, self.hs)
        shape = (rows, HEADS, self.hs)

        def rot(u):
            u = u.reshape(shape)
            return (u * self.cosine + rotate_half(u) * self.sine).astype(bf16)

        self.query = rot(self.query_normal * self.query_gain)
        key = rot(self.key_normal * self.key_gain).reshape(rows, width)
        value = projected[:, 2 * width :].astype(bf16)
        self.kept = key, value
        self.gather_keys(key, value)
        self.segment_all = segment_all
        self.segment_own = lax.dynamic_slice_in_dim(segment_all, place * rows, rows, 0)
        length = self.key_all.shape[0]
        scores = self.scores(self.key_all.reshape(length, HEADS, self.hs), segment_all, 0)
        top = jnp.max(scores, axis=-1, keepdims=True)
        weights = jnp.exp(scores - top)
        total = jnp.sum(weights, axis=-1, keepdims=True)
        acc = jnp.einsum(
            "hqk,khd->hqd",
            weights.astype(bf16),
            self.value_all.reshape(length, HEADS, self.hs),
            preferred_element_type=f32,
        )
        self.log_total = top + jnp.log(total)
        self.attended = jnp.transpose(acc / total, (1, 0, 2))
        self.attn_low = self.attended.reshape(rows, width).astype(bf16)
        self.mixed = jnp.dot(self.attn_low, self.out_all, preferred_element_type=f32)

    def gather_weights(self, w_in, w_out):
        self.in_all = lax.all_gather(w_in, BOTH, axis=0, tiled=True)
        self.out_all = lax.all_gather(w_out, BOTH, axis=0, tiled=True)

    def gather_keys(self, key, value):
        self.key_all = lax.all_gather(key, "seq", axis=0, tiled=True)
        self.value_all = lax.all_gather(value, "seq", axis=0, tiled=True)

    def scores(self, key, segment, start):
        scale = self.hs ** (-0.5)
        scores = jnp.einsum("qhd,khd->hqk", self.query, key, preferred_element_type=f32) * scale
        key_positions = start + jnp.arange(key.shape[0], dtype=jnp.int32)
        allowed = (key_positions[None, :] <= self.positions[:, None]) & (
            segment[None, :] == self.segment_own[:, None]
        )
        return jnp.where(allowed[None], scores, -jnp.inf)

    def back(self, middle_low):
        again = lax.optimization_barrier((middle_low, *self.sources, *self.kept))
        middle_low = again[0]
        self.gather_weights(*again[1:3])
        self.gather_keys(*again[3:])
        rows, width = self.rows, self.width
        scale = self.hs ** (-0.5)
        out_grad = dot(self.attn_low, middle_low, ((0,), (0,))).astype(bf16)
        out_shard = lax.psum_scatter(out_grad, BOTH, scatter_dimension=0, tiled=True).astype(f32)
        attn_grad = dot(middle_low, self.out_all, ((1,), (1,))).astype(bf16).reshape(rows, HEADS, self.hs)
        delta = jnp.sum(attn_grad.astype(f32) * self.attended, axis=-1).T
        length = self.key_all.shape[0]
        block = min(512, length)
        count = length // block

        def step(query_grad, item):
            key, value, segment, start = item
            probs = jnp.exp(self.scores(key, segment, start) - self.log_total)
            prob_grad = jnp.einsum("qhd,khd->hqk", attn_grad, value, preferred_element_type=f32)
            score_grad = (probs * (prob_grad - delta[..., None])).astype(bf16)
            query_grad = (
                query_grad + jnp.einsum("hqk,khd->qhd", score_grad, key, preferred_element_type=f32) * scale
            )
            key_grad = jnp.einsum("hqk,qhd->khd", score_grad, self.query, preferred_element_type=f32) * scale
            value_grad = jnp.einsum("hqk,qhd->khd", probs.astype(bf16), attn_grad, preferred_element_type=f32)
            return query_grad, jnp.concatenate(
                [key_grad.reshape(block, width), value_grad.reshape(block, width)], axis=1
            ).astype(bf16)

        query_grad, terms = lax.scan(
            step,
            jnp.zeros((rows, HEADS, self.hs), f32),
            (
                self.key_all.reshape(count, block, HEADS, self.hs),
                self.value_all.reshape(count, block, HEADS, self.hs),
                self.segment_all.reshape(count, block),
                jnp.arange(count, dtype=jnp.int32) * block,
            ),
        )
        kv_grad = lax.psum_scatter(
            terms.reshape(length, 2 * width), "seq", scatter_dimension=0, tiled=True
        ).astype(f32)
        key_grad = kv_grad[:, :width].reshape(rows, HEADS, self.hs)

        def rot_back(u):
            return (u * self.cosine - rotate_half(u * self.sine)).reshape(rows, width)

        query_norm_grad = rot_back(query_grad)
        key_norm_grad = rot_back(key_grad)
        query_gain_grad = jnp.sum(query_norm_grad * self.query_normal, axis=0)
        key_gain_grad = jnp.sum(key_norm_grad * self.key_normal, axis=0)
        query_raw_grad = norm_back(query_norm_grad, self.query_normal, self.query_scale, self.query_gain)
        key_raw_grad = norm_back(key_norm_grad, self.key_normal, self.key_scale, self.key_gain)
        projected_grad = jnp.concatenate([query_raw_grad, key_raw_grad, kv_grad[:, width:]], axis=1).astype(bf16)
        in_grad = dot(self.normed, projected_grad, ((0,), (0,))).astype(bf16)
        in_shard = lax.psum_scatter(in_grad, BOTH, scatter_dimension=0, tiled=True).astype(f32)
        normed_grad = dot(projected_grad, self.in_all, ((1,), (1,)))
        pair = lax.psum_scatter(
            jnp.stack([query_gain_grad, key_gain_grad], 1), BOTH, scatter_dimension=0, tiled=True
        )
        return normed_grad, in_shard, out_shard, pair


def expert_math(slots, grads, gate_slot, w_expert):
    w_gate, w_up, w_down = w_expert[:, 0], w_expert[:, 1], w_expert[:, 2]
    gate = jnp.einsum("esd,edf->esf", slots, w_gate, preferred_element_type=f32)
    up = jnp.einsum("esd,edf->esf", slots, w_up, preferred_element_type=f32)
    sigma = jax.nn.sigmoid(gate)
    silu = gate * sigma
    act = (silu * up).astype(bf16).astype(f32)
    act_gated = (act * gate_slot).astype(bf16)
    act_raw = jnp.einsum("esd,edf->esf", grads, w_down, preferred_element_type=f32)
    gate_grad = jnp.sum(act_raw * act, axis=-1)
    act_grad = act_raw * gate_slot
    gate_low = (act_grad * up * sigma * (1.0 + gate * (1.0 - sigma))).astype(bf16)
    up_low = (act_grad * silu).astype(bf16)
    slot_grad = (
        jnp.einsum("esf,edf->esd", gate_low, w_gate, preferred_element_type=f32)
        + jnp.einsum("esf,edf->esd", up_low, w_up, preferred_element_type=f32)
    ).astype(bf16)
    result = jnp.einsum("esf,edf->esd", act_gated, w_down, preferred_element_type=f32).astype(bf16)
    expert_grad = jnp.stack(
        [
            jnp.einsum("esd,esf->edf", slots, gate_low, preferred_element_type=f32),
            jnp.einsum("esd,esf->edf", slots, up_low, preferred_element_type=f32),
            jnp.einsum("esd,esf->edf", grads, act_gated, preferred_element_type=f32),
        ],
        axis=1,
    )
    return result, slot_grad, gate_grad, expert_grad


def slot_places(hit):
    count = hit.astype(jnp.int32)
    rank = jnp.where(hit, jnp.cumsum(count, axis=1) - count, -1)
    return rank[:, :, :, None] == jnp.arange(CAP, dtype=jnp.int32)


def experts_by_tokens(ffn_in, cotangent, routes, w_expert, router_all):
    seq, batch = lax.axis_size("seq"), lax.axis_size("batch")
    place = lax.axis_index("seq")
    everyone = seq * batch
    experts = w_expert.shape[0]
    rows, width = ffn_in.shape
    routes_all = lax.all_gather(routes, BOTH, axis=0, tiled=True)
    cotangent_all = lax.all_gather(cotangent, BOTH, axis=0, tiled=True)
    ffn_all = lax.all_gather(ffn_in, BOTH, axis=0, tiled=True)
    mine = place * experts + jnp.arange(experts, dtype=jnp.int32)
    hit = jnp.any(routes_all[:, :, None] == mine[None, None, :], axis=1).reshape(everyone, rows, experts)
    hot = slot_places(hit)
    place_hot = jnp.transpose(hot, (0, 2, 3, 1)).astype(bf16).reshape(everyone, experts * CAP, rows)
    router_every = jax.nn.softmax(jnp.dot(ffn_all, router_all, preferred_element_type=f32), axis=-1)
    router_mine = lax.dynamic_slice_in_dim(router_every, place * experts, experts, 1)
    gate_slot = jnp.sum(jnp.where(hot, router_mine.reshape(everyone, rows, experts, 1), 0.0), axis=1)
    gate_slot = jnp.transpose(gate_slot, (1, 0, 2)).reshape(experts, everyone * CAP, 1)

    def dispatch(tokens):
        slots = jnp.einsum(
            "dst,dth->dsh", place_hot, tokens.reshape(everyone, rows, width), preferred_element_type=f32
        ).astype(bf16)
        slots = jnp.transpose(slots.reshape(everyone, experts, CAP, width), (1, 0, 2, 3))
        return slots.reshape(experts, everyone * CAP, width)

    def combine(values):
        values = jnp.transpose(values.reshape(experts, everyone, CAP, width), (1, 0, 2, 3))
        values = values.reshape(everyone, experts * CAP, width)
        return (
            jnp.einsum("dst,dsh->dth", place_hot, values, preferred_element_type=f32)
            .astype(bf16)
            .reshape(everyone * rows, width)
        )

    result, slot_grad, gate_grad, expert_grad = expert_math(
        dispatch(ffn_all), dispatch(cotangent_all), gate_slot, w_expert
    )
    gate_grad = jnp.transpose(gate_grad.reshape(experts, everyone, CAP), (1, 0, 2))
    gate_part = jnp.sum(jnp.where(hot, gate_grad[:, None], 0.0), axis=-1)
    gate_part = gate_part.reshape(seq, batch * rows, experts)
    gate_part = lax.psum_scatter(gate_part, "batch", scatter_dimension=1, tiled=True)
    gate_part = lax.all_to_all(gate_part, "seq", split_axis=0, concat_axis=0, tiled=True)
    prob_grad = jnp.transpose(gate_part, (1, 0, 2)).reshape(rows, seq * experts)
    ffn_in_grad = lax.psum_scatter(combine(slot_grad), BOTH, scatter_dimension=0, tiled=True).astype(f32)
    mixture = lax.psum_scatter(combine(result), BOTH, scatter_dimension=0, tiled=True).astype(f32)
    return mixture, ffn_in_grad, prob_grad, expert_grad


def experts_by_slots(ffn_in, cotangent, routes, w_expert, router_all):
    seq, batch = lax.axis_size("seq"), lax.axis_size("batch")
    experts = w_expert.shape[0]
    total = experts * seq
    rows, width = ffn_in.shape
    hit = jnp.any(routes[:, :, None] == jnp.arange(total, dtype=jnp.int32), axis=1)[None]
    hot = slot_places(hit)[0]
    place_hot = hot.astype(bf16).reshape(rows, total * CAP)
    router = jax.nn.softmax(jnp.dot(ffn_in, router_all, preferred_element_type=f32), axis=-1)
    gate_slot = jnp.sum(jnp.where(hot, router[:, :, None], 0.0), axis=0).reshape(seq, experts, CAP, 1)

    def there(values):
        values = lax.all_to_all(values, "seq", split_axis=0, concat_axis=0, tiled=True)
        values = lax.all_gather(values, "batch", axis=0, tiled=True)
        values = jnp.transpose(values, (1, 0, 2, 3))
        return values.reshape(experts, batch * seq * CAP, values.shape[-1])

    def back(values):
        values = values.reshape(experts, batch * seq, CAP, values.shape[-1])
        values = jnp.transpose(values, (1, 0, 2, 3))
        values = lax.psum_scatter(values, "batch", scatter_dimension=0, tiled=True)
        values = lax.all_to_all(values, "seq", split_axis=0, concat_axis=0, tiled=True)
        return values.reshape(total * CAP, values.shape[-1])

    def slots_of(tokens):
        slots = dot(place_hot, tokens, ((0,), (0,))).astype(bf16)
        return there(slots.reshape(seq, experts, CAP, width))

    def tokens_of(slots):
        return jnp.dot(place_hot, back(slots), preferred_element_type=f32)

    result, slot_grad, gate_grad, expert_grad = expert_math(
        slots_of(ffn_in), slots_of(cotangent), there(gate_slot), w_expert
    )
    gate_grad = back(gate_grad[..., None]).reshape(1, total, CAP)
    prob_grad = jnp.sum(jnp.where(hot, gate_grad, 0.0), axis=-1)
    return tokens_of(result), tokens_of(slot_grad), prob_grad, expert_grad


def local(hidden, segments, routes, w_in, w_out, w_router, gains, w_expert, cotangent):
    seq = lax.axis_size("seq")
    total_experts = w_expert.shape[0] * seq

    small = lax.all_gather(jnp.concatenate([w_router, gains.T], axis=1), BOTH, axis=0, tiled=True)
    router_all = small[:, :total_experts]
    gains_all = small[:, total_experts:].T.astype(f32)
    segment_all = lax.all_gather(segments[0], "seq", axis=0, tiled=True)

    inputs = hidden[0].astype(f32)
    first_scale = rms_scale(inputs)
    first_normal = inputs * first_scale

    by_heads = HEADS % seq == 0
    attend = HeadsAttention if by_heads else TokensAttention
    mix = experts_by_tokens if by_heads else experts_by_slots
    attention = attend(hidden[0], segment_all, w_in, w_out, gains_all)

    middle = inputs + attention.mixed
    second_scale = rms_scale(middle)
    second_normal = middle * second_scale
    ffn_in = (second_normal * gains_all[3]).astype(bf16)
    mixture, ffn_in_grad, prob_grad, expert_grad = mix(
        ffn_in, cotangent[0], routes[0], w_expert, router_all
    )
    output = middle + mixture

    grad_out = cotangent[0].astype(f32)
    router = jax.nn.softmax(jnp.dot(ffn_in, router_all, preferred_element_type=f32), axis=-1)
    logit_grad = router * (prob_grad - jnp.sum(router * prob_grad, axis=-1, keepdims=True))
    logit_low = logit_grad.astype(bf16)
    router_grad = dot(ffn_in, logit_low, ((0,), (0,)))
    ffn_in_grad = ffn_in_grad + dot(logit_low, router_all, ((1,), (1,)))
    ffn_gain_grad = jnp.sum(ffn_in_grad * second_normal, axis=0)
    middle_grad = grad_out + norm_back(ffn_in_grad, second_normal, second_scale, gains_all[3])
    normed_grad, in_shard, out_shard, pair_shard = attention.back(middle_grad.astype(bf16))
    attn_gain_grad = jnp.sum(normed_grad * first_normal, axis=0)
    input_grad = middle_grad + norm_back(normed_grad, first_normal, first_scale, gains_all[0])
    sums = jnp.concatenate([router_grad, attn_gain_grad[:, None], ffn_gain_grad[:, None]], axis=1)
    sums = lax.psum_scatter(sums, BOTH, scatter_dimension=0, tiled=True)
    router_shard = sums[:, :total_experts]
    ends = sums[:, total_experts:]
    gains_shard = jnp.stack([ends[:, 0], pair_shard[:, 0], pair_shard[:, 1], ends[:, 1]], axis=0)
    return (
        output.astype(bf16)[None],
        input_grad[None],
        in_shard,
        out_shard,
        router_shard,
        gains_shard,
        expert_grad,
    )


def solution(mesh):
    placed = (
        P("batch", "seq", None),
        P("batch", "seq"),
        P("batch", "seq", None),
        P(BOTH, None),
        P(BOTH, None),
        P(BOTH, None),
        P(None, BOTH),
        P("seq", None, None, "batch"),
        P("batch", "seq", None),
    )
    return jax.shard_map(
        local,
        mesh=mesh,
        in_specs=placed,
        out_specs=(
            P("batch", "seq", None),
            P("batch", "seq", None),
            P(BOTH, None),
            P(BOTH, None),
            P(BOTH, None),
            P(None, BOTH),
            P("seq", None, None, "batch"),
        ),
        check_vma=False,
    )
```

time: 3350 us -> 1510 us (0.45)
  waiting for transfers between devices: 2410 us -> 699 us
  matrix products: 283 us -> 366 us
  blocking collectives: 261 us -> 183 us
  other arithmetic: 139 us -> 82 us
  local copies, waits for them, and re-layouts: 198 us -> 150 us
    reduce_scatter x5 -> x7, waiting for transfers between devices: 1490 us -> 452 us  [the longest x1 169 us: experts_by_tokens(): lax.psum_scatter(combine(slot_grad), BOTH, scatter_dimension=0, tiled=True)]
    all_gather x5 -> x6, waiting for transfers between devices: 577 us -> 102 us  [the longest x1 75 us: back(): grad_all = lax.all_gather(middle_low, 'seq', axis=0, tiled=True)]
    all_to_all x4 -> x2, waiting for transfers between devices: 311 us -> 6.66 us  [the longest x1 6.66 us: experts_by_tokens(): lax.all_to_all(gate_part, 'seq', split_axis=0, concat_axis=0, tiled=True)]
    all_gather x3, blocking collectives: 261 us -> 99.5 us  [the longest x1 40.8 us: experts_by_tokens(): routes_all = lax.all_gather(routes, BOTH, axis=0, tiled=True)]
    unnamed x12 -> x17, waiting for transfers between devices: 34.9 us -> 138 us
    dot_general x30 -> x29, matrix products: 283 us -> 366 us  [the longest x2 47.2 us: dispatch(): jnp.einsum('dst,dth->dsh', place_hot, tokens.reshape(everyone, rows, widt...]
    gather x4 -> x0, local copies, waits for them, and re-layouts: 57 us -> none  [the longest x1 19.1 us: local(): pair_grad[source].reshape(seq_count, local_experts, capacity, width)]
    another operation x7, other arithmetic: 87 us -> 38.4 us  [the longest x1 35.1 us: expert_math(): jnp.stack([jnp.einsum('esd,esf->edf', slots, gate_low, preferred_element_...]
  transfers between devices with their start and end apart: 15 -> 17, of which waited for: 12 -> 8; matrix products, arithmetic and copies ran while one was open for 12% -> 28% of each run, Pallas kernels for 0% -> 0%
where the time goes in v1:
time: 1510 us
  waiting for transfers between devices  699 us (46%)
  matrix products  366 us (24%)
  blocking collectives  183 us (12%)
  local copies, waits for them, and re-layouts  150 us (10%)
  other arithmetic  82 us (5%)
  between operations  16.6 us (1%)
    reduce_scatter x1, waiting for transfers between devices, experts_by_tokens(): lax.psum_scatter(combine(slot_grad), BOTH, scatter_dimension=0, tiled=True)  169 us
    reduce_scatter x1, waiting for transfers between devices, __init__(): lax.psum_scatter(partial, 'seq', scatter_dimension=0, tiled=True)  144 us
    reduce_scatter x1, waiting for transfers between devices, experts_by_tokens(): lax.psum_scatter(combine(result), BOTH, scatter_dimension=0, tiled=True)  139 us
    unnamed x17, waiting for transfers between devices  138 us
    all_gather x1, waiting for transfers between devices, back(): grad_all = lax.all_gather(middle_low, 'seq', axis=0, tiled=True)  75 us
    dot_general x2, matrix products, dispatch(): jnp.einsum('dst,dth->dsh', place_hot, tokens.reshape(everyone, rows, widt...  47.2 us
    transpose x2, local copies, waits for them, and re-layouts, combine(): jnp.transpose(values.reshape(experts, everyone, CAP, width), (1, 0, 2, 3))  46.6 us
    reshape x2, local copies, waits for them, and re-layouts, dispatch(): slots.reshape(everyone, experts, CAP, width)  45.9 us
  transfers between devices with their start and end apart: 17, of which 8 were waited for; matrix products, arithmetic and copies ran while one was open for 28% of the time, Pallas kernels for 0%

profile of v1, /device:TPU:0, one launch (start us, length us, event | category | flops | bytes accessed | tf_op | source)
XLA Modules:
  0.0 1505.4 jit_solution(4949413006171067511)
XLA Ops:
  10.3 42.6 %all_to_all.15 = bf16[64,3,8,256]{3,0,1,2:T(8,128)(2,1)S(1)} all-to-all(bf16[64,3,8,256]{3,0,1,2:T(8,128)(2,1)S(1)} %copy.263), channel_id=1, replica_groups=mesh['seq'=8,'batch'=4] {'seq'}, dimensions={2} | all-to-all | bytes 1572864 | tf_op jit(solution)/shard_map/all_to_all | solution.py:57
  54.7 18.0 %all-gather = s32[1,1024]{1,0:T(1,128)S(1)} all-gather(s32[1,128]{1,0:T(1,128)} %param.10), channel_id=2, replica_groups=mesh['seq'=8,'batch'=4] {'seq'}, dimensions={1}, use_global_device_ids=true | all-gather | bytes 4608 | tf_op jit(solution)/shard_map/all_gather | solution.py:414
  74.3 40.7 %all_gather.29 = bf16[2048,68]{1,0:T(8,128)(2,1)S(1)} all-gather(bf16[64,68]{1,0:T(8,128)(2,1)S(1)} %pad_maximum_fusion.6), channel_id=1, replica_groups=mesh['seq'=8,'batch'=4] {'seq','batch'}, dimensions={0}, use_global_device_ids=true | all-gather | bytes 287232 | tf_op jit(solution)/shard_map/all_gather | solution.py:411
  114.9 1.6 fusion.30
  116.6 2.9 broadcast_multiply_fusion.3
  121.0 3.1 fusion.2
  124.1 5.8 all-gather.11.cloned.1.call-done
  129.9 6.7 fusion.51
  136.8 21.8 %psum.14 = f32[2,1024]{1,0:T(2,128)S(1)} all-reduce(f32[2,1024]{1,0:T(2,128)S(1)} %pad_maximum_fusion.7), channel_id=1, replica_groups=mesh['seq'=8,'batch'=4] {'seq'}, use_global_device_ids=true, to_apply=%region_3.0 | all-reduce | flops 2048 | bytes 16384 | tf_op jit(solution)/shard_map/psum | solution.py:68
  160.5 1.9 fusion.25
  162.6 2.0 fusion.16
  166.0 3.6 fusion.98
  169.6 4.7 convolution_convert_fusion.5
  175.0 144.3 %reduce-scatter.14.cloned.1.call-done = bf16[128,2048]{1,0:T(8,128)(2,1)} async-done(((bf16[1024,2048]{1,0:T(8,128)(2,1)}), bf16[128,2048]{1,0:T(8,128)(2,1)}) %reduce-scatter.14.cloned.1.call-update) | async-done | bytes 524304 | tf_op jit(solution)/shard_map/reduce_scatter | solution.py:98
  320.7 2.1 multiply_convert_fusion.6
  322.9 40.8 %all-gather.2 = s32[1,4096,8]{1,2,0:T(8,128)S(1)} all-gather(s32[1,128,8]{1,2,0:T(8,128)S(1)} %copy-done.52), channel_id=4, replica_groups=mesh['seq'=8,'batch'=4] {'seq','batch'}, dimensions={1}, use_global_device_ids=true | all-gather | bytes 135168 | tf_op jit(solution)/shard_map/all_gather | solution.py:326
  363.9 1.7 copy.269
  369.3 23.8 %convolution_convert_fusion.1 = bf16[32,256,2048]{2,1,0:T(8,128)(2,1)} fusion(pred[32,256,128]{2,1,0:T(32,128)(4,1)S(1)} %bitcast_compare_fusion, bf16[32,128,2048]{2,1,0:T(8,128)(2,1)} %bitcast.236), kind=kOutput, calls=%fused_computation.3 | convolution fusion | flops 4311744512 | bytes 51380224 | tf_op jit(solution)/shard_map/dst,dth->dsh/dot_general | solution.py:339
  393.1 23.0 %copy.280 = bf16[32,8,32,2048]{3,2,0,1:T(8,128)(2,1)} copy(bf16[32,8,32,2048]{3,2,1,0:T(8,128)(2,1)} %bitcast.223) | data formatting | bytes 67108864 | tf_op jit(solution)/shard_map/reshape | solution.py:342
  416.2 20.9 %all-gather.15.cloned.1.call-done = bf16[4096,2048]{1,0:T(8,128)(2,1)} async-done(((bf16[128,2048]{1,0:T(8,128)(2,1)}), bf16[4096,2048]{1,0:T(8,128)(2,1)}) %all-gather.15.cloned.1.call-update) | async-done | bytes 16777232 | tf_op jit(solution)/shard_map/all_gather | solution.py:328
  437.1 23.3 %convolution_convert_fusion.2 = bf16[32,256,2048]{2,1,0:T(8,128)(2,1)} fusion(pred[32,256,128]{2,1,0:T(32,128)(4,1)S(1)} %bitcast_compare_fusion, bf16[32,128,2048]{2,1,0:T(8,128)(2,1)} %bitcast.227), kind=kOutput, calls=%fused_computation.4 | convolution fusion | flops 4311744512 | bytes 51380224 | tf_op jit(solution)/shard_map/dst,dth->dsh/dot_general | solution.py:339
  460.4 22.9 %copy.271 = bf16[32,8,32,2048]{3,2,0,1:T(8,128)(2,1)} copy(bf16[32,8,32,2048]{3,2,1,0:T(8,128)(2,1)} %bitcast.224) | data formatting | bytes 67108864 | tf_op jit(solution)/shard_map/reshape | solution.py:342
  483.3 19.9 %fusion.6 = f32[8,1024,256]{1,2,0:T(8,128)} fusion(bf16[8,1024,2048]{2,1,0:T(8,128)(2,1)} %bitcast.232, bf16[8,3,2048,256]{3,2,1,0:T(8,128)(2,1)} %param.16), kind=kOutput, calls=%fused_computation.17 | convolution fusion | flops 8589934592 | bytes 50331648 | tf_op jit(solution)/shard_map/esd,edf->esf/dot_general | solution.py:288
  503.3 20.0 %fusion.10 = f32[8,1024,256]{1,2,0:T(8,128)} fusion(bf16[8,1024,2048]{2,1,0:T(8,128)(2,1)} %bitcast.233, bf16[8,3,2048,256]{3,2,1,0:T(8,128)(2,1)} %param.16), kind=kOutput, calls=%fused_computation.21 | convolution fusion | flops 8589934592 | bytes 50331648 | tf_op jit(solution)/shard_map/esd,edf->esf/dot_general | solution.py:287
  523.3 25.7 %fusion.1 = (f32[8,1024]{1,0:T(8,128)S(1)}, bf16[8,1024,256]{1,2,0:T(8,128)(2,1)}, f32[8,1024,256]{1,2,0:T(8,128)}) fusion(f32[8,1024,256]{1,2,0:T(8,128)} %fusion.6, f32[8,1024,256]{1,2,0:T(8,128)} %fusion.10, bf16[8,1024,2048]{2,1,0:T(8,128)(2,1)} %bitcast.230, bf16[8,3,2048,256]{3,2,1,0:T(8,128)(2,1)} %param.16), kind=kOutput, calls=%fused_computation.12 | convolution fusion | flops 8608800768 | bytes 71335936 | tf_op jit(solution)/shard_map/esd,edf->esf/dot_general | solution.py:293
  549.2 11.0 fusion.99
  560.3 3.3 select_reduce_fusion
  563.9 13.5 multiply_convert_fusion.1
  577.4 27.6 %fusion.8 = f32[8,1024,2048]{2,1,0:T(8,128)} fusion(bf16[8,1024,256]{1,2,0:T(8,128)(2,1)} %get-tuple-element.80, bf16[8,3,2048,256]{3,2,1,0:T(8,128)(2,1)} %param.16), kind=kOutput, calls=%fused_computation.19 | convolution fusion | flops 8589934592 | bytes 79691776 | tf_op jit(solution)/shard_map/esf,edf->esd/dot_general | solution.py:299
  605.0 36.8 %add_convert_fusion = bf16[8,1024,2048]{2,1,0:T(8,128)(2,1)} fusion(f32[8,1024,2048]{2,1,0:T(8,128)} %fusion.8, bf16[8,1024,256]{1,2,0:T(8,128)(2,1)} %get-tuple-element.79, bf16[8,3,2048,256]{3,2,1,0:T(8,128)(2,1)} %param.16), kind=kOutput, calls=%fused_computation | convolution fusion | flops 8623489024 | bytes 113246208 | tf_op jit(solution)/shard_map/esf,edf->esd/dot_general | solution.py:300
  641.8 23.0 %copy.286 = bf16[32,8,32,2048]{3,2,1,0:T(8,128)(2,1)} copy(bf16[32,8,32,2048]{3,2,0,1:T(8,128)(2,1)} %bitcast.225) | data formatting | bytes 67108864 | tf_op jit(solution)/shard_map/transpose | solution.py:346
  664.7 19.1 %convolution_convert_fusion.3 = bf16[32,128,2048]{2,1,0:T(8,128)(2,1)} fusion(pred[32,256,128]{2,1,0:T(32,128)(4,1)S(1)} %copy-done.1, bf16[32,256,2048]{2,1,0:T(8,128)(2,1)} %bitcast.222), kind=kOutput, calls=%fused_computation.5 | convolution fusion | flops 4303355904 | bytes 51380224 | tf_op jit(solution)/shard_map/dst,dsh->dth/dot_general | solution.py:349
  685.3 3.8 all-to-all-start.1
  689.1 6.7 all-to-all-done.1
  695.8 169.2 %reduce-scatter.18.cloned.1.call-done = bf16[128,2048]{1,0:T(8,128)(2,1)} async-done(((bf16[4096,2048]{1,0:T(8,128)(2,1)}), bf16[128,2048]{1,0:T(8,128)(2,1)}) %reduce-scatter.18.cloned.1.call-update) | async-done | bytes 524304 | tf_op jit(solution)/shard_map/reduce_scatter | solution.py:363
  865.0 1.7 multiply_reduce_fusion
  867.8 2.3 fusion.92
  870.4 75.0 %all-gather.17.cloned.1.call-done = bf16[1024,2048]{1,0:T(8,128)(2,1)} async-done(((bf16[128,2048]{1,0:T(8,128)(2,1)}), bf16[1024,2048]{1,0:T(8,128)(2,1)}) %all-gather.17.cloned.1.call-update) | async-done | bytes 4194320 | tf_op jit(solution)/shard_map/all_gather | solution.py:111
  945.4 4.2 multiply_reduce_fusion.3
  949.6 7.1 fusion.46
  956.8 3.2 multiply_convert_fusion
  960.1 1.5 convolution_bitcast_fusion.3
  964.4 19.4 %psum.15 = f32[2,1024]{1,0:T(2,128)S(1)} all-reduce(f32[2,1024]{1,0:T(2,128)S(1)} %pad_maximum_fusion.8), channel_id=1, replica_groups=mesh['seq'=8,'batch'=4] {'seq'}, use_global_device_ids=true, to_apply=%region_26.27 | all-reduce | flops 2048 | bytes 16384 | tf_op jit(solution)/shard_map/psum | solution.py:132
  983.8 2.3 multiply_convert_fusion.5
  986.2 8.2 convolution_convert_fusion.7
  994.4 7.6 convolution_convert_fusion.6
  1002.2 18.4 %convolution_convert_fusion = bf16[8,1024,2048]{2,1,0:T(8,128)(2,1)} fusion(bf16[8,3,2048,256]{3,2,1,0:T(8,128)(2,1)} %param.16, bf16[8,1024,256]{1,2,0:T(8,128)(2,1)} %get-tuple-element.78, f32[8,1024]{1,0:T(8,128)S(1)} %mul.414), kind=kOutput, calls=%fused_computation.2 | convolution fusion | flops 8613003264 | bytes 46170112 | tf_op jit(solution)/shard_map/esf,edf->esd/dot_general | solution.py:302
  1020.6 23.6 %copy.278 = bf16[32,8,32,2048]{3,2,1,0:T(8,128)(2,1)} copy(bf16[32,8,32,2048]{3,2,0,1:T(8,128)(2,1)} %bitcast.226) | data formatting | bytes 67108864 | tf_op jit(solution)/shard_map/transpose | solution.py:346
  1045.3 4.4 convolution_convert_fusion.8
  1049.8 19.6 %convolution_convert_fusion.4 = bf16[32,128,2048]{2,1,0:T(8,128)(2,1)} fusion(pred[32,256,128]{2,1,0:T(32,128)(4,1)S(1)} %copy-done.1, bf16[32,256,2048]{2,1,0:T(8,128)(2,1)} %bitcast.221), kind=kOutput, calls=%fused_computation.6 | convolution fusion | flops 4303355904 | bytes 51380224 | tf_op jit(solution)/shard_map/dst,dsh->dth/dot_general | solution.py:349
  1069.4 21.2 %convolution_bitcast_fusion.1 = f32[8,1,2048,256]{3,2,0,1:T(8,128)} fusion(bf16[8,1024,2048]{2,1,0:T(8,128)(2,1)} %bitcast.234, bf16[8,1024,256]{1,2,0:T(8,128)(2,1)} %get-tuple-element.79), kind=kOutput, calls=%fused_computation.45 | convolution fusion | flops 8589934592 | bytes 54525952 | tf_op jit(solution)/shard_map/esd,esf->edf/dot_general | solution.py:306
  1090.6 21.1 %convolution_bitcast_fusion.2 = f32[8,1,2048,256]{3,2,0,1:T(8,128)} fusion(bf16[8,1024,2048]{2,1,0:T(8,128)(2,1)} %bitcast.235, bf16[8,1024,256]{1,2,0:T(8,128)(2,1)} %get-tuple-element.80), kind=kOutput, calls=%fused_computation.46 | convolution fusion | flops 8589934592 | bytes 54525952 | tf_op jit(solution)/shard_map/esd,esf->edf/dot_general | solution.py:305
  1111.7 21.9 %convolution_bitcast_fusion = f32[8,1,2048,256]{3,2,0,1:T(8,128)} fusion(bf16[8,1024,2048]{2,1,0:T(8,128)(2,1)} %bitcast.231, bf16[8,1024,256]{1,2,0:T(8,128)(2,1)} %get-tuple-element.78, f32[8,1024]{1,0:T(8,128)S(1)} %mul.414), kind=kOutput, calls=%fused_computation.44 | convolution fusion | flops 8596226048 | bytes 54558720 | tf_op jit(solution)/shard_map/esd,esf->edf/dot_general | solution.py:307
  1133.9 3.6 all-to-all-start.2
  1137.8 1.5 fusion.57
  1140.6 35.1 %pad_maximum_fusion = f32[8,3,2048,256]{3,2,0,1:T(8,128)} fusion(f32[8,1,2048,256]{3,2,0,1:T(8,128)} %convolution_bitcast_fusion, f32[8,1,2048,256]{3,2,0,1:T(8,128)} %convolution_bitcast_fusion.1, f32[8,1,2048,256]{3,2,0,1:T(8,128)} %convolution_bitcast_fusion.2), kind=kLoop, calls=%fused_computation.1 | loop fusion | flops 25165824 | bytes 100663296 | tf_op jit(solution)/shard_map/stack | solution.py:303
  1175.7 33.7 %copy.303 = f32[8,3,2048,256]{3,2,1,0:T(8,128)} copy(f32[8,3,2048,256]{3,2,0,1:T(8,128)} %pad_maximum_fusion) | data formatting | bytes 100663296
  1210.6 1.8 convert_element_type.196
  1212.5 1.8 reshape.316
  1214.3 2.5 copy.295
  1216.8 1.6 copy.341
  1218.4 138.8 %reduce-scatter.16.cloned.1.call-done = bf16[128,2048]{1,0:T(8,128)(2,1)} async-done(((bf16[4096,2048]{1,0:T(8,128)(2,1)}), bf16[128,2048]{1,0:T(8,128)(2,1)}) %reduce-scatter.16.cloned.1.call-update) | async-done | bytes 524304 | tf_op jit(solution)/shard_map/reduce_scatter | solution.py:364
  1357.2 3.1 fusion.55
  1360.4 136.0 %reduce-scatter.28.cloned.1.call-done = f32[64,66]{1,0:T(8,128)} async-done(((f32[2048,66]{1,0:T(8,128)}), f32[64,66]{1,0:T(8,128)}) %reduce-scatter.28.cloned.1.call-update) | async-done | bytes 16912
  (225 shorter events, 28.6 us)
Async XLA Ops:
  8.0 113.0 %all-gather.19.cloned.1.call-start = ((), (), s32[]{:S(2)}) async-start(), calls=%async_computation.23 | async-start | bytes 4718592 | tf_op jit(solution)/shard_map/all_gather | solution.py:53
  8.7 121.2 %all-gather.11.cloned.1.call-start = ((), (), s32[]{:S(2)}) async-start(), calls=%async_computation.12 | async-start | bytes 3932160 | tf_op jit(solution)/shard_map/all_gather | solution.py:59
  53.9 115.8 %all-gather.13.cloned.1.call-start = ((), (), s32[]{:S(2)}) async-start(), calls=%async_computation.13 | async-start | bytes 1310720 | tf_op jit(solution)/shard_map/all_gather | solution.py:60
  54.6 264.7 %reduce-scatter.14.cloned.1.call-start = ((), (), s32[]{:S(2)}) async-start(), calls=%async_computation.14 | async-start | bytes 4718592 | tf_op jit(solution)/shard_map/reduce_scatter | solution.py:98
  114.9 4.6 copy-start.7
  120.0 38.7 %copy-start.45 = (f32[256]{0:T(256)}, f32[256]{0:T(256)S(1)}, u32[]{:S(2)}) copy-start(f32[256]{0:T(256)S(1)} %get-tuple-element.73) | copy-start | bytes 3076
  120.0 38.7 %copy-start.47 = (f32[256]{0:T(256)}, f32[256]{0:T(256)S(1)}, u32[]{:S(2)}) copy-start(f32[256]{0:T(256)S(1)} %get-tuple-element.74) | copy-start | bytes 3076
  120.9 15.6 %copy-start.35 = (f32[2048]{0:T(1024)}, f32[2048]{0:T(1024)S(1)}, u32[]{:S(2)}) copy-start(f32[2048]{0:T(1024)S(1)} %get-tuple-element.69) | copy-start | bytes 24580
  120.9 199.7 %copy-start.32 = (f32[2048]{0:T(1024)}, f32[2048]{0:T(1024)S(1)}, u32[]{:S(2)}) copy-start(f32[2048]{0:T(1024)S(1)} %get-tuple-element.68) | copy-start | bytes 24580
  124.1 12.5 copy-start.53
  136.6 25.9 %copy-start.2 = (f32[1024,768]{0,1:T(8,128)}, f32[1024,768]{0,1:T(8,128)S(1)}, u32[]{:S(2)}) copy-start(f32[1024,768]{0,1:T(8,128)S(1)} %fusion.51) | copy-start | bytes 9437188
  160.5 4.1 copy-start.19
  160.5 4.1 copy-start.23
  162.5 3.4 copy-start.9
  162.5 3.3 copy-start.41
  162.6 3.5 copy-start.30
  164.6 5.0 copy-start.43
  169.6 194.3 %copy-start.26 = (bf16[1024,2,128]{0,2,1:T(8,128)(2,1)}, bf16[1024,2,128]{0,2,1:T(8,128)(2,1)S(1)}, u32[]{:S(2)}) copy-start(bf16[1024,2,128]{0,2,1:T(8,128)(2,1)S(1)} %get-tuple-element.117) | copy-start | bytes 1572868
  169.6 149.7 %copy-start.4 = (bf16[1,128,2048]{2,1,0:T(8,128)(2,1)S(1)}, bf16[1,128,2048]{2,1,0:T(8,128)(2,1)}, u32[]{:S(2)}) copy-start(bf16[1,128,2048]{2,1,0:T(8,128)(2,1)} %param.9) | copy-start | bytes 1572868
  169.6 153.3 %copy-start.52 = (s32[1,128,8]{1,2,0:T(8,128)S(1)}, s32[1,128,8]{1,2,0:T(8,128)}, u32[]{:S(2)}) copy-start(s32[1,128,8]{1,2,0:T(8,128)} %param.11) | copy-start | bytes 12292
  174.4 194.9 %all-gather.21.cloned.1.call-start = ((), (), s32[]{:S(2)}) async-start(), calls=%async_computation.24 | async-start | bytes 17301504 | tf_op jit(solution)/shard_map/all_gather | solution.py:327
  175.0 262.1 %all-gather.15.cloned.1.call-start = ((), (), s32[]{:S(2)}) async-start(), calls=%async_computation.15 | async-start | bytes 17301504 | tf_op jit(solution)/shard_map/all_gather | solution.py:328
  320.6 43.3 %copy-start.49 = (f32[128]{0:T(128)}, f32[128]{0:T(128)S(1)}, u32[]{:S(2)}) copy-start(f32[128]{0:T(128)S(1)} %add_rsqrt_fusion.3) | copy-start | bytes 1540
  322.7 362.5 %reduce-scatter.20.cloned.1.call-start = ((), (), s32[]{:S(2)}) async-start(), calls=%async_computation.18 | async-start | bytes 163840 | tf_op jit(solution)/shard_map/reduce_scatter | solution.py:360
  369.3 67.8 %copy-start = (pred[32,256,128]{2,1,0:T(32,128)(4,1)}, pred[32,256,128]{2,1,0:T(32,128)(4,1)S(1)}, u32[]{:S(2)}) copy-start(pred[32,256,128]{2,1,0:T(32,128)(4,1)S(1)} %bitcast_compare_fusion) | copy-start | bytes 3145732
  523.3 25.9 %copy-start.8 = (bf16[2048,68]{1,0:T(8,128)(2,1)S(1)}, bf16[2048,68]{1,0:T(8,128)(2,1)}, u32[]{:S(2)}) copy-start(bf16[2048,68]{1,0:T(8,128)(2,1)} %copy-done.7) | copy-start | bytes 835588
  563.8 301.2 %reduce-scatter.18.cloned.1.call-start = ((), (), s32[]{:S(2)}) async-start(), calls=%async_computation.17 | async-start | bytes 17301504 | tf_op jit(solution)/shard_map/reduce_scatter | solution.py:363
  641.8 23.0 %copy-start.1 = (pred[32,256,128]{2,1,0:T(32,128)(4,1)S(1)}, pred[32,256,128]{2,1,0:T(32,128)(4,1)}, u32[]{:S(2)}) copy-start(pred[32,256,128]{2,1,0:T(32,128)(4,1)} %copy-done) | copy-start | bytes 3145732
  683.9 181.2 %copy-start.5 = (bf16[1,128,2048]{2,1,0:T(8,128)(2,1)S(1)}, bf16[1,128,2048]{2,1,0:T(8,128)(2,1)}, u32[]{:S(2)}) copy-start(bf16[1,128,2048]{2,1,0:T(8,128)(2,1)} %param.9) | copy-start | bytes 1572868
  683.9 181.2 %copy-start.10 = (bf16[128,2048]{1,0:T(8,128)(2,1)S(1)}, bf16[128,2048]{1,0:T(8,128)(2,1)}, u32[]{:S(2)}) copy-start(bf16[128,2048]{1,0:T(8,128)(2,1)} %reduce-scatter.14.cloned.1.call-done) | copy-start | bytes 1572868
  683.9 181.2 %copy-start.33 = (f32[2048]{0:T(1024)S(1)}, f32[2048]{0:T(1024)}, u32[]{:S(2)}) copy-start(f32[2048]{0:T(1024)} %copy-done.32) | copy-start | bytes 24580
  683.9 181.2 %copy-start.50 = (f32[128]{0:T(128)S(1)}, f32[128]{0:T(128)}, u32[]{:S(2)}) copy-start(f32[128]{0:T(128)} %copy-done.49) | copy-start | bytes 1540
  684.9 185.5 %copy-start.42 = (f32[2,1024]{1,0:T(2,128)S(1)}, f32[2,1024]{1,0:T(2,128)}, u32[]{:S(2)}) copy-start(f32[2,1024]{1,0:T(2,128)} %copy-done.41) | copy-start | bytes 24580
  684.9 185.5 %copy-start.44 = (f32[2,1024]{1,0:T(2,128)S(1)}, f32[2,1024]{1,0:T(2,128)}, u32[]{:S(2)}) copy-start(f32[2,1024]{1,0:T(2,128)} %copy-done.43) | copy-start | bytes 24580
  685.3 10.5 all-to-all-start.1
  689.0 256.3 %all-gather.17.cloned.1.call-start = ((), (), s32[]{:S(2)}) async-start(), calls=%async_computation.19 | async-start | bytes 4718592 | tf_op jit(solution)/shard_map/all_gather | solution.py:111
  866.8 90.0 %copy-start.55 = (f32[128]{0:T(128)}, f32[128]{0:T(128)S(1)}, u32[]{:S(2)}) copy-start(f32[128]{0:T(128)S(1)} %broadcast_multiply_fusion.7) | copy-start | bytes 1540
  870.1 263.8 %reduce-scatter.24.cloned.1.call-start = ((), (), s32[]{:S(2)}) async-start(), calls=%async_computation.21 | async-start | bytes 3932160 | tf_op jit(solution)/shard_map/reduce_scatter | solution.py:145
  945.4 11.4 slice-start
  949.6 7.1 copy-start.16
  949.6 7.1 copy-start.31
  949.6 7.1 slice-start.1
  956.8 3.3 copy-start.24
  956.8 4.8 copy-start.13
  956.8 4.8 copy-start.20
  961.6 2.0 copy-start.3
  962.7 23.4 %copy-start.36 = (f32[2048]{0:T(1024)S(1)}, f32[2048]{0:T(1024)}, u32[]{:S(2)}) copy-start(f32[2048]{0:T(1024)} %copy-done.35) | copy-start | bytes 24580
  962.7 23.4 %copy-start.54 = (f32[1024]{0:T(1024)S(1)}, f32[1024]{0:T(1024)}, u32[]{:S(2)}) copy-start(f32[1024]{0:T(1024)} %copy-done.53) | copy-start | bytes 12292
  986.1 8.2 copy-start.28
  986.2 8.2 copy-start.29
  986.2 8.3 copy-start.57
  994.4 143.4 %reduce-scatter.22.cloned.1.call-start = ((), (), s32[]{:S(2)}) async-start(), calls=%async_computation.20 | async-start | bytes 4718592 | tf_op jit(solution)/shard_map/reduce_scatter | solution.py:142
  1002.1 207.4 %reduce-scatter.30.cloned.1.call-start = ((), (), s32[]{:S(2)}) async-start(), calls=%async_computation.26 | async-start | bytes 163840
  1020.6 24.7 %copy-start.27 = (bf16[1024,2,128]{0,2,1:T(8,128)(2,1)S(1)}, bf16[1024,2,128]{0,2,1:T(8,128)(2,1)}, u32[]{:S(2)}) copy-start(bf16[1024,2,128]{0,2,1:T(8,128)(2,1)} %copy-done.26) | copy-start | bytes 1572868
  1045.1 165.6 %reduce-scatter.26.cloned.1.call-start = ((), (), s32[]{:S(2)}) async-start(), calls=%async_computation.22 | async-start | bytes 1310720 | tf_op jit(solution)/shard_map/reduce_scatter | solution.py:113
  1049.7 307.4 %reduce-scatter.16.cloned.1.call-start = ((), (), s32[]{:S(2)}) async-start(), calls=%async_computation.16 | async-start | bytes 17301504 | tf_op jit(solution)/shard_map/reduce_scatter | solution.py:364
  1133.9 78.6 %all-to-all-start.2 = ((bf16[8,64,768]{2,1,0:T(8,128)(2,1)}), bf16[8,64,768]{2,1,0:T(8,128)(2,1)S(1)}, u32[]{:S(2)}, u32[]{:S(2)}) async-start(bf16[8,64,768]{2,1,0:T(8,128)(2,1)} %reduce-scatter.24.cloned.1.call-done), calls=%async_computation.8 | async-start | bytes 1572864 | tf_op jit(solution)/shard_map/all_to_all | solution.py:148
  1137.5 358.9 %reduce-scatter.28.cloned.1.call-start = ((), (), s32[]{:S(2)}) async-start(), calls=%async_computation.25 | async-start | bytes 1081344
  1209.5 147.7 %copy-start.11 = (bf16[128,2048]{1,0:T(8,128)(2,1)S(1)}, bf16[128,2048]{1,0:T(8,128)(2,1)}, u32[]{:S(2)}) copy-start(bf16[128,2048]{1,0:T(8,128)(2,1)} %reduce-scatter.14.cloned.1.call-done) | copy-start | bytes 1572868
  1209.5 147.7 %copy-start.14 = (bf16[1,128,2048]{2,1,0:T(8,128)(2,1)S(1)}, bf16[1,128,2048]{2,1,0:T(8,128)(2,1)}, u32[]{:S(2)}) copy-start(bf16[1,128,2048]{2,1,0:T(8,128)(2,1)} %param.17) | copy-start | bytes 1572868
  1209.5 147.7 %copy-start.18 = (f32[128,2048]{1,0:T(8,128)S(1)}, f32[128,2048]{1,0:T(8,128)}, u32[]{:S(2)}) copy-start(f32[128,2048]{1,0:T(8,128)} %copy-done.17) | copy-start | bytes 3145732
  1209.5 147.7 %copy-start.34 = (f32[2048]{0:T(1024)S(1)}, f32[2048]{0:T(1024)}, u32[]{:S(2)}) copy-start(f32[2048]{0:T(1024)} %copy-done.32) | copy-start | bytes 24580
  1209.5 147.7 %copy-start.51 = (f32[128]{0:T(128)S(1)}, f32[128]{0:T(128)}, u32[]{:S(2)}) copy-start(f32[128]{0:T(128)} %copy-done.49) | copy-start | bytes 1540
  1209.5 147.7 %copy-start.56 = (f32[128]{0:T(128)S(1)}, f32[128]{0:T(128)}, u32[]{:S(2)}) copy-start(f32[128]{0:T(128)} %copy-done.55) | copy-start | bytes 1540
  (13 other events, 17.5 us)
Sparse Core Ops, SparseCore 0:
  11.0 90.2 all-gather.18
  103.4 26.4 all-gather.10
  131.5 16.7 all-gather.12
  174.5 144.7 reduce-scatter.13
  564.0 17.7 reduce-scatter.19
  684.0 180.9 reduce-scatter.17
  870.2 75.1 all-gather.16
  994.5 35.1 reduce-scatter.23
  1033.8 87.8 reduce-scatter.21
  1124.6 19.3 reduce-scatter.29
  1147.2 24.8 reduce-scatter.25
  1174.3 182.8 reduce-scatter.15
  1360.0 136.3 reduce-scatter.27
Sparse Core Ops, SparseCore 1:
  178.2 137.7 all-gather.20
  322.8 114.2 all-gather.14

commit v2 on v1

--- a/solution.py
+++ b/solution.py
@@ -1,6 +1,10 @@
+import functools
+
 import jax
 import jax.numpy as jnp
 from jax import lax
+from jax.experimental import pallas as pl
+from jax.experimental.pallas import tpu as pltpu
 from jax.sharding import PartitionSpec as P
 
 HEADS = 16
@@ -9,6 +13,7 @@
 BOTH = ("seq", "batch")
 f32 = jnp.float32
 bf16 = jnp.bfloat16
+MESH = pl.DeviceIdType.MESH
 
 
 def rms_scale(values):
@@ -37,35 +42,800 @@
     return lax.dot_general(a, b, (dims, ((), ())), preferred_element_type=f32)
 
 
+ANY = pl.BlockSpec(memory_space=pl.ANY)
+WHOLE = pl.BlockSpec(memory_space=pltpu.VMEM)
+
+
+class Place:
+    def __init__(self):
+        s, b = lax.axis_index("seq"), lax.axis_index("batch")
+        self.z, self.y = s // 2, lax.rem(s, 2)
+        self.x, self.c = b // 2, lax.rem(b, 2)
+
+    def at(self, r=0, y=0, x=0, c=0):
+        z = lax.rem(self.z + r, 4)
+        yy = 1 - self.y if y else self.y
+        xx = 1 - self.x if x else self.x
+        cc = 1 - self.c if c else self.c
+        return (z * 2 + yy, xx * 2 + cc)
+
+    def index(self, r=0, y=0, x=0, c=0):
+        s, b = self.at(r, y, x, c)
+        return s * 4 + b
+
+
+def barrier(peers):
+    sem = pltpu.get_barrier_semaphore()
+    for peer in peers:
+        pl.semaphore_signal(sem, inc=1, device_id=peer, device_id_type=MESH)
+    pl.semaphore_wait(sem, len(peers))
+
+
+class Sends:
+    def __init__(self, send_sem, recv_sem):
+        self.send_sem, self.recv_sem, self.copies = send_sem, recv_sem, []
+
+    def start(self, src, dst, peer):
+        k = len(self.copies)
+        copy = pltpu.make_async_remote_copy(
+            src_ref=src,
+            dst_ref=dst,
+            send_sem=self.send_sem.at[k],
+            recv_sem=self.recv_sem.at[k],
+            device_id=peer,
+            device_id_type=MESH,
+        )
+        copy.start()
+        self.copies.append(copy)
+        return copy
+
+    def finish(self):
+        for copy in self.copies:
+            copy.wait_send()
+
+
+def gather_all_kernel(x_ref, out_ref, send_sem, recv_sem, own_sem):
+    p = Place()
+    rows = x_ref.shape[0]
+    half = rows // 2
+    barrier([p.at(1), p.at(2), p.at(3), p.at(y=1), p.at(x=1), p.at(c=1)])
+    own = pltpu.make_async_copy(x_ref, out_ref.at[p.index()], own_sem)
+    own.start()
+    sends = Sends(send_sem, recv_sem)
+    A, B = pl.ds(0, half), pl.ds(half, half)
+
+    def forward(index, peer, part=None):
+        ref = out_ref.at[index] if part is None else out_ref.at[index, part]
+        return sends.start(ref, ref, peer)
+
+    mine = p.index()
+    along = [None] + [sends.start(x_ref, out_ref.at[mine], p.at(r)) for r in (1, 3, 2)]
+    along = {0: None, 1: along[1], 3: along[2], 2: along[3]}
+    from_x, from_y, from_core, diag = {}, {}, [], []
+    order = (0, 1, 3, 2)
+    for r in order:
+        index = p.index(-r % 4)
+        if r:
+            along[r].wait_recv()
+        src = x_ref if r == 0 else out_ref.at[index]
+        from_x[r] = sends.start(src, out_ref.at[index], p.at(x=1))
+        from_y[r] = sends.start(src, out_ref.at[index], p.at(y=1))
+        from_core.append(sends.start(src, out_ref.at[index], p.at(c=1)))
+    for r in order:
+        ix, iy = p.index(-r % 4, x=1), p.index(-r % 4, y=1)
+        from_x[r].wait_recv()
+        diag.append(forward(ix, p.at(y=1), A))
+        from_y[r].wait_recv()
+        diag.append(forward(iy, p.at(x=1), B))
+        from_core.append(forward(ix, p.at(c=1)))
+        from_core.append(forward(iy, p.at(c=1)))
+    for n, r in enumerate(order):
+        index = p.index(-r % 4, x=1, y=1)
+        diag[2 * n].wait_recv()
+        diag[2 * n + 1].wait_recv()
+        from_core.append(forward(index, p.at(c=1)))
+    for copy in from_core:
+        copy.wait_recv()
+    sends.finish()
+    own.wait()
+
+
+def gather_all(x, collective_id):
+    n = 3 + 12 + 8 + 12
+    return pl.pallas_call(
+        gather_all_kernel,
+        name="gather_all",
+        out_shape=jax.ShapeDtypeStruct((32,) + x.shape, x.dtype),
+        in_specs=[ANY],
+        out_specs=ANY,
+        scratch_shapes=[
+            pltpu.SemaphoreType.DMA((n,)),
+            pltpu.SemaphoreType.DMA((n,)),
+            pltpu.SemaphoreType.DMA,
+        ],
+        compiler_params=pltpu.CompilerParams(collective_id=collective_id, has_side_effects=True),
+    )(x)
+
+
+def add_rows(dst, src, start, rows):
+    step = 16
+
+    def body(i, _):
+        at = pl.ds(pl.multiple_of(start + i * step, step), step)
+        dst[at] = (dst[at].astype(f32) + src[at].astype(f32)).astype(dst.dtype)
+        return 0
+
+    lax.fori_loop(0, rows // step, body, 0)
+
+
+def scatter_all_kernel(p_ref, out_ref, acc, rc, rdx, rdy, rx, ry, rz, send_sem, recv_sem, own_sem):
+    p = Place()
+    rows = acc.shape[1]
+    half = rows // 2
+    A, B = pl.ds(0, half), pl.ds(half, half)
+    barrier([p.at(1), p.at(2), p.at(3), p.at(y=1), p.at(x=1), p.at(c=1)])
+    sends = Sends(send_sem, recv_sem)
+    order = (2, 1, 3, 0)
+    slots = [(r, y, x) for (y, x) in ((1, 1), (0, 1), (1, 0), (0, 0)) for r in order]
+    loads, cores = [], []
+    for k, (r, y, x) in enumerate(slots):
+        load = pltpu.make_async_copy(p_ref.at[p.index(r, y, x)], acc.at[k], own_sem.at[k])
+        load.start()
+        loads.append(load)
+        cores.append(sends.start(p_ref.at[p.index(r, y, x, 1)], rc.at[k], p.at(c=1)))
+
+    def core_sum(k):
+        loads[k].wait()
+        cores[k].wait_recv()
+        add_rows(acc.at[k], rc.at[k], 0, rows)
+
+    dx, dy, fx, fy, fz = [], [], [], [], []
+    for n in range(4):
+        core_sum(n)
+        dy.append(sends.start(acc.at[n, A], rdy.at[n], p.at(y=1)))
+        dx.append(sends.start(acc.at[n, B], rdx.at[n], p.at(x=1)))
+    for n in range(4):
+        core_sum(4 + n)
+        dy[n].wait_recv()
+        add_rows(acc.at[4 + n], rdy.at[n], 0, half)
+        fx.append(sends.start(acc.at[4 + n], rx.at[n], p.at(x=1)))
+        core_sum(8 + n)
+        dx[n].wait_recv()
+        add_rows(acc.at[8 + n, B], rdx.at[n], 0, half)
+        fy.append(sends.start(acc.at[8 + n], ry.at[n], p.at(y=1)))
+    for n, r in enumerate(order):
+        core_sum(12 + n)
+        fx[n].wait_recv()
+        add_rows(acc.at[12 + n], rx.at[n], 0, rows)
+        fy[n].wait_recv()
+        add_rows(acc.at[12 + n], ry.at[n], 0, rows)
+        if r:
+            fz.append(sends.start(acc.at[12 + n], rz.at[n], p.at(r)))
+    for copy in fz:
+        copy.wait_recv()
+
+    def total(i, _):
+        at = pl.ds(pl.multiple_of(i * 16, 16), 16)
+        value = acc[15, at].astype(f32)
+        for n in range(3):
+            value = value + rz[n, at].astype(f32)
+        out_ref[at] = value.astype(out_ref.dtype)
+        return 0
+
+    lax.fori_loop(0, rows // 16, total, 0)
+    sends.finish()
+
+
+def scatter_all(parts, collective_id, dtype=bf16):
+    block = parts.shape[1:]
+    half = (block[0] // 2,) + block[1:]
+    n = 16 + 8 + 8 + 3
+    return pl.pallas_call(
+        scatter_all_kernel,
+        name="scatter_all",
+        out_shape=jax.ShapeDtypeStruct(block, dtype),
+        in_specs=[ANY],
+        out_specs=WHOLE,
+        scratch_shapes=[
+            pltpu.VMEM((16,) + block, parts.dtype),
+            pltpu.VMEM((16,) + block, parts.dtype),
+            pltpu.VMEM((4,) + half, parts.dtype),
+            pltpu.VMEM((4,) + half, parts.dtype),
+            pltpu.VMEM((4,) + block, parts.dtype),
+            pltpu.VMEM((4,) + block, parts.dtype),
+            pltpu.VMEM((3,) + block, parts.dtype),
+            pltpu.SemaphoreType.DMA((n,)),
+            pltpu.SemaphoreType.DMA((n,)),
+            pltpu.SemaphoreType.DMA((16,)),
+        ],
+        compiler_params=pltpu.CompilerParams(
+            collective_id=collective_id, has_side_effects=True, vmem_limit_bytes=48 << 20
+        ),
+    )(parts)
+
+
+def call(kernel, name, collective_id, out_shape, in_specs, out_specs, scratch, copies, local=1, vmem=32):
+    return pl.pallas_call(
+        kernel,
+        name=name,
+        out_shape=out_shape,
+        in_specs=in_specs,
+        out_specs=out_specs,
+        scratch_shapes=[
+            *scratch,
+            pltpu.SemaphoreType.DMA((copies,)),
+            pltpu.SemaphoreType.DMA((copies,)),
+            pltpu.SemaphoreType.DMA((local,)),
+        ],
+        compiler_params=pltpu.CompilerParams(
+            collective_id=collective_id, has_side_effects=True, vmem_limit_bytes=vmem << 20
+        ),
+    )
+
+
+Z_ORDER = (1, 3, 2)
+
+
+def gather_first_kernel(
+    h_ref, wi_ref, wo_ref, ints_ref, small_ref,
+    h_out, wi_out, wo_out, ints_out, small_out,
+    ints, small, send_sem, recv_sem, own_sem,
+):
+    p = Place()
+    seq, b = p.at()
+    x, c = p.x, p.c
+    others = [p.at(r, y) for y in (0, 1) for r in range(4) if r or y]
+    barrier(others + [p.at(x=1), p.at(c=1)])
+    sends = Sends(send_sem, recv_sem)
+    owns = [
+        pltpu.make_async_copy(h_ref, h_out.at[seq], own_sem.at[0]),
+        pltpu.make_async_copy(wi_ref.at[seq], wi_out.at[seq, b], own_sem.at[1]),
+        pltpu.make_async_copy(wo_ref, wo_out.at[b], own_sem.at[2]),
+    ]
+    for own in owns:
+        own.start()
+    me = p.index()
+    pairs = ((ints_ref, ints), (small_ref, small))
+    for src, dst in pairs:
+        dst[me] = src[...]
+    first = [sends.start(dst.at[me], dst.at[me], p.at(c=1)) for _, dst in pairs]
+    h_z = {r: sends.start(h_ref, h_out.at[seq], p.at(r)) for r in Z_ORDER}
+    h_y = [sends.start(h_ref, h_out.at[seq], p.at(y=1))]
+    w_s = {}
+    for r, y in ((0, 1), (1, 0), (3, 0), (2, 0), (1, 1), (3, 1), (2, 1)):
+        to = p.at(r, y)
+        w_s[r, y] = sends.start(wi_ref.at[to[0]], wi_out.at[seq, b], to)
+    w_x = [sends.start(wi_ref.at[seq], wi_out.at[seq, b], p.at(x=1))]
+    w_c = [sends.start(wi_ref.at[seq], wi_out.at[seq, b], p.at(c=1))]
+    o_x = sends.start(wo_ref, wo_out.at[b], p.at(x=1))
+    w_c.append(sends.start(wo_ref, wo_out.at[b], p.at(c=1)))
+    for copy in first:
+        copy.wait_recv()
+    base = me - c
+    second = [sends.start(dst.at[pl.ds(base, 2)], dst.at[pl.ds(base, 2)], p.at(x=1)) for _, dst in pairs]
+    for copy in second:
+        copy.wait_recv()
+    base = me - b
+    third = [sends.start(dst.at[pl.ds(base, 4)], dst.at[pl.ds(base, 4)], p.at(y=1)) for _, dst in pairs]
+    for copy in third:
+        copy.wait_recv()
+    base = p.z * 8
+    fourth = [
+        sends.start(dst.at[pl.ds(base, 8)], dst.at[pl.ds(base, 8)], p.at(r)) for _, dst in pairs for r in Z_ORDER
+    ]
+    for r in Z_ORDER:
+        h_z[r].wait_recv()
+        s = p.at(-r % 4)[0]
+        h_y.append(sends.start(h_out.at[s], h_out.at[s], p.at(y=1)))
+    for r, y in ((0, 1), (1, 0), (3, 0), (2, 0), (1, 1), (3, 1), (2, 1)):
+        w_s[r, y].wait_recv()
+        s = p.at(-r % 4, y)[0]
+        w_x.append(sends.start(wi_out.at[s, b], wi_out.at[s, b], p.at(x=1)))
+        w_c.append(sends.start(wi_out.at[s, b], wi_out.at[s, b], p.at(c=1)))
+    bx = p.at(x=1)[1]
+    o_x.wait_recv()
+    w_c.append(sends.start(wo_out.at[bx], wo_out.at[bx], p.at(c=1)))
+    places = [(0, 0), (0, 1), (1, 0), (3, 0), (2, 0), (1, 1), (3, 1), (2, 1)]
+    for copy, (r, y) in zip(w_x, places):
+        copy.wait_recv()
+        s = p.at(-r % 4, y)[0]
+        w_c.append(sends.start(wi_out.at[s, bx], wi_out.at[s, bx], p.at(c=1)))
+    for copy in fourth + h_y + w_c:
+        copy.wait_recv()
+    ints_out[...] = ints[...]
+    small_out[...] = small[...]
+    sends.finish()
+    for own in owns:
+        own.wait()
+
+
+def gather_first(hidden, w_in, w_out, ints, small, collective_id):
+    own = w_in.shape[0]
+    parts = jnp.transpose(w_in.reshape(own, 3, 8, -1), (2, 0, 1, 3)).reshape(8, own, -1)
+    struct = jax.ShapeDtypeStruct
+    outs = call(
+        gather_first_kernel,
+        "gather_first",
+        collective_id,
+        (
+            struct((8,) + hidden.shape, bf16),
+            struct((8, 4) + parts.shape[1:], bf16),
+            struct((4,) + w_out.shape, bf16),
+            struct((32,) + ints.shape, ints.dtype),
+            struct((32,) + small.shape, small.dtype),
+        ),
+        [ANY, ANY, ANY, WHOLE, WHOLE],
+        (ANY, ANY, ANY, WHOLE, WHOLE),
+        [pltpu.VMEM((32,) + ints.shape, ints.dtype), pltpu.VMEM((32,) + small.shape, small.dtype)],
+        2 + 3 + 1 + 7 + 1 + 1 + 2 + 2 + 2 + 6 + 3 + 14 + 1 + 8,
+        3,
+    )(hidden, parts, w_out, ints, small)
+    return outs
+
+
+def gather_seq_kernel(h_ref, h_out, send_sem, recv_sem, own_sem):
+    p = Place()
+    seq, b = p.at()
+    barrier([p.at(1), p.at(2), p.at(3), p.at(y=1)])
+    sends = Sends(send_sem, recv_sem)
+    own = pltpu.make_async_copy(h_ref, h_out.at[seq], own_sem.at[0])
+    own.start()
+    h_z = {r: sends.start(h_ref, h_out.at[seq], p.at(r)) for r in Z_ORDER}
+    h_y = [sends.start(h_ref, h_out.at[seq], p.at(y=1))]
+    for r in Z_ORDER:
+        h_z[r].wait_recv()
+        s = p.at(-r % 4)[0]
+        h_y.append(sends.start(h_out.at[s], h_out.at[s], p.at(y=1)))
+    for copy in h_y:
+        copy.wait_recv()
+    sends.finish()
+    own.wait()
+
+
+def gather_seq(x, collective_id):
+    return call(
+        gather_seq_kernel,
+        "gather_seq",
+        collective_id,
+        jax.ShapeDtypeStruct((8,) + x.shape, x.dtype),
+        [ANY],
+        ANY,
+        [],
+        7,
+    )(x)
+
+
+def scatter_seq_kernel(p_ref, out_ref, acc, ry, rz, send_sem, recv_sem, own_sem):
+    p = Place()
+    barrier([p.at(1), p.at(2), p.at(3), p.at(y=1)])
+    sends = Sends(send_sem, recv_sem)
+    order = (2, 1, 3, 0)
+    loads, fy, fz = [], [], []
+    for n, r in enumerate(order):
+        fy.append(sends.start(p_ref.at[p.at(r, 1)[0]], ry.at[n], p.at(y=1)))
+        load = pltpu.make_async_copy(p_ref.at[p.at(r)[0]], acc.at[n], own_sem.at[n])
+        load.start()
+        loads.append(load)
+    rows = acc.shape[1]
+    for n, r in enumerate(order):
+        loads[n].wait()
+        fy[n].wait_recv()
+        add_rows(acc.at[n], ry.at[n], 0, rows)
+        if r:
+            fz.append(sends.start(acc.at[n], rz.at[n], p.at(r)))
+    for copy in fz:
+        copy.wait_recv()
+
+    def total(i, _):
+        at = pl.ds(pl.multiple_of(i * 16, 16), 16)
+        value = acc[3, at].astype(f32)
+        for n in range(3):
+            value = value + rz[n, at].astype(f32)
+        out_ref[at] = value.astype(out_ref.dtype)
+        return 0
+
+    lax.fori_loop(0, rows // 16, total, 0)
+    sends.finish()
+
+
+def scatter_seq(parts, collective_id, dtype=bf16):
+    block = parts.shape[1:]
+    return call(
+        scatter_seq_kernel,
+        "scatter_seq",
+        collective_id,
+        jax.ShapeDtypeStruct(block, dtype),
+        [ANY],
+        WHOLE,
+        [pltpu.VMEM((n,) + block, parts.dtype) for n in (4, 4, 3)],
+        7,
+        4,
+    )(parts)
+
+
+def sum_seq_kernel(x_ref, out_ref, got, send_sem, recv_sem, own_sem):
+    p = Place()
+    others = [p.at(r, y) for y in (0, 1) for r in range(4) if r or y]
+    barrier(others)
+    sends = Sends(send_sem, recv_sem)
+    me = p.at()[0]
+    got[me] = x_ref[...]
+    copies = [sends.start(x_ref, got.at[me], to) for to in others]
+    for copy in copies:
+        copy.wait_recv()
+    total = got[0]
+    for n in range(1, 8):
+        total = total + got[n]
+    out_ref[...] = total
+    sends.finish()
+
+
+def sum_seq(x, collective_id):
+    return call(
+        sum_seq_kernel,
+        "sum_seq",
+        collective_id,
+        jax.ShapeDtypeStruct(x.shape, x.dtype),
+        [WHOLE],
+        WHOLE,
+        [pltpu.VMEM((8,) + x.shape, x.dtype)],
+        7,
+    )(x)
+
+
+def scatter_probs_kernel(p_ref, out_ref, sum_x, sum_s, r1, r2, got, send_sem, recv_sem, own_sem):
+    p = Place()
+    others = [p.at(r, y) for y in (0, 1) for r in range(4) if r or y]
+    barrier(others + [p.at(x=1), p.at(c=1)])
+    sends = Sends(send_sem, recv_sem)
+    first = sends.start(p_ref.at[1 - p.c], r1, p.at(c=1))
+    first.wait_recv()
+    sum_x[...] = p_ref[p.c] + r1[...]
+    second = sends.start(sum_x.at[1 - p.x], r2, p.at(x=1))
+    second.wait_recv()
+    sum_s[...] = sum_x[p.x] + r2[...]
+    copies = []
+    for r, y in ((0, 1), (1, 0), (3, 0), (2, 0), (1, 1), (3, 1), (2, 1)):
+        to = lax.rem(p.z + r, 4)
+        yy = 1 - p.y if y else p.y
+        copies.append(sends.start(sum_s.at[yy, to], got.at[p.z, p.y], p.at(r, y)))
+    got[p.z, p.y] = sum_s[p.y, p.z]
+    for copy in copies:
+        copy.wait_recv()
+    out_ref[...] = got[...]
+    sends.finish()
+
+
+def scatter_probs(parts, collective_id):
+    experts, rows = parts.shape[-2:]
+    block = (experts, rows)
+    out = call(
+        scatter_probs_kernel,
+        "scatter_probs",
+        collective_id,
+        jax.ShapeDtypeStruct((4, 2) + block, f32),
+        [WHOLE],
+        WHOLE,
+        [
+            pltpu.VMEM((2, 2, 4) + block, f32),
+            pltpu.VMEM((2, 4) + block, f32),
+            pltpu.VMEM((2, 2, 4) + block, f32),
+            pltpu.VMEM((2, 4) + block, f32),
+            pltpu.VMEM((4, 2) + block, f32),
+        ],
+        9,
+    )(parts)
+    return out.reshape(8 * experts, rows)
+
+
+def add_blocks(dst, src):
+    def body(i, _):
+        dst[i] = (dst[i].astype(f32) + src[i].astype(f32)).astype(dst.dtype)
+        return 0
+
+    lax.fori_loop(0, dst.shape[0], body, 0)
+
+
+def scatter_last_kernel(
+    n_ref, wi_ref, wo_ref, sm_ref,
+    n_out, wi_out, wo_out, sm_out,
+    n_acc, n_y, n_z, wi_acc, wi_c, wi_x, wi_got, wo_acc, wo_c, wo_x, sm_acc, sm_c, sm_x, sm_y, sm_z,
+    send_sem, recv_sem, own_sem,
+):
+    p = Place()
+    c, x, y, z = p.c, p.x, p.y, p.z
+    others = [p.at(r, yy) for yy in (0, 1) for r in range(4) if r or yy]
+    barrier(others + [p.at(x=1), p.at(c=1)])
+    sends = Sends(send_sem, recv_sem)
+    core, nbr_x, nbr_y = p.at(c=1), p.at(x=1), p.at(y=1)
+    order = (2, 1, 3, 0)
+    loads = [
+        pltpu.make_async_copy(wi_ref.at[c], wi_acc, own_sem.at[4]),
+        pltpu.make_async_copy(wo_ref.at[c], wo_acc, own_sem.at[5]),
+        pltpu.make_async_copy(sm_ref.at[c], sm_acc, own_sem.at[6]),
+    ]
+    for load in loads:
+        load.start()
+    wi1 = sends.start(wi_ref.at[1 - c, 1 - x], wi_c.at[0], core)
+    sm1 = sends.start(sm_ref.at[1 - c], sm_c, core)
+    wo1 = sends.start(wo_ref.at[1 - c], wo_c, core)
+    wi2 = sends.start(wi_ref.at[1 - c, x], wi_c.at[1], core)
+    fy, n_loads, fz = [], [], []
+    for n, r in enumerate(order):
+        fy.append(sends.start(n_ref.at[p.at(r, 1)[0]], n_y.at[n], nbr_y))
+        load = pltpu.make_async_copy(n_ref.at[p.at(r)[0]], n_acc.at[n], own_sem.at[n])
+        load.start()
+        n_loads.append(load)
+    for load in loads:
+        load.wait()
+    wi1.wait_recv()
+    add_blocks(wi_acc.at[1 - x], wi_c.at[0])
+    wi3 = sends.start(wi_acc.at[1 - x], wi_x, nbr_x)
+    sm1.wait_recv()
+    sm_acc[...] = sm_acc[...] + sm_c[...]
+    sm2 = sends.start(sm_acc.at[1 - x], sm_x, nbr_x)
+    wo1.wait_recv()
+    add_blocks(wo_acc, wo_c)
+    wo2 = sends.start(wo_acc.at[1 - x], wo_x, nbr_x)
+    wi2.wait_recv()
+    add_blocks(wi_acc.at[x], wi_c.at[1])
+    rows = n_acc.shape[1]
+    for n, r in enumerate(order):
+        n_loads[n].wait()
+        fy[n].wait_recv()
+        add_rows(n_acc.at[n], n_y.at[n], 0, rows)
+        if r:
+            fz.append(sends.start(n_acc.at[n], n_z.at[n], p.at(r)))
+    wi3.wait_recv()
+    add_blocks(wi_acc.at[x], wi_x)
+    me = p.at()[0]
+    wi4 = []
+    for r, yy in ((0, 1), (1, 0), (3, 0), (2, 0), (1, 1), (3, 1), (2, 1)):
+        to = p.at(r, yy)
+        wi4.append(sends.start(wi_acc.at[x, to[0]], wi_got.at[me], to))
+    sm2.wait_recv()
+    sm_acc[x] = sm_acc[x] + sm_x[...]
+    sm3 = sends.start(sm_acc.at[x, 1 - y], sm_y, nbr_y)
+    wi_got[me] = wi_acc[x, me]
+    wo2.wait_recv()
+    wo_out[...] = wo_acc[x].astype(f32) + wo_x[...].astype(f32)
+    sm3.wait_recv()
+    sm_acc[x, y] = sm_acc[x, y] + sm_y[...]
+    sm4 = [
+        sends.start(sm_acc.at[x, y, lax.rem(z + r, 4)], sm_z.at[n], p.at(r)) for n, r in enumerate(Z_ORDER)
+    ]
+    for copy in wi4:
+        copy.wait_recv()
+    wi_out[...] = wi_got[...].astype(f32)
+    for copy in sm4:
+        copy.wait_recv()
+    sm_out[...] = sm_acc[x, y, z] + sm_z[0] + sm_z[1] + sm_z[2]
+    for copy in fz:
+        copy.wait_recv()
+
+    def total(i, _):
+        at = pl.ds(pl.multiple_of(i * 16, 16), 16)
+        value = n_acc[3, at].astype(f32)
+        for n in range(3):
+            value = value + n_z[n, at].astype(f32)
+        n_out[at] = value
+        return 0
+
+    lax.fori_loop(0, rows // 16, total, 0)
+    sends.finish()
+
+
+def scatter_last(normed, w_in, w_out, small, collective_id):
+    struct = jax.ShapeDtypeStruct
+    nb, ib, ob, sb = normed.shape[1:], w_in.shape[2:], w_out.shape[2:], small.shape[4:]
+    V = pltpu.VMEM
+    return call(
+        scatter_last_kernel,
+        "scatter_last",
+        collective_id,
+        (struct(nb, f32), struct(ib, f32), struct(ob, f32), struct(sb, f32)),
+        [ANY] * 4,
+        (WHOLE,) * 4,
+        [
+            V((4,) + nb, bf16), V((4,) + nb, bf16), V((3,) + nb, bf16),
+            V((2,) + ib, bf16), V((2,) + ib, bf16), V(ib, bf16), V(ib, bf16),
+            V((2,) + ob, bf16), V((2,) + ob, bf16), V(ob, bf16),
+            V((2, 2, 4) + sb, f32), V((2, 2, 4) + sb, f32), V((2, 4) + sb, f32), V((4,) + sb, f32), V((3,) + sb, f32),
+        ],
+        4 + 4 + 3 + 1 + 1 + 1 + 7 + 1 + 3,
+        7,
+        48,
+    )(normed, w_in, w_out, small)
+
+
+def slots_of_rows(ranks):
+    experts, rows = ranks.shape
+    slot = lax.broadcasted_iota(jnp.int32, (experts, CAP, rows), 1)
+    return ranks[:, None, :] == slot
+
+
+def one_hot(hot):
+    experts, _, rows = hot.shape
+    return jnp.where(hot, 1.0, 0.0).reshape(experts * CAP, rows).astype(bf16)
+
+
+def dispatch_kernel(first_ref, routes_ref, x_ref, g_ref, router_ref, xs_ref, gs_ref, gate_ref, rank_ref, probs):
+    experts = rank_ref.shape[1]
+    rows = x_ref.shape[1]
+    first = pl.multiple_of(first_ref[0], experts)
+    routes = routes_ref[0]
+    hits = []
+    for e in range(experts):
+        same = jnp.where(routes == first + e, 1.0, 0.0)
+        hits.append(jnp.max(same, axis=0, keepdims=True))
+    hit = jnp.concatenate(hits, axis=0)
+    before = lax.broadcasted_iota(jnp.int32, (rows, rows), 0) < lax.broadcasted_iota(jnp.int32, (rows, rows), 1)
+    rank = jnp.dot(hit.astype(bf16), jnp.where(before, 1.0, 0.0).astype(bf16), preferred_element_type=f32)
+    rank = jnp.where(hit > 0.5, rank.astype(jnp.int32), -1)
+    rank_ref[0] = rank
+    hot = slots_of_rows(rank)
+    place = one_hot(hot)
+    x = x_ref[0]
+    logits = dot(router_ref[...], x, ((1,), (1,)))
+    weights = jnp.exp(logits - jnp.max(logits, axis=0, keepdims=True))
+    probs[...] = weights / jnp.sum(weights, axis=0, keepdims=True)
+    mine = probs[pl.ds(first, experts)]
+    gate = jnp.sum(jnp.where(hot, mine[:, None, :], 0.0), axis=-1, keepdims=True)
+    gate_ref[...] = jnp.broadcast_to(gate, gate_ref.shape)
+    xs_ref[...] = jnp.dot(place, x, preferred_element_type=f32).astype(bf16).reshape(xs_ref.shape)
+    gs_ref[...] = jnp.dot(place, g_ref[0], preferred_element_type=f32).astype(bf16).reshape(gs_ref.shape)
+
+
+def dispatch(first, routes_all, x_all, g_all, router_rows, experts):
+    groups, rows, width = x_all.shape
+    slots = groups * CAP
+    return pl.pallas_call(
+        dispatch_kernel,
+        name="dispatch",
+        grid=(groups,),
+        out_shape=(
+            jax.ShapeDtypeStruct((experts, slots, width), bf16),
+            jax.ShapeDtypeStruct((experts, slots, width), bf16),
+            jax.ShapeDtypeStruct((experts, slots, 128), f32),
+            jax.ShapeDtypeStruct((groups, experts, rows), jnp.int32),
+        ),
+        in_specs=[
+            pl.BlockSpec(memory_space=pltpu.SMEM),
+            pl.BlockSpec((1,) + routes_all.shape[1:], lambda d: (d, 0, 0)),
+            pl.BlockSpec((1, rows, width), lambda d: (d, 0, 0)),
+            pl.BlockSpec((1, rows, width), lambda d: (d, 0, 0)),
+            pl.BlockSpec(router_rows.shape, lambda d: (0, 0)),
+        ],
+        out_specs=(
+            pl.BlockSpec((experts, CAP, width), lambda d: (0, d, 0)),
+            pl.BlockSpec((experts, CAP, width), lambda d: (0, d, 0)),
+            pl.BlockSpec((experts, CAP, 128), lambda d: (0, d, 0)),
+            pl.BlockSpec((1, experts, rows), lambda d: (d, 0, 0)),
+        ),
+        scratch_shapes=[pltpu.VMEM((router_rows.shape[0], rows), f32)],
+        compiler_params=pltpu.CompilerParams(vmem_limit_bytes=40 << 20),
+    )(first, routes_all, x_all, g_all, router_rows)
+
+
+def experts_kernel(w_ref, xs_ref, gs_ref, gate_ref, y_ref, z_ref, wg_ref, gg_ref):
+    x, g = xs_ref[0], gs_ref[0]
+    gain = gate_ref[0][:, :1]
+    gate = jnp.dot(x, w_ref[0, 0], preferred_element_type=f32)
+    up = jnp.dot(x, w_ref[0, 1], preferred_element_type=f32)
+    raw = jnp.dot(g, w_ref[0, 2], preferred_element_type=f32)
+    sigma = 1.0 / (1.0 + jnp.exp(-gate))
+    silu = gate * sigma
+    act = (silu * up).astype(bf16).astype(f32)
+    gg_ref[0] = jnp.broadcast_to(jnp.sum(raw * act, axis=-1, keepdims=True), gg_ref.shape[1:])
+    act_gated = (act * gain).astype(bf16)
+    act_grad = raw * gain
+    gate_low = (act_grad * up * sigma * (1.0 + gate * (1.0 - sigma))).astype(bf16)
+    up_low = (act_grad * silu).astype(bf16)
+    y_ref[0] = dot(act_gated, w_ref[0, 2], ((1,), (1,))).astype(bf16)
+    z = dot(gate_low, w_ref[0, 0], ((1,), (1,))) + dot(up_low, w_ref[0, 1], ((1,), (1,)))
+    z_ref[0] = z.astype(bf16)
+    first = pl.program_id(1) == 0
+    for n, (left, right) in enumerate(((x, gate_low), (x, up_low), (g, act_gated))):
+        term = dot(left, right, ((0,), (0,)))
+
+        @pl.when(first)
+        def _():
+            wg_ref[0, n] = term
+
+        @pl.when(jnp.logical_not(first))
+        def _():
+            wg_ref[0, n] += term
+
+
+def experts_all(w_expert, xs, gs, gates, tile=512):
+    experts, slots, width = xs.shape
+    hidden = w_expert.shape[-1]
+    row = pl.BlockSpec((1, tile, width), lambda e, t: (e, t, 0))
+    thin = pl.BlockSpec((1, tile, 128), lambda e, t: (e, t, 0))
+    weight = pl.BlockSpec((1, 3, width, hidden), lambda e, t: (e, 0, 0, 0))
+    return pl.pallas_call(
+        experts_kernel,
+        name="experts",
+        grid=(experts, slots // tile),
+        out_shape=(
+            jax.ShapeDtypeStruct(xs.shape, bf16),
+            jax.ShapeDtypeStruct(xs.shape, bf16),
+            jax.ShapeDtypeStruct(w_expert.shape, f32),
+            jax.ShapeDtypeStruct((experts, slots, 128), f32),
+        ),
+        in_specs=[weight, row, row, thin],
+        out_specs=(row, row, weight, thin),
+        compiler_params=pltpu.CompilerParams(vmem_limit_bytes=60 << 20),
+    )(w_expert, xs, gs, gates)
+
+
+def combine_kernel(rank_ref, y_ref, z_ref, gg_ref, my_ref, mz_ref, pg_ref):
+    hot = slots_of_rows(rank_ref[0])
+    place = one_hot(hot)
+    flat = (place.shape[0], y_ref.shape[-1])
+    my_ref[0] = dot(place, y_ref[...].reshape(flat), ((0,), (0,))).astype(bf16)
+    mz_ref[0] = dot(place, z_ref[...].reshape(flat), ((0,), (0,))).astype(bf16)
+    pg_ref[0] = jnp.sum(jnp.where(hot, gg_ref[:, :, :1], 0.0), axis=1)
+
+
+def combine(ranks, y, z, gate_grads):
+    groups, experts, rows = ranks.shape
+    width = y.shape[-1]
+    part = pl.BlockSpec((experts, CAP, width), lambda d: (0, d, 0))
+    whole = pl.BlockSpec((1, rows, width), lambda d: (d, 0, 0))
+    thin = pl.BlockSpec((1, experts, rows), lambda d: (d, 0, 0))
+    return pl.pallas_call(
+        combine_kernel,
+        name="combine",
+        grid=(groups,),
+        out_shape=(
+            jax.ShapeDtypeStruct((groups, rows, width), bf16),
+            jax.ShapeDtypeStruct((groups, rows, width), bf16),
+            jax.ShapeDtypeStruct((groups, experts, rows), f32),
+        ),
+        in_specs=[thin, part, part, pl.BlockSpec((experts, CAP, 128), lambda d: (0, d, 0))],
+        out_specs=(whole, whole, thin),
+        compiler_params=pltpu.CompilerParams(vmem_limit_bytes=40 << 20),
+    )(ranks, y, z, gate_grads)
+
+
 class HeadsAttention:
-    def __init__(self, hidden, segment_all, w_in, w_out, gains_all):
-        seq = lax.axis_size("seq")
-        batch = lax.axis_size("batch")
-        place = lax.axis_index("seq")
-        self.rows = hidden.shape[0]
-        width = hidden.shape[1]
-        self.width = width
+    def __init__(self, hidden, segments, routes, w_in, w_out, w_router, gains, experts):
+        seq, batch = 8, 4
+        place, b = lax.axis_index("seq"), lax.axis_index("batch")
+        self.rows, self.width = hidden.shape
+        width = self.width
         self.hs = width // HEADS
         self.hl = HEADS // seq
         cols = self.hl * self.hs
         self.cols = cols
-        own = w_in.shape[0]
-        hidden_all = lax.all_gather(hidden, "seq", axis=0, tiled=True)
-        length = hidden_all.shape[0]
+        top = routes.shape[1]
+        total = experts * seq
+        ints = jnp.concatenate([routes.T, segments[None], jnp.zeros((7, self.rows), jnp.int32)], axis=0)
+        small = jnp.concatenate(
+            [w_router, gains.T, jnp.zeros((w_router.shape[0], 128 - total - gains.shape[0]), bf16)], axis=1
+        )
+        hidden_all, w_cols, w_rows, ints, small = gather_first(hidden, w_in, w_out, ints, small, 0)
+        length = seq * self.rows
         self.length = length
-        parts = w_in.reshape(own, 3, seq, cols)
-        parts = lax.all_to_all(parts, "seq", split_axis=2, concat_axis=2, tiled=True)
-        parts = jnp.transpose(parts, (2, 0, 1, 3)).reshape(seq, own, 3 * cols)
-        self.w_cols = lax.all_gather(parts, "batch", axis=1, tiled=True).reshape(width, 3 * cols)
-        self.w_rows = lax.all_gather(w_out, "batch", axis=0, tiled=True)
-        inputs = hidden_all.astype(f32)
-        normed = (inputs * rms_scale(inputs) * gains_all[0]).astype(bf16)
+        self.w_cols = w_cols.reshape(width, 3 * cols)
+        self.w_rows = w_rows.reshape(cols, width)
+        small = small.reshape(width, 128)
+        self.router_all = small[:, :total]
+        self.gains_all = small[:, total : total + 4].T.astype(f32)
+        self.routes_all = ints[:, :top]
+        segment_all = lax.dynamic_slice_in_dim(ints.reshape(seq, batch, -1, self.rows), b, 1, 1)
+        segment_all = segment_all[:, 0, top].reshape(length)
+        gains_all = self.gains_all
+        inputs = hidden_all.reshape(length, width).astype(f32)
+        self.first_normal = inputs * rms_scale(inputs)
+        normed = (self.first_normal * gains_all[0]).astype(bf16)
         self.normed = normed
         projected = jnp.dot(normed, self.w_cols, preferred_element_type=f32)
         query_raw = projected[:, :cols]
         key_raw = projected[:, cols : 2 * cols]
         squares = jnp.stack([jnp.sum(query_raw * query_raw, -1), jnp.sum(key_raw * key_raw, -1)], 0)
-        scales = lax.rsqrt(lax.psum(squares, "seq") / width + epsilon)
+        scales = lax.rsqrt(self.over_heads(squares, 1) / width + epsilon)
         self.query_scale = scales[0][:, None]
         self.key_scale = scales[1][:, None]
         self.query_normal = query_raw * self.query_scale
@@ -95,22 +865,23 @@
         self.attended = jnp.transpose(acc / total, (1, 0, 2))
         self.attn_low = self.attended.reshape(length, cols).astype(bf16)
         partial = jnp.dot(self.attn_low, self.w_rows, preferred_element_type=f32).astype(bf16)
-        self.mixed = lax.psum_scatter(partial, "seq", scatter_dimension=0, tiled=True).astype(f32)
+        self.mixed = scatter_seq(partial.reshape(seq, self.rows, width), 2, f32)
+
+    def over_heads(self, sums, collective_id):
+        return sum_seq(sums.reshape(2, -1, 128), collective_id).reshape(2, self.length)
 
     def scores(self):
         scale = self.hs ** (-0.5)
         scores = jnp.einsum("qhd,khd->hqk", self.query, self.key, preferred_element_type=f32) * scale
         return jnp.where(self.allowed[None], scores, -jnp.inf)
 
-    def back(self, middle_low):
-        seq = lax.axis_size("seq")
-        batch = lax.axis_size("batch")
+    def back(self, middle_low, router_grad, ffn_gain_grad):
+        seq, batch = 8, 4
         length, cols, width = self.length, self.cols, self.width
         scale = self.hs ** (-0.5)
         shape = (length, self.hl, self.hs)
-        grad_all = lax.all_gather(middle_low, "seq", axis=0, tiled=True)
+        grad_all = gather_seq(middle_low, 3).reshape(length, width)
         out_grad = dot(self.attn_low, grad_all, ((0,), (0,))).astype(bf16)
-        out_shard = lax.psum_scatter(out_grad, "batch", scatter_dimension=0, tiled=True).astype(f32)
         attn_grad = dot(grad_all, self.w_rows, ((1,), (1,))).astype(bf16).reshape(shape)
         delta = jnp.sum(attn_grad.astype(f32) * self.attended, axis=-1)
         probs = jnp.exp(self.scores() - self.log_total)
@@ -129,28 +900,57 @@
         key_gain_grad = jnp.sum(key_norm_grad * self.key_normal, axis=0)
         query_scaled = query_norm_grad * self.query_gain
         key_scaled = key_norm_grad * self.key_gain
-        means = lax.psum(
-            jnp.stack([jnp.sum(query_scaled * self.query_normal, -1), jnp.sum(key_scaled * self.key_normal, -1)], 0),
-            "seq",
-        ) / width
+        dots = jnp.stack(
+            [jnp.sum(query_scaled * self.query_normal, -1), jnp.sum(key_scaled * self.key_normal, -1)], 0
+        )
+        means = self.over_heads(dots, 4) / width
         query_raw_grad = self.query_scale * (query_scaled - self.query_normal * means[0][:, None])
         key_raw_grad = self.key_scale * (key_scaled - self.key_normal * means[1][:, None])
         projected_grad = jnp.concatenate(
             [query_raw_grad, key_raw_grad, value_grad.reshape(length, cols)], axis=1
         ).astype(bf16)
-        partial = dot(projected_grad, self.w_cols, ((1,), (1,))).astype(bf16)
-        normed_grad = lax.psum_scatter(partial, "seq", scatter_dimension=0, tiled=True).astype(f32)
+        partial = dot(projected_grad, self.w_cols, ((1,), (1,)))
+        attn_gain_grad = jnp.sum(partial * self.first_normal, axis=0)
         in_grad = dot(self.normed, projected_grad, ((0,), (0,))).astype(bf16)
         own = width // (seq * batch)
-        in_grad = lax.psum_scatter(
-            in_grad.reshape(seq, batch * own, 3 * cols), "batch", scatter_dimension=1, tiled=True
-        )
-        in_grad = lax.all_to_all(in_grad, "seq", split_axis=0, concat_axis=0, tiled=True)
-        in_shard = jnp.transpose(in_grad.reshape(seq, own, 3, cols), (1, 2, 0, 3)).reshape(own, 3 * width)
-        pair = lax.psum_scatter(
-            jnp.stack([query_gain_grad, key_gain_grad], 1), "batch", scatter_dimension=0, tiled=True
-        )
-        return normed_grad, in_shard.astype(f32), out_shard, pair
+
+        def by_batch(value, *shape):
+            return jnp.swapaxes(value.reshape(2, 2, *shape), 0, 1)
+
+        in_grad = jnp.transpose(in_grad.reshape(seq, 2, 2, own, 3 * cols), (2, 1, 0, 3, 4))
+        out_grad = by_batch(out_grad, own, width)
+        mine = jnp.arange(seq)[:, None] == lax.axis_index("seq")
+
+        def own_columns(value):
+            return jnp.where(mine, value[None], 0.0).reshape(width)
+
+        gains_grad = jnp.stack(
+            [attn_gain_grad, own_columns(query_gain_grad), own_columns(key_gain_grad), ffn_gain_grad], axis=1
+        )
+        total = router_grad.shape[1]
+        small = jnp.concatenate([router_grad, gains_grad, jnp.zeros((width, 128 - total - 4), f32)], axis=1)
+        small = jnp.transpose(small.reshape(4, 2, 2, 2, own, 128), (3, 2, 1, 0, 4, 5))
+        normed_grad, in_shard, out_shard, small = scatter_last(
+            partial.astype(bf16).reshape(seq, self.rows, width), in_grad, out_grad, small, 5
+        )
+        in_shard = jnp.transpose(in_shard.reshape(seq, own, 3, cols), (1, 2, 0, 3)).reshape(own, 3 * width)
+        return normed_grad, in_shard, out_shard, small[:, :total], small[:, total : total + 4].T
+
+
+def experts_by_tokens(ffn_in, cotangent_all, routes_all, w_expert, router_all):
+    experts = w_expert.shape[0]
+    rows, width = ffn_in.shape
+    first = (lax.axis_index("seq") * experts).astype(jnp.int32).reshape(1)
+    ffn_all = gather_all(ffn_in, 6)
+    xs, gs, gates, ranks = dispatch(
+        first, routes_all, ffn_all, cotangent_all.reshape(32, rows, width), router_all.T, experts
+    )
+    y, z, expert_grad, gate_grads = experts_all(w_expert, xs, gs, gates)
+    mixture, ffn_in_grad, probs = combine(ranks, y, z, gate_grads)
+    prob_grad = scatter_probs(jnp.transpose(probs.reshape(4, 2, 2, 2, experts, rows), (3, 2, 1, 0, 4, 5)), 7).T
+    ffn_in_grad = scatter_all(ffn_in_grad, 8, f32)
+    mixture = scatter_all(mixture, 9, f32)
+    return mixture, ffn_in_grad, prob_grad, expert_grad
 
 
 class TokensAttention:
@@ -219,7 +1019,7 @@
         )
         return jnp.where(allowed[None], scores, -jnp.inf)
 
-    def back(self, middle_low):
+    def back(self, middle_low, router_grad, ffn_gain_grad):
         again = lax.optimization_barrier((middle_low, *self.sources, *self.kept))
         middle_low = again[0]
         self.gather_weights(*again[1:3])
@@ -279,7 +1079,7 @@
         pair = lax.psum_scatter(
             jnp.stack([query_gain_grad, key_gain_grad], 1), BOTH, scatter_dimension=0, tiled=True
         )
-        return normed_grad, in_shard, out_shard, pair
+        return normed_grad, in_shard, out_shard, router_grad, pair
 
 
 def expert_math(slots, grads, gate_slot, w_expert):
@@ -317,54 +1117,6 @@
     return rank[:, :, :, None] == jnp.arange(CAP, dtype=jnp.int32)
 
 
-def experts_by_tokens(ffn_in, cotangent, routes, w_expert, router_all):
-    seq, batch = lax.axis_size("seq"), lax.axis_size("batch")
-    place = lax.axis_index("seq")
-    everyone = seq * batch
-    experts = w_expert.shape[0]
-    rows, width = ffn_in.shape
-    routes_all = lax.all_gather(routes, BOTH, axis=0, tiled=True)
-    cotangent_all = lax.all_gather(cotangent, BOTH, axis=0, tiled=True)
-    ffn_all = lax.all_gather(ffn_in, BOTH, axis=0, tiled=True)
-    mine = place * experts + jnp.arange(experts, dtype=jnp.int32)
-    hit = jnp.any(routes_all[:, :, None] == mine[None, None, :], axis=1).reshape(everyone, rows, experts)
-    hot = slot_places(hit)
-    place_hot = jnp.transpose(hot, (0, 2, 3, 1)).astype(bf16).reshape(everyone, experts * CAP, rows)
-    router_every = jax.nn.softmax(jnp.dot(ffn_all, router_all, preferred_element_type=f32), axis=-1)
-    router_mine = lax.dynamic_slice_in_dim(router_every, place * experts, experts, 1)
-    gate_slot = jnp.sum(jnp.where(hot, router_mine.reshape(everyone, rows, experts, 1), 0.0), axis=1)
-    gate_slot = jnp.transpose(gate_slot, (1, 0, 2)).reshape(experts, everyone * CAP, 1)
-
-    def dispatch(tokens):
-        slots = jnp.einsum(
-            "dst,dth->dsh", place_hot, tokens.reshape(everyone, rows, width), preferred_element_type=f32
-        ).astype(bf16)
-        slots = jnp.transpose(slots.reshape(everyone, experts, CAP, width), (1, 0, 2, 3))
-        return slots.reshape(experts, everyone * CAP, width)
-
-    def combine(values):
-        values = jnp.transpose(values.reshape(experts, everyone, CAP, width), (1, 0, 2, 3))
-        values = values.reshape(everyone, experts * CAP, width)
-        return (
-            jnp.einsum("dst,dsh->dth", place_hot, values, preferred_element_type=f32)
-            .astype(bf16)
-            .reshape(everyone * rows, width)
-        )
-
-    result, slot_grad, gate_grad, expert_grad = expert_math(
-        dispatch(ffn_all), dispatch(cotangent_all), gate_slot, w_expert
-    )
-    gate_grad = jnp.transpose(gate_grad.reshape(experts, everyone, CAP), (1, 0, 2))
-    gate_part = jnp.sum(jnp.where(hot, gate_grad[:, None], 0.0), axis=-1)
-    gate_part = gate_part.reshape(seq, batch * rows, experts)
-    gate_part = lax.psum_scatter(gate_part, "batch", scatter_dimension=1, tiled=True)
-    gate_part = lax.all_to_all(gate_part, "seq", split_axis=0, concat_axis=0, tiled=True)
-    prob_grad = jnp.transpose(gate_part, (1, 0, 2)).reshape(rows, seq * experts)
-    ffn_in_grad = lax.psum_scatter(combine(slot_grad), BOTH, scatter_dimension=0, tiled=True).astype(f32)
-    mixture = lax.psum_scatter(combine(result), BOTH, scatter_dimension=0, tiled=True).astype(f32)
-    return mixture, ffn_in_grad, prob_grad, expert_grad
-
-
 def experts_by_slots(ffn_in, cotangent, routes, w_expert, router_all):
     seq, batch = lax.axis_size("seq"), lax.axis_size("batch")
     experts = w_expert.shape[0]
@@ -407,28 +1159,36 @@
 def local(hidden, segments, routes, w_in, w_out, w_router, gains, w_expert, cotangent):
     seq = lax.axis_size("seq")
     total_experts = w_expert.shape[0] * seq
-
-    small = lax.all_gather(jnp.concatenate([w_router, gains.T], axis=1), BOTH, axis=0, tiled=True)
-    router_all = small[:, :total_experts]
-    gains_all = small[:, total_experts:].T.astype(f32)
-    segment_all = lax.all_gather(segments[0], "seq", axis=0, tiled=True)
+    by_heads = seq == 8 and lax.axis_size("batch") == 4
 
     inputs = hidden[0].astype(f32)
     first_scale = rms_scale(inputs)
     first_normal = inputs * first_scale
-
-    by_heads = HEADS % seq == 0
-    attend = HeadsAttention if by_heads else TokensAttention
-    mix = experts_by_tokens if by_heads else experts_by_slots
-    attention = attend(hidden[0], segment_all, w_in, w_out, gains_all)
+    if by_heads:
+        cotangent_all = lax.all_gather(cotangent[0], BOTH, axis=0, tiled=True)
+        attention = HeadsAttention(
+            hidden[0], segments[0], routes[0], w_in, w_out, w_router, gains, w_expert.shape[0]
+        )
+        gains_all, router_all = attention.gains_all, attention.router_all
+    else:
+        small = lax.all_gather(jnp.concatenate([w_router, gains.T], axis=1), BOTH, axis=0, tiled=True)
+        router_all = small[:, :total_experts]
+        gains_all = small[:, total_experts:].T.astype(f32)
+        segment_all = lax.all_gather(segments[0], "seq", axis=0, tiled=True)
+        attention = TokensAttention(hidden[0], segment_all, w_in, w_out, gains_all)
 
     middle = inputs + attention.mixed
     second_scale = rms_scale(middle)
     second_normal = middle * second_scale
     ffn_in = (second_normal * gains_all[3]).astype(bf16)
-    mixture, ffn_in_grad, prob_grad, expert_grad = mix(
-        ffn_in, cotangent[0], routes[0], w_expert, router_all
-    )
+    if by_heads:
+        mixture, ffn_in_grad, prob_grad, expert_grad = experts_by_tokens(
+            ffn_in, cotangent_all, attention.routes_all, w_expert, router_all
+        )
+    else:
+        mixture, ffn_in_grad, prob_grad, expert_grad = experts_by_slots(
+            ffn_in, cotangent[0], routes[0], w_expert, router_all
+        )
     output = middle + mixture
 
     grad_out = cotangent[0].astype(f32)
@@ -439,14 +1199,18 @@
     ffn_in_grad = ffn_in_grad + dot(logit_low, router_all, ((1,), (1,)))
     ffn_gain_grad = jnp.sum(ffn_in_grad * second_normal, axis=0)
     middle_grad = grad_out + norm_back(ffn_in_grad, second_normal, second_scale, gains_all[3])
-    normed_grad, in_shard, out_shard, pair_shard = attention.back(middle_grad.astype(bf16))
-    attn_gain_grad = jnp.sum(normed_grad * first_normal, axis=0)
+    normed_grad, in_shard, out_shard, router_shard, gains_shard = attention.back(
+        middle_grad.astype(bf16), router_grad, ffn_gain_grad
+    )
+    if not by_heads:
+        attn_gain_grad = jnp.sum(normed_grad * first_normal, axis=0)
+        ends = jnp.stack([attn_gain_grad, ffn_gain_grad], axis=1)
+        sums = lax.psum_scatter(
+            jnp.concatenate([router_shard, ends], axis=1), BOTH, scatter_dimension=0, tiled=True
+        )
+        router_shard, ends = sums[:, :total_experts], sums[:, total_experts:]
+        gains_shard = jnp.stack([ends[:, 0], gains_shard[:, 0], gains_shard[:, 1], ends[:, 1]], axis=0)
     input_grad = middle_grad + norm_back(normed_grad, first_normal, first_scale, gains_all[0])
-    sums = jnp.concatenate([router_grad, attn_gain_grad[:, None], ffn_gain_grad[:, None]], axis=1)
-    sums = lax.psum_scatter(sums, BOTH, scatter_dimension=0, tiled=True)
-    router_shard = sums[:, :total_experts]
-    ends = sums[:, total_experts:]
-    gains_shard = jnp.stack([ends[:, 0], pair_shard[:, 0], pair_shard[:, 1], ends[:, 1]], axis=0)
     return (
         output.astype(bf16)[None],
         input_grad[None],

time: 1510 us -> 955 us (0.63)
  Pallas kernels: 0 us -> 838 us
  waiting for transfers between devices: 699 us -> 0.68 us
  matrix products: 366 us -> 33 us
  blocking collectives: 183 us -> 0 us
  local copies, waits for them, and re-layouts: 150 us -> 36.6 us
  other arithmetic: 82 us -> 21.5 us
    pallas_call x0 -> x13, Pallas kernels: none -> 838 us  [the longest x2 186 us: scatter_all(): pl.pallas_call(scatter_all_kernel, name='scatter_all', out_shape=jax.Shap...]
    reduce_scatter x7 -> x0, waiting for transfers between devices: 452 us -> none  [the longest x1 169 us: experts_by_tokens(): lax.psum_scatter(combine(slot_grad), BOTH, scatter_dimension=0, tiled=True)]
    dot_general x14 -> x0, matrix products: 309 us -> none  [the longest x2 47.2 us: dispatch(): jnp.einsum('dst,dth->dsh', place_hot, tokens.reshape(everyone, rows, widt...]
    unnamed x17 -> x1, waiting for transfers between devices: 138 us -> 0.68 us
    all_gather x6 -> x1, waiting for transfers between devices: 102 us -> 0.01 us  [local(): cotangent_all = lax.all_gather(cotangent[0], BOTH, axis=0, tiled=True)]
    all_gather x3 -> x0, blocking collectives: 99.5 us -> none  [the longest x1 40.8 us: experts_by_tokens(): routes_all = lax.all_gather(routes, BOTH, axis=0, tiled=True)]
    transpose x5 -> x2, local copies, waits for them, and re-layouts: 47.5 us -> 2.67 us  [the longest x1 2.59 us: back(): jnp.transpose(in_shard.reshape(seq, own, 3, cols), (1, 2, 0, 3))]
    all_to_all x1 -> x0, blocking collectives: 42.6 us -> none  [__init__(): lax.all_to_all(parts, 'seq', split_axis=2, concat_axis=2, tiled=True)]
  transfers between devices with their start and end apart: 17 -> 1, of which waited for: 8 -> 0; matrix products, arithmetic and copies ran while one was open for 28% -> 3% of each run, Pallas kernels for 0% -> 30%
where the time goes in v2:
time: 955 us; the launch traced here: 946 us
  Pallas kernels  838 us (88%)
  local copies, waits for them, and re-layouts  36.6 us (4%)
  matrix products  33 us (3%)
  other arithmetic  21.5 us (2%)
  between operations  15.5 us (2%)
    pallas_call x2, Pallas kernels, scatter_all(): pl.pallas_call(scatter_all_kernel, name='scatter_all', out_shape=jax.Shap...  186 us
    pallas_call x1, Pallas kernels, gather_first(): call(gather_first_kernel, 'gather_first', collective_id, (struct((8,) + h...  132 us
    pallas_call x1, Pallas kernels, experts_all(): pl.pallas_call(experts_kernel, name='experts', grid=(experts, slots // ti...  122 us
    pallas_call x1, Pallas kernels, gather_all(): pl.pallas_call(gather_all_kernel, name='gather_all', out_shape=jax.ShapeD...  88 us
    pallas_call x1, Pallas kernels, scatter_last(): call(scatter_last_kernel, 'scatter_last', collective_id, (struct(nb, f32)...  78.2 us
    pallas_call x1, Pallas kernels, gather_seq(): call(gather_seq_kernel, 'gather_seq', collective_id, jax.ShapeDtypeStruct...  60.1 us
    pallas_call x1, Pallas kernels, dispatch(): pl.pallas_call(dispatch_kernel, name='dispatch', grid=(groups,), out_shap...  49.5 us
    pallas_call x1, Pallas kernels, scatter_seq(): call(scatter_seq_kernel, 'scatter_seq', collective_id, jax.ShapeDtypeStru...  47.3 us
  transfers between devices with their start and end apart: 1, of which 0 were waited for; matrix products, arithmetic and copies ran while one was open for 3% of the time, Pallas kernels for 30%

profile of v2, /device:TPU:0, one launch (start us, length us, event | category | flops | bytes accessed | tf_op | source)
XLA Modules:
  0.0 945.6 jit_solution(13010814988893759443)
XLA Ops:
  7.3 0.7 all-gather.3.cloned.1.call-update
  8.0 1.3 copy.83
  9.7 0.9 reshape.355.wi_ref
  11.1 132.0 %gather_first.1 = (bf16[8,128,2048]{2,1,0:T(8,128)(2,1)S(1)}, bf16[8,4,64,768]{3,2,1,0:T(8,128)(2,1)S(1)}, bf16[4,64,2048]{2,1,0:T(8,128)(2,1)S(1)}, s32[32,16,128]{2,1,0:T(8,128)S(1)}, bf16[32,64,128]{2,1,0:T(8,128)(2,1)S(1)}) custom-call(bf16[128,2048]{1,0:T(8,128)(2,1)S(1)} %bitcast.159, bf16[8,64,768]{2,1,0:T(8,128)(2,1)S(1)} %reshape.355.wi_ref, ...), custom_call_target="tpu_custom_call" | custom-call | tf_op jit(solution)/shard_map/gather_first/pallas_call | solution.py:356
  143.1 1.4 slice_convert_fusion.1
  144.5 0.9 slice_reduce_fusion
  145.4 0.9 multiply_reduce_fusion.1
  146.3 0.6 fusion.52
  146.9 1.0 multiply_convert_fusion.2
  147.9 3.6 fusion.59
  151.9 13.5 %sum_seq.2 = f32[2,8,128]{2,1,0:T(8,128)S(1)} custom-call(f32[2,8,128]{2,1,0:T(8,128)S(1)} %pad_maximum_fusion.4.x_ref), custom_call_target="tpu_custom_call" | custom-call | tf_op jit(solution)/shard_map/sum_seq/pallas_call | solution.py:474
  165.4 1.1 dynamic-slice_bitcast_fusion
  166.9 3.1 broadcast_multiply_fusion.3
  170.6 0.6 fusion.28
  171.3 0.6 fusion.8
  171.9 1.9 fusion.3
  173.9 2.0 fusion
  175.9 1.2 copy-done.17
  177.1 3.6 fusion.57
  180.7 1.3 convolution_convert_fusion
  182.0 47.3 %scatter_seq.1 = f32[128,2048]{1,0:T(8,128)S(1)} custom-call(bf16[8,128,2048]{2,1,0:T(8,128)(2,1)S(1)} %bitcast.158), custom_call_target="tpu_custom_call" | custom-call | tf_op jit(solution)/shard_map/scatter_seq/pallas_call | solution.py:443
  229.7 1.0 copy-done.11
  230.6 0.9 multiply_convert_fusion.5.x_ref
  231.6 88.0 %gather_all.1.x_ref = bf16[32,128,2048]{2,1,0:T(8,128)(2,1)} custom-call(bf16[128,2048]{1,0:T(8,128)(2,1)} %multiply_convert_fusion.5.x_ref), custom_call_target="tpu_custom_call" | custom-call | tf_op jit(solution)/shard_map/gather_all/pallas_call | solution.py:145
  319.8 0.5 add_compare_fusion
  320.7 0.6 add_rsqrt_fusion.2
  321.3 0.6 log_add_fusion
  321.9 49.5 %dispatch.1 = (bf16[8,1024,2048]{2,1,0:T(8,128)(2,1)}, bf16[8,1024,2048]{2,1,0:T(8,128)(2,1)}, f32[8,1024,128]{2,1,0:T(8,128)S(1)}, s32[32,8,128]{2,1,0:T(8,128)S(1)}) custom-call(s32[1]{0:T(128)} %bitcast.24.first_ref, s32[32,8,128]{2,1,0:T(8,128)S(1)} %slice.96.routes_ref, bf16[32,128,2048]{2,1,0:T(8,128)(2,1)} %gather_all.1.x_ref, ...), custom_call_target="tpu_custom_call" | custom-call | tf_op jit(solution)/shard_map/dispatch/pallas_call | solution.py:692
  371.5 1.9 copy-done.3
  373.4 122.2 %experts.1 = (bf16[8,1024,2048]{2,1,0:T(8,128)(2,1)}, bf16[8,1024,2048]{2,1,0:T(8,128)(2,1)}, f32[8,3,2048,256]{3,2,1,0:T(8,128)}, f32[8,1024,128]{2,1,0:T(8,128)}) custom-call(bf16[8,3,2048,256]{3,2,1,0:T(8,128)(2,1)} %w_ref.1, bf16[8,1024,2048]{2,1,0:T(8,128)(2,1)} %get-tuple-element.33.xs_ref, bf16[8,1024,2048]{2,1,0:T(8,128)(2,1)} %get-tuple-element.34.gs_ref, ...), custom_call_target="tpu_custom_call" | custom-call | tf_op jit(solution)/shard_map/experts/pallas_call | solution.py:756
  495.6 2.2 copy-done.4
  497.8 44.0 %combine.1 = (bf16[32,128,2048]{2,1,0:T(8,128)(2,1)}, bf16[32,128,2048]{2,1,0:T(8,128)(2,1)}, f32[32,8,128]{2,1,0:T(8,128)S(1)}) custom-call(s32[32,8,128]{2,1,0:T(8,128)S(1)} %get-tuple-element.32.rank_ref, bf16[8,1024,2048]{2,1,0:T(8,128)(2,1)} %get-tuple-element.36.y_ref, bf16[8,1024,2048]{2,1,0:T(8,128)(2,1)} %get-tuple-element.37.z_ref, ...), custom_call_target="tpu_custom_call" | custom-call | tf_op jit(solution)/shard_map/combine/pallas_call | solution.py:787
  541.7 97.1 %scatter_all.3 = f32[128,2048]{1,0:T(8,128)S(1)} custom-call(bf16[32,128,2048]{2,1,0:T(8,128)(2,1)} %get-tuple-element.40.p_ref), custom_call_target="tpu_custom_call" | custom-call | tf_op jit(solution)/shard_map/scatter_all/pallas_call | solution.py:233
  638.9 10.5 %scatter_probs.1 = f32[4,2,8,128]{3,2,1,0:T(8,128)S(1)} custom-call(f32[2,2,2,4,8,128]{5,4,3,2,1,0:T(8,128)S(1)} %bitcast.171), custom_call_target="tpu_custom_call" | custom-call | tf_op jit(solution)/shard_map/scatter_probs/pallas_call | solution.py:512
  650.6 60.1 %gather_seq.1 = bf16[8,128,2048]{2,1,0:T(8,128)(2,1)S(1)} custom-call(bf16[128,2048]{1,0:T(8,128)(2,1)S(1)} %fusion.56.h_ref), custom_call_target="tpu_custom_call" | custom-call | tf_op jit(solution)/shard_map/gather_seq/pallas_call | solution.py:396
  710.7 1.3 convolution_convert_fusion.2
  712.0 1.3 multiply_reduce_fusion.5
  713.7 2.6 fusion.14
  716.4 3.2 multiply_convert_fusion.1
  719.6 1.5 convolution_bitcast_fusion
  721.2 0.9 broadcast_multiply_fusion.1
  722.3 0.8 copy-done.27
  723.6 0.5 copy-done.15
  724.2 0.6 fusion.29
  724.8 6.8 sum_seq.3
  732.1 6.7 multiply_reduce_fusion
  738.8 4.0 convolution_convert_fusion.1
  742.9 1.9 copy.89
  744.8 0.8 concatenate.53
  745.6 1.7 copy.68
  747.3 1.4 copy.69
  749.0 1.4 copy.70
  750.4 1.7 broadcast_select_fusion
  752.0 1.1 broadcast_in_dim.97
  753.2 4.2 concatenate.56
  757.3 78.2 %scatter_last.1 = (f32[128,2048]{1,0:T(8,128)S(1)}, f32[8,64,768]{2,1,0:T(8,128)S(1)}, f32[64,2048]{1,0:T(8,128)S(1)}, f32[64,128]{1,0:T(8,128)S(1)}) custom-call(bf16[8,128,2048]{2,1,0:T(8,128)(2,1)} %bitcast.188, bf16[2,2,8,64,768]{4,3,2,1,0:T(8,128)(2,1)} %bitcast.178, bf16[2,2,64,2048]{3,2,1,0:T(8,128)(2,1)S(1)} %bitcast.165, ...), custom_call_target="tpu_custom_call" | custom-call | tf_op jit(solution)/shard_map/scatter_last/pallas_call | solution.py:632
  835.9 89.1 %scatter_all.2 = f32[128,2048]{1,0:T(8,128)S(1)} custom-call(bf16[32,128,2048]{2,1,0:T(8,128)(2,1)} %get-tuple-element.39.p_ref), custom_call_target="tpu_custom_call" | custom-call | tf_op jit(solution)/shard_map/scatter_all/pallas_call | solution.py:233
  925.0 3.7 reshape.376
  928.7 2.6 copy.71
  931.3 1.6 copy.84
  933.0 0.7 copy.72
  933.7 3.3 fusion.23
  936.9 0.8 copy.95
  937.7 0.6 copy.96
  (159 shorter events, 6.6 us)
Async XLA Ops:
  7.2 3.5 copy-start.50
  7.2 3.7 copy-start.52
  7.2 3.7 copy-start.46
  7.2 3.8 copy-start.36
  7.2 3.9 copy-start.2
  7.2 3.9 copy-start.8
  7.2 314.7 %all-gather.3.cloned.1.call-start = ((), (), s32[]{:S(2)}) async-start(), calls=%async_computation | async-start | bytes 17301504 | tf_op jit(solution)/shard_map/all_gather | solution.py:1168
  143.1 3.8 copy-start
  143.1 4.8 copy-start.9
  151.5 13.8 %copy-start.13 = (f32[1024,768]{0,1:T(8,128)}, f32[1024,768]{0,1:T(8,128)S(1)}, u32[]{:S(2)}) copy-start(f32[1024,768]{0,1:T(8,128)S(1)} %fusion.59) | copy-start | bytes 9437188
  151.6 24.2 %copy-start.30 = (bf16[1024,256]{0,1:T(8,128)(2,1)}, bf16[1024,256]{0,1:T(8,128)(2,1)S(1)}, u32[]{:S(2)}) copy-start(bf16[1024,256]{0,1:T(8,128)(2,1)S(1)} %slice.169) | copy-start | bytes 1572868
  165.4 4.7 copy-start.14
  166.8 3.8 copy-start.37
  166.8 3.8 copy-start.39
  170.0 0.6 copy-start.32
  170.0 0.6 copy-start.34
  171.3 2.6 copy-start.23
  171.3 2.6 copy-start.25
  171.9 4.0 copy-start.21
  173.9 3.3 copy-start.17
  180.7 1.3 copy-start.28
  229.6 1.0 copy-start.11
  229.7 89.9 %copy-start.41 = (f32[128]{0:T(128)}, f32[128]{0:T(128)S(1)}, u32[]{:S(2)}) copy-start(f32[128]{0:T(128)S(1)} %add_rsqrt_fusion.3) | copy-start | bytes 1540
  231.6 88.8 %copy-start.18 = (bf16[128,2048]{1,0:T(8,128)(2,1)S(1)}, bf16[128,2048]{1,0:T(8,128)(2,1)}, u32[]{:S(2)}) copy-start(bf16[128,2048]{1,0:T(8,128)(2,1)} %multiply_convert_fusion.5.x_ref) | copy-start | bytes 1572868
  371.5 1.9 copy-start.3
  495.6 2.2 copy-start.4
  541.7 107.9 %copy-start.12 = (f32[128,2048]{1,0:T(8,128)S(1)}, f32[128,2048]{1,0:T(8,128)}, u32[]{:S(2)}) copy-start(f32[128,2048]{1,0:T(8,128)} %copy-done.11) | copy-start | bytes 3145732
  541.7 107.9 %copy-start.42 = (f32[128]{0:T(128)S(1)}, f32[128]{0:T(128)}, u32[]{:S(2)}) copy-start(f32[128]{0:T(128)} %copy-done.41) | copy-start | bytes 1540
  638.9 11.4 %copy-start.20 = (bf16[1,128,2048]{2,1,0:T(8,128)(2,1)S(1)}, bf16[1,128,2048]{2,1,0:T(8,128)(2,1)}, u32[]{:S(2)}) copy-start(bf16[1,128,2048]{2,1,0:T(8,128)(2,1)} %param.17) | copy-start | bytes 1572868
  650.2 61.8 %copy-start.16 = (f32[128,2048]{1,0:T(8,128)}, f32[128,2048]{1,0:T(8,128)S(1)}, u32[]{:S(2)}) copy-start(f32[128,2048]{1,0:T(8,128)S(1)} %get-tuple-element.128) | copy-start | bytes 3145732
  650.2 60.5 %copy-start.29 = (bf16[1024,2,128]{0,2,1:T(8,128)(2,1)S(1)}, bf16[1024,2,128]{0,2,1:T(8,128)(2,1)}, u32[]{:S(2)}) copy-start(bf16[1024,2,128]{0,2,1:T(8,128)(2,1)} %copy-done.28) | copy-start | bytes 1572868
  650.2 61.7 %copy-start.48 = (f32[128]{0:T(128)}, f32[128]{0:T(128)S(1)}, u32[]{:S(2)}) copy-start(f32[128]{0:T(128)S(1)} %broadcast_multiply_fusion.7) | copy-start | bytes 1540
  650.6 62.7 %slice-start = ((s8[8388608]{0:T(1024)(128)(4,1)}), s8[4194304]{0:T(1024)(128)(4,1)S(1)}, s32[]{:S(2)}) async-start(s8[8388608]{0:T(1024)(128)(4,1)} %bitcast.184), calls=%async_computation.1 | async-start | bytes 8388608
  710.7 1.3 copy-start.53
  710.7 2.6 slice-start.1
  712.0 1.7 copy-start.22
  712.0 1.7 copy-start.44
  713.7 2.6 copy-start.31
  716.4 3.3 copy-start.26
  719.6 1.6 copy-start.19
  719.6 1.6 copy-start.24
  722.1 1.0 copy-start.27
  722.2 2.0 copy-start.15
  722.2 2.0 copy-start.33
  722.2 2.0 copy-start.35
  722.2 2.0 copy-start.38
  722.2 2.0 copy-start.40
  724.2 7.9 copy-start.1
  724.2 7.9 copy-start.10
  724.2 7.9 copy-start.45
  744.7 5.6 copy-start.51
  757.3 78.3 %copy-start.47 = (f32[128]{0:T(128)S(1)}, f32[128]{0:T(128)}, u32[]{:S(2)}) copy-start(f32[128]{0:T(128)} %add_rsqrt_fusion.2) | copy-start | bytes 1540
  835.6 89.4 %copy-start.5 = (f32[128,2048]{1,0:T(8,128)}, f32[128,2048]{1,0:T(8,128)S(1)}, u32[]{:S(2)}) copy-start(f32[128,2048]{1,0:T(8,128)S(1)} %get-tuple-element.42) | copy-start | bytes 3145732
  835.6 89.4 %copy-start.7 = (f32[8,64,768]{2,1,0:T(8,128)}, f32[8,64,768]{2,1,0:T(8,128)S(1)}, u32[]{:S(2)}) copy-start(f32[8,64,768]{2,1,0:T(8,128)S(1)} %get-tuple-element.43) | copy-start | bytes 4718596
  928.7 5.0 copy-start.6
  928.7 5.0 copy-start.43
  928.7 5.0 copy-start.49
Sparse Core Ops, SparseCore 0:
  10.9 169.1 all-gather.2

commit v3 on v2

--- a/solution.py
+++ b/solution.py
@@ -94,69 +94,6 @@
             copy.wait_send()
 
 
-def gather_all_kernel(x_ref, out_ref, send_sem, recv_sem, own_sem):
-    p = Place()
-    rows = x_ref.shape[0]
-    half = rows // 2
-    barrier([p.at(1), p.at(2), p.at(3), p.at(y=1), p.at(x=1), p.at(c=1)])
-    own = pltpu.make_async_copy(x_ref, out_ref.at[p.index()], own_sem)
-    own.start()
-    sends = Sends(send_sem, recv_sem)
-    A, B = pl.ds(0, half), pl.ds(half, half)
-
-    def forward(index, peer, part=None):
-        ref = out_ref.at[index] if part is None else out_ref.at[index, part]
-        return sends.start(ref, ref, peer)
-
-    mine = p.index()
-    along = [None] + [sends.start(x_ref, out_ref.at[mine], p.at(r)) for r in (1, 3, 2)]
-    along = {0: None, 1: along[1], 3: along[2], 2: along[3]}
-    from_x, from_y, from_core, diag = {}, {}, [], []
-    order = (0, 1, 3, 2)
-    for r in order:
-        index = p.index(-r % 4)
-        if r:
-            along[r].wait_recv()
-        src = x_ref if r == 0 else out_ref.at[index]
-        from_x[r] = sends.start(src, out_ref.at[index], p.at(x=1))
-        from_y[r] = sends.start(src, out_ref.at[index], p.at(y=1))
-        from_core.append(sends.start(src, out_ref.at[index], p.at(c=1)))
-    for r in order:
-        ix, iy = p.index(-r % 4, x=1), p.index(-r % 4, y=1)
-        from_x[r].wait_recv()
-        diag.append(forward(ix, p.at(y=1), A))
-        from_y[r].wait_recv()
-        diag.append(forward(iy, p.at(x=1), B))
-        from_core.append(forward(ix, p.at(c=1)))
-        from_core.append(forward(iy, p.at(c=1)))
-    for n, r in enumerate(order):
-        index = p.index(-r % 4, x=1, y=1)
-        diag[2 * n].wait_recv()
-        diag[2 * n + 1].wait_recv()
-        from_core.append(forward(index, p.at(c=1)))
-    for copy in from_core:
-        copy.wait_recv()
-    sends.finish()
-    own.wait()
-
-
-def gather_all(x, collective_id):
-    n = 3 + 12 + 8 + 12
-    return pl.pallas_call(
-        gather_all_kernel,
-        name="gather_all",
-        out_shape=jax.ShapeDtypeStruct((32,) + x.shape, x.dtype),
-        in_specs=[ANY],
-        out_specs=ANY,
-        scratch_shapes=[
-            pltpu.SemaphoreType.DMA((n,)),
-            pltpu.SemaphoreType.DMA((n,)),
-            pltpu.SemaphoreType.DMA,
-        ],
-        compiler_params=pltpu.CompilerParams(collective_id=collective_id, has_side_effects=True),
-    )(x)
-
-
 def add_rows(dst, src, start, rows):
     step = 16
 
@@ -166,92 +103,6 @@
         return 0
 
     lax.fori_loop(0, rows // step, body, 0)
-
-
-def scatter_all_kernel(p_ref, out_ref, acc, rc, rdx, rdy, rx, ry, rz, send_sem, recv_sem, own_sem):
-    p = Place()
-    rows = acc.shape[1]
-    half = rows // 2
-    A, B = pl.ds(0, half), pl.ds(half, half)
-    barrier([p.at(1), p.at(2), p.at(3), p.at(y=1), p.at(x=1), p.at(c=1)])
-    sends = Sends(send_sem, recv_sem)
-    order = (2, 1, 3, 0)
-    slots = [(r, y, x) for (y, x) in ((1, 1), (0, 1), (1, 0), (0, 0)) for r in order]
-    loads, cores = [], []
-    for k, (r, y, x) in enumerate(slots):
-        load = pltpu.make_async_copy(p_ref.at[p.index(r, y, x)], acc.at[k], own_sem.at[k])
-        load.start()
-        loads.append(load)
-        cores.append(sends.start(p_ref.at[p.index(r, y, x, 1)], rc.at[k], p.at(c=1)))
-
-    def core_sum(k):
-        loads[k].wait()
-        cores[k].wait_recv()
-        add_rows(acc.at[k], rc.at[k], 0, rows)
-
-    dx, dy, fx, fy, fz = [], [], [], [], []
-    for n in range(4):
-        core_sum(n)
-        dy.append(sends.start(acc.at[n, A], rdy.at[n], p.at(y=1)))
-        dx.append(sends.start(acc.at[n, B], rdx.at[n], p.at(x=1)))
-    for n in range(4):
-        core_sum(4 + n)
-        dy[n].wait_recv()
-        add_rows(acc.at[4 + n], rdy.at[n], 0, half)
-        fx.append(sends.start(acc.at[4 + n], rx.at[n], p.at(x=1)))
-        core_sum(8 + n)
-        dx[n].wait_recv()
-        add_rows(acc.at[8 + n, B], rdx.at[n], 0, half)
-        fy.append(sends.start(acc.at[8 + n], ry.at[n], p.at(y=1)))
-    for n, r in enumerate(order):
-        core_sum(12 + n)
-        fx[n].wait_recv()
-        add_rows(acc.at[12 + n], rx.at[n], 0, rows)
-        fy[n].wait_recv()
-        add_rows(acc.at[12 + n], ry.at[n], 0, rows)
-        if r:
-            fz.append(sends.start(acc.at[12 + n], rz.at[n], p.at(r)))
-    for copy in fz:
-        copy.wait_recv()
-
-    def total(i, _):
-        at = pl.ds(pl.multiple_of(i * 16, 16), 16)
-        value = acc[15, at].astype(f32)
-        for n in range(3):
-            value = value + rz[n, at].astype(f32)
-        out_ref[at] = value.astype(out_ref.dtype)
-        return 0
-
-    lax.fori_loop(0, rows // 16, total, 0)
-    sends.finish()
-
-
-def scatter_all(parts, collective_id, dtype=bf16):
-    block = parts.shape[1:]
-    half = (block[0] // 2,) + block[1:]
-    n = 16 + 8 + 8 + 3
-    return pl.pallas_call(
-        scatter_all_kernel,
-        name="scatter_all",
-        out_shape=jax.ShapeDtypeStruct(block, dtype),
-        in_specs=[ANY],
-        out_specs=WHOLE,
-        scratch_shapes=[
-            pltpu.VMEM((16,) + block, parts.dtype),
-            pltpu.VMEM((16,) + block, parts.dtype),
-            pltpu.VMEM((4,) + half, parts.dtype),
-            pltpu.VMEM((4,) + half, parts.dtype),
-            pltpu.VMEM((4,) + block, parts.dtype),
-            pltpu.VMEM((4,) + block, parts.dtype),
-            pltpu.VMEM((3,) + block, parts.dtype),
-            pltpu.SemaphoreType.DMA((n,)),
-            pltpu.SemaphoreType.DMA((n,)),
-            pltpu.SemaphoreType.DMA((16,)),
-        ],
-        compiler_params=pltpu.CompilerParams(
-            collective_id=collective_id, has_side_effects=True, vmem_limit_bytes=48 << 20
-        ),
-    )(parts)
 
 
 def call(kernel, name, collective_id, out_shape, in_specs, out_specs, scratch, copies, local=1, vmem=32):
@@ -481,51 +332,6 @@
         [pltpu.VMEM((8,) + x.shape, x.dtype)],
         7,
     )(x)
-
-
-def scatter_probs_kernel(p_ref, out_ref, sum_x, sum_s, r1, r2, got, send_sem, recv_sem, own_sem):
-    p = Place()
-    others = [p.at(r, y) for y in (0, 1) for r in range(4) if r or y]
-    barrier(others + [p.at(x=1), p.at(c=1)])
-    sends = Sends(send_sem, recv_sem)
-    first = sends.start(p_ref.at[1 - p.c], r1, p.at(c=1))
-    first.wait_recv()
-    sum_x[...] = p_ref[p.c] + r1[...]
-    second = sends.start(sum_x.at[1 - p.x], r2, p.at(x=1))
-    second.wait_recv()
-    sum_s[...] = sum_x[p.x] + r2[...]
-    copies = []
-    for r, y in ((0, 1), (1, 0), (3, 0), (2, 0), (1, 1), (3, 1), (2, 1)):
-        to = lax.rem(p.z + r, 4)
-        yy = 1 - p.y if y else p.y
-        copies.append(sends.start(sum_s.at[yy, to], got.at[p.z, p.y], p.at(r, y)))
-    got[p.z, p.y] = sum_s[p.y, p.z]
-    for copy in copies:
-        copy.wait_recv()
-    out_ref[...] = got[...]
-    sends.finish()
-
-
-def scatter_probs(parts, collective_id):
-    experts, rows = parts.shape[-2:]
-    block = (experts, rows)
-    out = call(
-        scatter_probs_kernel,
-        "scatter_probs",
-        collective_id,
-        jax.ShapeDtypeStruct((4, 2) + block, f32),
-        [WHOLE],
-        WHOLE,
-        [
-            pltpu.VMEM((2, 2, 4) + block, f32),
-            pltpu.VMEM((2, 4) + block, f32),
-            pltpu.VMEM((2, 2, 4) + block, f32),
-            pltpu.VMEM((2, 4) + block, f32),
-            pltpu.VMEM((4, 2) + block, f32),
-        ],
-        9,
-    )(parts)
-    return out.reshape(8 * experts, rows)
 
 
 def add_blocks(dst, src):
@@ -659,144 +465,533 @@
     return jnp.where(hot, 1.0, 0.0).reshape(experts * CAP, rows).astype(bf16)
 
 
-def dispatch_kernel(first_ref, routes_ref, x_ref, g_ref, router_ref, xs_ref, gs_ref, gate_ref, rank_ref, probs):
-    experts = rank_ref.shape[1]
-    rows = x_ref.shape[1]
-    first = pl.multiple_of(first_ref[0], experts)
-    routes = routes_ref[0]
-    hits = []
-    for e in range(experts):
-        same = jnp.where(routes == first + e, 1.0, 0.0)
-        hits.append(jnp.max(same, axis=0, keepdims=True))
-    hit = jnp.concatenate(hits, axis=0)
-    before = lax.broadcasted_iota(jnp.int32, (rows, rows), 0) < lax.broadcasted_iota(jnp.int32, (rows, rows), 1)
-    rank = jnp.dot(hit.astype(bf16), jnp.where(before, 1.0, 0.0).astype(bf16), preferred_element_type=f32)
-    rank = jnp.where(hit > 0.5, rank.astype(jnp.int32), -1)
-    rank_ref[0] = rank
-    hot = slots_of_rows(rank)
-    place = one_hot(hot)
-    x = x_ref[0]
-    logits = dot(router_ref[...], x, ((1,), (1,)))
-    weights = jnp.exp(logits - jnp.max(logits, axis=0, keepdims=True))
-    probs[...] = weights / jnp.sum(weights, axis=0, keepdims=True)
-    mine = probs[pl.ds(first, experts)]
-    gate = jnp.sum(jnp.where(hot, mine[:, None, :], 0.0), axis=-1, keepdims=True)
-    gate_ref[...] = jnp.broadcast_to(gate, gate_ref.shape)
-    xs_ref[...] = jnp.dot(place, x, preferred_element_type=f32).astype(bf16).reshape(xs_ref.shape)
-    gs_ref[...] = jnp.dot(place, g_ref[0], preferred_element_type=f32).astype(bf16).reshape(gs_ref.shape)
-
-
-def dispatch(first, routes_all, x_all, g_all, router_rows, experts):
-    groups, rows, width = x_all.shape
-    slots = groups * CAP
-    return pl.pallas_call(
-        dispatch_kernel,
-        name="dispatch",
-        grid=(groups,),
-        out_shape=(
-            jax.ShapeDtypeStruct((experts, slots, width), bf16),
-            jax.ShapeDtypeStruct((experts, slots, width), bf16),
-            jax.ShapeDtypeStruct((experts, slots, 128), f32),
-            jax.ShapeDtypeStruct((groups, experts, rows), jnp.int32),
-        ),
-        in_specs=[
-            pl.BlockSpec(memory_space=pltpu.SMEM),
-            pl.BlockSpec((1,) + routes_all.shape[1:], lambda d: (d, 0, 0)),
-            pl.BlockSpec((1, rows, width), lambda d: (d, 0, 0)),
-            pl.BlockSpec((1, rows, width), lambda d: (d, 0, 0)),
-            pl.BlockSpec(router_rows.shape, lambda d: (0, 0)),
-        ],
-        out_specs=(
-            pl.BlockSpec((experts, CAP, width), lambda d: (0, d, 0)),
-            pl.BlockSpec((experts, CAP, width), lambda d: (0, d, 0)),
-            pl.BlockSpec((experts, CAP, 128), lambda d: (0, d, 0)),
-            pl.BlockSpec((1, experts, rows), lambda d: (d, 0, 0)),
-        ),
-        scratch_shapes=[pltpu.VMEM((router_rows.shape[0], rows), f32)],
-        compiler_params=pltpu.CompilerParams(vmem_limit_bytes=40 << 20),
-    )(first, routes_all, x_all, g_all, router_rows)
-
-
-def experts_kernel(w_ref, xs_ref, gs_ref, gate_ref, y_ref, z_ref, wg_ref, gg_ref):
-    x, g = xs_ref[0], gs_ref[0]
-    gain = gate_ref[0][:, :1]
-    gate = jnp.dot(x, w_ref[0, 0], preferred_element_type=f32)
-    up = jnp.dot(x, w_ref[0, 1], preferred_element_type=f32)
-    raw = jnp.dot(g, w_ref[0, 2], preferred_element_type=f32)
+BACK = (1, 3, 2, 0)
+
+
+class Flip(Place):
+    def block(self, r=0, y=0, x=0, c=0):
+        z = lax.rem(self.z + 4 - r, 4)
+        yy, xx, cc = lax.rem(self.y + y, 2), lax.rem(self.x + x, 2), lax.rem(self.c + c, 2)
+        return ((z * 2 + yy) * 2 + xx) * 2 + cc
+
+
+def remote(src, dst, send, recv, peer):
+    return pltpu.make_async_remote_copy(
+        src_ref=src, dst_ref=dst, send_sem=send, recv_sem=recv, device_id=peer, device_id_type=MESH
+    )
+
+
+class Gather:
+    @staticmethod
+    def scratch():
+        S = pltpu.SemaphoreType.DMA
+        return [S((35,)), S((35,)), S]
+
+    def __init__(self, p, x_ref, x_all, refs):
+        send, recv, own_sem = refs
+        rows = x_ref.shape[0]
+        A, B = pl.ds(0, rows // 2), pl.ds(rows // 2, rows // 2)
+        nx, ny, core = p.at(x=1), p.at(y=1), p.at(c=1)
+        self.peers = [p.at(1), p.at(2), p.at(3), nx, ny, core]
+        mine = p.block()
+        self.own = pltpu.make_async_copy(x_ref, x_all.at[mine], own_sem)
+        count = [0]
+
+        def copy(src, dst, peer):
+            i = count[0]
+            count[0] += 1
+            return remote(src, dst, send.at[i], recv.at[i], peer)
+
+        self.along, self.to_x, self.to_y, self.to_core, self.by_y, self.by_x = [], [], [], [], [], []
+        for k, r in enumerate(BACK):
+            at, ix, iy, far = p.block(r), p.block(r, x=1), p.block(r, y=1), p.block(r, y=1, x=1)
+            src = x_all.at[at]
+            if r:
+                self.along.append(copy(x_ref, x_all.at[mine], p.at(r)))
+            else:
+                src = x_ref
+            self.to_x.append(copy(src, x_all.at[at], nx))
+            self.to_y.append(copy(src, x_all.at[at], ny))
+            self.by_y.append(copy(x_all.at[ix, A], x_all.at[ix, A], ny))
+            self.by_x.append(copy(x_all.at[iy, B], x_all.at[iy, B], nx))
+            self.to_core.append(
+                [copy(src, x_all.at[at], core)]
+                + [copy(x_all.at[i], x_all.at[i], core) for i in (ix, iy, far)]
+            )
+
+    def start(self):
+        self.own.start()
+        for copy in self.along:
+            copy.start()
+        self.own.wait()
+
+    def spread(self, k):
+        if BACK[k]:
+            self.along[k].wait_recv()
+        self.to_x[k].start()
+        self.to_y[k].start()
+        self.to_core[k][0].start()
+
+    def cross(self, k):
+        self.to_x[k].wait_recv()
+        self.by_y[k].start()
+        self.to_core[k][1].start()
+        self.to_y[k].wait_recv()
+        self.by_x[k].start()
+        self.to_core[k][2].start()
+
+    def close(self, k):
+        self.by_y[k].wait_recv()
+        self.by_x[k].wait_recv()
+        self.to_core[k][3].start()
+
+    def finish(self):
+        for copy in self.along:
+            copy.wait_send()
+        for k in range(4):
+            for copy in [self.to_x[k], self.to_y[k], self.by_y[k], self.by_x[k]] + self.to_core[k]:
+                copy.wait_send()
+
+
+class Scatter:
+    @staticmethod
+    def scratch(rows, width):
+        V, S = pltpu.VMEM, pltpu.SemaphoreType.DMA
+        block, half = (rows, width), (rows // 2, width)
+        return [
+            V((2, 4) + block, bf16), V((2, 2, 3) + block, bf16), V((2, 4) + block, bf16), V((2, 2) + half, bf16),
+            V((2, 2) + block, bf16), V((4, 2) + block, bf16), V((3, 2) + block, bf16),
+            S((32,)), S((32,)), S((38,)), S((38,)), pltpu.SemaphoreType.REGULAR((5,)),
+        ]
+
+    def __init__(self, p, refs):
+        self.give, self.stage, self.pair, self.half, self.near, self.acc, self.far = refs[:7]
+        self.core_send, self.core_recv, send, recv, self.free = refs[7:]
+        self.p = p
+        rows = self.give.shape[2]
+        self.parts = A, B = pl.ds(0, rows // 2), pl.ds(rows // 2, rows // 2)
+        nx, ny = p.at(x=1), p.at(y=1)
+        self.core, self.nx, self.ny = p.at(c=1), nx, ny
+        count = [0]
+
+        def copy(src, dst, peer):
+            i = count[0]
+            count[0] += 1
+            return remote(src, dst, send.at[i], recv.at[i], peer)
+
+        self.by_y, self.by_x, self.to_x, self.to_y, self.to_z = [], [], [], [], []
+        for k in range(4):
+            out = [self.stage.at[k % 2, i] for i in (0, 1)]
+            self.by_y.append([copy(out[i].at[2, A], self.half.at[i, 0], ny) for i in (0, 1)])
+            self.by_x.append([copy(out[i].at[2, B], self.half.at[i, 1], nx) for i in (0, 1)])
+            self.to_x.append([copy(out[i].at[0], self.near.at[i, 0], nx) for i in (0, 1)])
+            self.to_y.append([copy(out[i].at[1], self.near.at[i, 1], ny) for i in (0, 1)])
+            if BACK[k]:
+                to = p.at((4 - BACK[k]) % 4)
+                self.to_z.append([copy(self.acc.at[k, i], self.far.at[k, i], to) for i in (0, 1)])
+
+    def to_core(self, k, i, pos):
+        at = k * 8 + i * 4 + pos
+        return remote(
+            self.give.at[i, pos], self.pair.at[i, pos], self.core_send.at[at], self.core_recv.at[at], self.core
+        )
+
+    def add(self, dst, terms):
+        step = 32
+
+        def body(i, _):
+            at = pl.ds(pl.multiple_of(i * step, step), step)
+            if len(terms) == 2 and dst.dtype == bf16:
+                dst[at] = terms[0][at] + terms[1][at]
+                return 0
+            value = terms[0][at].astype(f32)
+            for term in terms[1:]:
+                value = value + term[at].astype(f32)
+            dst[at] = value.astype(dst.dtype)
+            return 0
+
+        lax.fori_loop(0, dst.shape[0] // step, body, 0)
+
+    def signal(self, n, peer):
+        pl.semaphore_signal(self.free.at[n], inc=1, device_id=peer, device_id_type=MESH)
+
+    def diagonal(self, k, i):
+        if k and not i:
+            pl.semaphore_wait(self.free.at[1], 1)
+            pl.semaphore_wait(self.free.at[2], 1)
+        self.to_core(k, i, 3).wait_recv()
+        at = self.stage.at[k % 2, i, 2]
+        self.add(at, [at, self.pair.at[i, 3]])
+        self.by_y[k][i].start()
+        self.by_x[k][i].start()
+
+    def across(self, k, i):
+        A, B = self.parts
+        for_x, for_y = self.stage.at[k % 2, i, 0], self.stage.at[k % 2, i, 1]
+        if k and not i:
+            pl.semaphore_wait(self.free.at[3], 1)
+            pl.semaphore_wait(self.free.at[4], 1)
+        self.to_core(k, i, 1).wait_recv()
+        self.add(for_x.at[B], [for_x.at[B], self.pair.at[i, 1, B]])
+        self.by_y[k][i].wait_recv()
+        self.add(for_x.at[A], [for_x.at[A], self.pair.at[i, 1, A], self.half.at[i, 0]])
+        self.to_x[k][i].start()
+        self.to_core(k, i, 2).wait_recv()
+        self.add(for_y.at[A], [for_y.at[A], self.pair.at[i, 2, A]])
+        self.by_x[k][i].wait_recv()
+        self.add(for_y.at[B], [for_y.at[B], self.pair.at[i, 2, B], self.half.at[i, 1]])
+        self.to_y[k][i].start()
+        self.to_core(k, i, 0).wait_recv()
+        self.add(self.acc.at[k, i], [self.acc.at[k, i], self.pair.at[i, 0]])
+        if k < 3 and i:
+            self.signal(0, self.core)
+            self.signal(1, self.nx)
+            self.signal(2, self.ny)
+
+    def line(self, k, i):
+        self.to_x[k][i].wait_recv()
+        self.to_y[k][i].wait_recv()
+        self.add(self.acc.at[k, i], [self.acc.at[k, i], self.near.at[i, 0], self.near.at[i, 1]])
+        if BACK[k]:
+            self.to_z[k][i].start()
+        if k < 3 and i:
+            self.signal(3, self.nx)
+            self.signal(4, self.ny)
+
+    def settle_core(self, k):
+        for i in (0, 1):
+            for pos in range(4):
+                self.to_core(k, i, pos).wait_send()
+
+    def settle(self, k):
+        for i in (0, 1):
+            for copies in (self.by_y, self.by_x, self.to_x, self.to_y):
+                copies[k][i].wait_send()
+
+    def finish(self, i, out_ref):
+        for copies in self.to_z:
+            copies[i].wait_recv()
+        self.add(out_ref, [self.acc.at[3, i]] + [self.far.at[n, i] for n in range(3)])
+
+    def end(self):
+        self.settle_core(3)
+        self.settle(2)
+        self.settle(3)
+        for copies in self.to_z:
+            for copy in copies:
+                copy.wait_send()
+
+
+class Probs:
+    TURNS = ((0, 1), (1, 0), (3, 0), (2, 0), (1, 1), (3, 1), (2, 1))
+
+    @staticmethod
+    def scratch(block):
+        V, S = pltpu.VMEM, pltpu.SemaphoreType.DMA
+        return [
+            V((2, 2, 2, 4) + block, f32), V((2, 2, 4) + block, f32), V((2, 4) + block, f32), V((2, 2, 4) + block, f32),
+            V((2, 4) + block, f32), V((4, 2) + block, f32), S((9,)), S((9,)),
+        ]
+
+    def __init__(self, p, refs):
+        self.p = p
+        self.own, self.sum_x, self.sum_s, self.r1, self.r2, self.got, send, recv = refs
+        self.peers = [p.at(r, y) for r, y in self.TURNS]
+        self.first = remote(self.own.at[1 - p.c], self.r1, send.at[0], recv.at[0], p.at(c=1))
+        self.second = remote(self.sum_x.at[1 - p.x], self.r2, send.at[1], recv.at[1], p.at(x=1))
+        self.third = []
+        for n, (r, y) in enumerate(self.TURNS):
+            to = lax.rem(p.z + r, 4)
+            yy = 1 - p.y if y else p.y
+            self.third.append(
+                remote(self.sum_s.at[yy, to], self.got.at[p.z, p.y], send.at[2 + n], recv.at[2 + n], p.at(r, y))
+            )
+
+    def start(self):
+        self.first.start()
+
+    def over_x(self):
+        self.first.wait_recv()
+        self.sum_x[...] = self.own[self.p.c] + self.r1[...]
+        self.second.start()
+
+    def over_seq(self):
+        p = self.p
+        self.second.wait_recv()
+        self.sum_s[...] = self.sum_x[p.x] + self.r2[...]
+        for copy in self.third:
+            copy.start()
+        self.got[p.z, p.y] = self.sum_s[p.y, p.z]
+
+    def finish(self, out_ref):
+        for copy in self.third:
+            copy.wait_recv()
+        out_ref[...] = self.got[...]
+        for copy in [self.first, self.second] + self.third:
+            copy.wait_send()
+
+
+GATHER, SCATTER, PROBS = 3, 12, 8
+
+
+def mixture_kernel(
+    routes_ref, router_ref, x_ref, g_ref, w_ref,
+    x_all, xs_out, gs_out, st_ref, grad_out, sum_out, probs_out,
+    tx, tg, xs, gs, gates, grads, ranks, weights, load_sem, save_sem, *rest,
+):
+    p = Flip()
+    chunk, e = pl.program_id(0), pl.program_id(1)
+    experts, slots, width = xs.shape
+    rows = tx.shape[1]
+    gather = Gather(p, x_ref, x_all, rest[:GATHER])
+    scatter = Scatter(p, rest[GATHER : GATHER + SCATTER])
+    probs = Probs(p, rest[GATHER + SCATTER :])
+    last = experts - 1
+
+    def at_step(k, step, *events):
+        def run():
+            for event, *args in events:
+                event(*args)
+
+        pl.when((chunk == k) & (e == step))(run)
+
+    def begin():
+        barrier(gather.peers + [peer for peer, (r, y) in zip(probs.peers, probs.TURNS) if r and y])
+        gather.start()
+        gather.spread(3)
+        gather.spread(0)
+        gather.spread(1)
+        gather.cross(0)
+        gather.spread(2)
+        gather.close(0)
+
+    at_step(0, 0, (begin,))
+    at_step(0, 1, (gather.cross, 1))
+    at_step(0, 4, (gather.close, 1), (gather.cross, 2))
+    at_step(0, 6, (gather.close, 2), (gather.cross, 3))
+    at_step(1, 1, (gather.close, 3))
+    for k in range(3):
+        before = [(scatter.line, k - 1, 1)] if k else []
+        at_step(k + 1, 0, *before, (scatter.diagonal, k, 0), (scatter.diagonal, k, 1))
+        at_step(k + 1, 1, (scatter.across, k, 0))
+        at_step(k + 1, 2, (scatter.across, k, 1))
+        at_step(k + 1, 6, (scatter.line, k, 0))
+
+    back = jnp.where(chunk == 0, BACK[0], jnp.where(chunk == 1, BACK[1], jnp.where(chunk == 2, BACK[2], BACK[3])))
+    first = p.at()[0] * experts
+
+    def save(k, i):
+        src, dst = ((xs, xs_out), (gs, gs_out))[i]
+        return pltpu.make_async_copy(src.at[k], dst.at[chunk, k], save_sem.at[i, k])
+
+    def place_rows(j):
+        y, x, c = j // 4, (j // 2) % 2, j % 2
+        routes = routes_ref[p.block(back, y, x, c)]
+        hits = []
+        for k in range(experts):
+            same = jnp.where(routes == first + k, 1.0, 0.0)
+            hits.append(jnp.max(same, axis=0, keepdims=True))
+        hit = jnp.concatenate(hits, axis=0)
+        before = lax.broadcasted_iota(jnp.int32, (rows, rows), 0) < lax.broadcasted_iota(
+            jnp.int32, (rows, rows), 1
+        )
+        rank = jnp.dot(hit.astype(bf16), jnp.where(before, 1.0, 0.0).astype(bf16), preferred_element_type=f32)
+        rank = jnp.where(hit > 0.5, rank.astype(jnp.int32), -1)
+        ranks[j] = rank
+        hot = slots_of_rows(rank)
+        place = one_hot(hot)
+        b = j % 2
+        rows_x = tx[b]
+        logits = dot(router_ref[...], rows_x, ((1,), (1,)))
+        powers = jnp.exp(logits - jnp.max(logits, axis=0, keepdims=True))
+        weights[...] = powers / jnp.sum(powers, axis=0, keepdims=True)
+        chosen = weights[pl.ds(pl.multiple_of(first, experts), experts)]
+        gate = jnp.sum(jnp.where(hot, chosen[:, None, :], 0.0), axis=-1, keepdims=True)
+        at = pl.ds(j * CAP, CAP)
+        gates[:, at] = jnp.broadcast_to(gate, (experts, CAP, 128))
+        shape = (experts, CAP, width)
+        xs[:, at] = jnp.dot(place, rows_x, preferred_element_type=f32).astype(bf16).reshape(shape)
+        gs[:, at] = jnp.dot(place, tg[b], preferred_element_type=f32).astype(bf16).reshape(shape)
+
+    @pl.when(e == 0)
+    def _():
+        def loads(j):
+            at = p.block(back, j // 4, (j // 2) % 2, j % 2)
+            b = j % 2
+            return (
+                pltpu.make_async_copy(x_all.at[at], tx.at[b], load_sem.at[b]),
+                pltpu.make_async_copy(g_ref.at[at], tg.at[b], load_sem.at[2 + b]),
+            )
+
+        def arrive(j):
+            if j % 2:
+                for k in range(4):
+                    pl.when(chunk == k)(gather.to_core[k][j // 2].wait_recv)
+
+        arrive(0)
+        for copy in loads(0):
+            copy.start()
+        for j in range(8):
+            if j < 7:
+                arrive(j + 1)
+                for copy in loads(j + 1):
+                    copy.start()
+            for copy in loads(j):
+                copy.wait()
+            place_rows(j)
+        for k in range(experts):
+            save(k, 0).start()
+            save(k, 1).start()
+
+    rows_x, rows_g = xs[e], gs[e]
+    gain = gates[e][:, :1]
+    gate = jnp.dot(rows_x, w_ref[0, 0], preferred_element_type=f32)
+    up = jnp.dot(rows_x, w_ref[0, 1], preferred_element_type=f32)
+    raw = jnp.dot(rows_g, w_ref[0, 2], preferred_element_type=f32)
     sigma = 1.0 / (1.0 + jnp.exp(-gate))
     silu = gate * sigma
     act = (silu * up).astype(bf16).astype(f32)
-    gg_ref[0] = jnp.broadcast_to(jnp.sum(raw * act, axis=-1, keepdims=True), gg_ref.shape[1:])
+    grads[e] = jnp.broadcast_to(jnp.sum(raw * act, axis=-1, keepdims=True), (slots, 128))
     act_gated = (act * gain).astype(bf16)
     act_grad = raw * gain
     gate_low = (act_grad * up * sigma * (1.0 + gate * (1.0 - sigma))).astype(bf16)
     up_low = (act_grad * silu).astype(bf16)
-    y_ref[0] = dot(act_gated, w_ref[0, 2], ((1,), (1,))).astype(bf16)
+    st_ref[0, 0, 0] = act_gated
+    st_ref[0, 0, 1] = gate_low
+    st_ref[0, 0, 2] = up_low
+    save(e, 0).wait()
+    save(e, 1).wait()
     z = dot(gate_low, w_ref[0, 0], ((1,), (1,))) + dot(up_low, w_ref[0, 1], ((1,), (1,)))
-    z_ref[0] = z.astype(bf16)
-    first = pl.program_id(1) == 0
-    for n, (left, right) in enumerate(((x, gate_low), (x, up_low), (g, act_gated))):
-        term = dot(left, right, ((0,), (0,)))
-
-        @pl.when(first)
+    xs[e] = z.astype(bf16)
+    gs[e] = dot(act_gated, w_ref[0, 2], ((1,), (1,))).astype(bf16)
+
+    for k in range(3):
+        at_step(k + 1, last, (scatter.settle_core, k), *([(scatter.settle, k - 1)] if k else []))
+
+    @pl.when(e == last)
+    def _():
+        @pl.when(chunk > 0)
         def _():
-            wg_ref[0, n] = term
-
-        @pl.when(jnp.logical_not(first))
-        def _():
-            wg_ref[0, n] += term
-
-
-def experts_all(w_expert, xs, gs, gates, tile=512):
-    experts, slots, width = xs.shape
-    hidden = w_expert.shape[-1]
-    row = pl.BlockSpec((1, tile, width), lambda e, t: (e, t, 0))
-    thin = pl.BlockSpec((1, tile, 128), lambda e, t: (e, t, 0))
-    weight = pl.BlockSpec((1, 3, width, hidden), lambda e, t: (e, 0, 0, 0))
+            pl.semaphore_wait(scatter.free.at[0], 1)
+
+        for pos in (3, 1, 2, 0):
+            for c in (1, 0):
+                j = pos * 2 + c
+                hot = slots_of_rows(ranks[j])
+                place = one_hot(hot)
+                at = pl.ds(j * CAP, CAP)
+                for i, values in enumerate((xs, gs)):
+                    flat = values[:, at].reshape(experts * CAP, width)
+                    total = dot(place, flat, ((0,), (0,))).astype(bf16)
+                    if c:
+                        scatter.give[i, pos] = total
+                        scatter.to_core(chunk, i, pos).start()
+                    elif pos:
+                        scatter.stage[lax.rem(chunk, 2), i, pos - 1] = total
+                    else:
+                        scatter.acc[chunk, i] = total
+                zz = lax.rem(p.z + 4 - back, 4)
+                yy, xx, cc = lax.rem(p.y + pos // 2, 2), lax.rem(p.x + pos % 2, 2), lax.rem(p.c + c, 2)
+                probs.own[cc, xx, yy, zz] = jnp.sum(jnp.where(hot, grads[:, at, :1], 0.0), axis=1)
+
+    @pl.when((chunk == 3) & (e == last))
+    def _():
+        probs.start()
+        scatter.line(2, 1)
+        scatter.diagonal(3, 0)
+        scatter.diagonal(3, 1)
+        probs.over_x()
+        scatter.across(3, 0)
+        scatter.across(3, 1)
+        probs.over_seq()
+        gather.finish()
+        scatter.line(3, 0)
+        scatter.finish(0, grad_out)
+        probs.finish(probs_out)
+        scatter.line(3, 1)
+        scatter.finish(1, sum_out)
+        scatter.end()
+
+
+def mixture_all(routes_all, router_rows, x, g_all, w_expert, collective_id):
+    experts, _, width, hidden = w_expert.shape
+    rows = x.shape[0]
+    slots = 8 * CAP
+    struct = jax.ShapeDtypeStruct
+    V, S = pltpu.VMEM, pltpu.SemaphoreType.DMA
+    slot = struct((4, experts, slots, width), bf16)
+    whole = pl.BlockSpec((rows, width), lambda k, e: (0, 0))
+    outs = pl.pallas_call(
+        mixture_kernel,
+        name="mixture",
+        grid=(4, experts),
+        out_shape=(
+            struct((32, rows, width), bf16),
+            slot,
+            slot,
+            struct((4, experts, 3, slots, hidden), bf16),
+            struct((rows, width), f32),
+            struct((rows, width), f32),
+            struct((4, 2, experts, rows), f32),
+        ),
+        in_specs=[
+            pl.BlockSpec(routes_all.shape, lambda k, e: (0, 0, 0)),
+            pl.BlockSpec(router_rows.shape, lambda k, e: (0, 0)),
+            ANY,
+            ANY,
+            pl.BlockSpec((1, 3, width, hidden), lambda k, e: (e, 0, 0, 0)),
+        ],
+        out_specs=(
+            ANY,
+            ANY,
+            ANY,
+            pl.BlockSpec((1, 1, 3, slots, hidden), lambda k, e: (k, e, 0, 0, 0)),
+            whole,
+            whole,
+            pl.BlockSpec((4, 2, experts, rows), lambda k, e: (0, 0, 0, 0)),
+        ),
+        scratch_shapes=[
+            V((2, rows, width), bf16), V((2, rows, width), bf16),
+            V((experts, slots, width), bf16), V((experts, slots, width), bf16),
+            V((experts, slots, 128), f32), V((experts, slots, 128), f32),
+            V((8, experts, rows), jnp.int32), V((router_rows.shape[0], rows), f32),
+            S((4,)), S((2, experts)),
+            *Gather.scratch(), *Scatter.scratch(rows, width), *Probs.scratch((experts, rows)),
+        ],
+        compiler_params=pltpu.CompilerParams(
+            collective_id=collective_id, has_side_effects=True, vmem_limit_bytes=62 << 20,
+            dimension_semantics=("arbitrary", "arbitrary"),
+        ),
+    )(routes_all, router_rows, x, g_all, w_expert)
+    return outs[1:]
+
+
+def weights_kernel(xs_ref, gs_ref, st_ref, wg_ref):
+    rows = xs_ref.shape[0] * xs_ref.shape[2]
+    width = xs_ref.shape[-1]
+    x = xs_ref[...].reshape(rows, width)
+    g = gs_ref[...].reshape(rows, width)
+    act, gate_low, up_low = (st_ref[:, 0, i].reshape(rows, -1) for i in range(3))
+    hidden = act.shape[-1]
+    both = dot(x, jnp.concatenate([gate_low, up_low], axis=1), ((0,), (0,)))
+    wg_ref[0, 0] = both[:, :hidden]
+    wg_ref[0, 1] = both[:, hidden:]
+    wg_ref[0, 2] = dot(g, act, ((0,), (0,)))
+
+
+def weights_all(xs, gs, st):
+    chunks, experts, slots, width = xs.shape
+    hidden = st.shape[-1]
+    row = pl.BlockSpec((chunks, 1, slots, width), lambda e: (0, e, 0, 0))
     return pl.pallas_call(
-        experts_kernel,
-        name="experts",
-        grid=(experts, slots // tile),
-        out_shape=(
-            jax.ShapeDtypeStruct(xs.shape, bf16),
-            jax.ShapeDtypeStruct(xs.shape, bf16),
-            jax.ShapeDtypeStruct(w_expert.shape, f32),
-            jax.ShapeDtypeStruct((experts, slots, 128), f32),
-        ),
-        in_specs=[weight, row, row, thin],
-        out_specs=(row, row, weight, thin),
+        weights_kernel,
+        name="weights",
+        grid=(experts,),
+        out_shape=jax.ShapeDtypeStruct((experts, 3, width, hidden), f32),
+        in_specs=[row, row, pl.BlockSpec((chunks, 1, 3, slots, hidden), lambda e: (0, e, 0, 0, 0))],
+        out_specs=pl.BlockSpec((1, 3, width, hidden), lambda e: (e, 0, 0, 0)),
         compiler_params=pltpu.CompilerParams(vmem_limit_bytes=60 << 20),
-    )(w_expert, xs, gs, gates)
-
-
-def combine_kernel(rank_ref, y_ref, z_ref, gg_ref, my_ref, mz_ref, pg_ref):
-    hot = slots_of_rows(rank_ref[0])
-    place = one_hot(hot)
-    flat = (place.shape[0], y_ref.shape[-1])
-    my_ref[0] = dot(place, y_ref[...].reshape(flat), ((0,), (0,))).astype(bf16)
-    mz_ref[0] = dot(place, z_ref[...].reshape(flat), ((0,), (0,))).astype(bf16)
-    pg_ref[0] = jnp.sum(jnp.where(hot, gg_ref[:, :, :1], 0.0), axis=1)
-
-
-def combine(ranks, y, z, gate_grads):
-    groups, experts, rows = ranks.shape
-    width = y.shape[-1]
-    part = pl.BlockSpec((experts, CAP, width), lambda d: (0, d, 0))
-    whole = pl.BlockSpec((1, rows, width), lambda d: (d, 0, 0))
-    thin = pl.BlockSpec((1, experts, rows), lambda d: (d, 0, 0))
-    return pl.pallas_call(
-        combine_kernel,
-        name="combine",
-        grid=(groups,),
-        out_shape=(
-            jax.ShapeDtypeStruct((groups, rows, width), bf16),
-            jax.ShapeDtypeStruct((groups, rows, width), bf16),
-            jax.ShapeDtypeStruct((groups, experts, rows), f32),
-        ),
-        in_specs=[thin, part, part, pl.BlockSpec((experts, CAP, 128), lambda d: (0, d, 0))],
-        out_specs=(whole, whole, thin),
-        compiler_params=pltpu.CompilerParams(vmem_limit_bytes=40 << 20),
-    )(ranks, y, z, gate_grads)
+    )(xs, gs, st)
 
 
 class HeadsAttention:
@@ -938,19 +1133,12 @@
 
 
 def experts_by_tokens(ffn_in, cotangent_all, routes_all, w_expert, router_all):
-    experts = w_expert.shape[0]
     rows, width = ffn_in.shape
-    first = (lax.axis_index("seq") * experts).astype(jnp.int32).reshape(1)
-    ffn_all = gather_all(ffn_in, 6)
-    xs, gs, gates, ranks = dispatch(
-        first, routes_all, ffn_all, cotangent_all.reshape(32, rows, width), router_all.T, experts
+    xs, gs, factors, ffn_in_grad, mixture, probs = mixture_all(
+        routes_all, router_all.T, ffn_in, cotangent_all.reshape(32, rows, width), w_expert, 6
     )
-    y, z, expert_grad, gate_grads = experts_all(w_expert, xs, gs, gates)
-    mixture, ffn_in_grad, probs = combine(ranks, y, z, gate_grads)
-    prob_grad = scatter_probs(jnp.transpose(probs.reshape(4, 2, 2, 2, experts, rows), (3, 2, 1, 0, 4, 5)), 7).T
-    ffn_in_grad = scatter_all(ffn_in_grad, 8, f32)
-    mixture = scatter_all(mixture, 9, f32)
-    return mixture, ffn_in_grad, prob_grad, expert_grad
+    prob_grad = probs.reshape(-1, rows).T
+    return mixture, ffn_in_grad, prob_grad, weights_all(xs, gs, factors)
 
 
 class TokensAttention:

time: 955 us -> 776 us (0.81)
  Pallas kernels: 838 us -> 660 us
    pallas_call x7 -> x2, Pallas kernels: 500 us -> 319 us  [the longest x1 268 us: mixture_all(): pl.pallas_call(mixture_kernel, name='mixture', grid=(4, experts), out_sha...]
  transfers between devices with their start and end apart: 1 -> 1, of which waited for: 0 -> 0; matrix products, arithmetic and copies ran while one was open for 3% -> 4% of each run, Pallas kernels for 30% -> 25%
where the time goes in v3:
time: 776 us; the launch traced here: 768 us
  Pallas kernels  660 us (85%)
  local copies, waits for them, and re-layouts  36.7 us (5%)
  matrix products  35.6 us (5%)
  other arithmetic  20.1 us (3%)
  between operations  15.1 us (2%)
    pallas_call x1, Pallas kernels, mixture_all(): pl.pallas_call(mixture_kernel, name='mixture', grid=(4, experts), out_sha...  268 us
    pallas_call x1, Pallas kernels, gather_first(): call(gather_first_kernel, 'gather_first', collective_id, (struct((8,) + h...  132 us
    pallas_call x1, Pallas kernels, scatter_last(): call(scatter_last_kernel, 'scatter_last', collective_id, (struct(nb, f32)...  78.3 us
    pallas_call x1, Pallas kernels, gather_seq(): call(gather_seq_kernel, 'gather_seq', collective_id, jax.ShapeDtypeStruct...  63.5 us
    pallas_call x1, Pallas kernels, weights_all(): pl.pallas_call(weights_kernel, name='weights', grid=(experts,), out_shape...  50.2 us
    pallas_call x1, Pallas kernels, scatter_seq(): call(scatter_seq_kernel, 'scatter_seq', collective_id, jax.ShapeDtypeStru...  46.4 us
    pallas_call x2, Pallas kernels, sum_seq(): call(sum_seq_kernel, 'sum_seq', collective_id, jax.ShapeDtypeStruct(x.sha...  20.7 us
    dot_general x6, matrix products, dot(): return lax.dot_general(a, b, (dims, ((), ())), preferred_element_type=f32)  16.5 us
  transfers between devices with their start and end apart: 1, of which 0 were waited for; matrix products, arithmetic and copies ran while one was open for 4% of the time, Pallas kernels for 25%

profile of v3, /device:TPU:0, one launch (start us, length us, event | category | flops | bytes accessed | tf_op | source)
XLA Modules:
  0.0 767.8 jit_solution(16829340588500814181)
XLA Ops:
  7.3 0.7 all-gather.3.cloned.1.call-update
  8.0 1.3 copy.81
  9.3 0.4 copy.88
  9.7 0.9 reshape.349.wi_ref
  11.1 132.0 %gather_first.1 = (bf16[8,128,2048]{2,1,0:T(8,128)(2,1)S(1)}, bf16[8,4,64,768]{3,2,1,0:T(8,128)(2,1)S(1)}, bf16[4,64,2048]{2,1,0:T(8,128)(2,1)S(1)}, s32[32,16,128]{2,1,0:T(8,128)S(1)}, bf16[32,64,128]{2,1,0:T(8,128)(2,1)S(1)}) custom-call(bf16[128,2048]{1,0:T(8,128)(2,1)S(1)} %bitcast.154, bf16[8,64,768]{2,1,0:T(8,128)(2,1)S(1)} %reshape.349.wi_ref, ...), custom_call_target="tpu_custom_call" | custom-call | tf_op jit(solution)/shard_map/gather_first/pallas_call | solution.py:207
  143.1 1.3 slice_convert_fusion.1
  144.5 0.9 slice_reduce_fusion
  145.4 0.9 multiply_reduce_fusion.1
  146.3 1.0 multiply_convert_fusion.2
  147.4 3.6 fusion.59
  151.3 13.9 %sum_seq.2 = f32[2,8,128]{2,1,0:T(8,128)S(1)} custom-call(f32[2,8,128]{2,1,0:T(8,128)S(1)} %pad_maximum_fusion.4.x_ref), custom_call_target="tpu_custom_call" | custom-call | tf_op jit(solution)/shard_map/sum_seq/pallas_call | solution.py:325
  165.2 0.7 slice.96.routes_ref
  165.9 1.1 dynamic-slice_bitcast_fusion
  167.3 3.2 broadcast_multiply_fusion.3
  171.1 0.6 fusion.28
  171.7 0.6 fusion.8
  172.4 1.9 fusion.3
  174.3 2.0 fusion
  176.3 1.4 copy-done.19
  177.7 3.6 fusion.57
  181.3 1.3 convolution_convert_fusion
  182.6 46.4 %scatter_seq.1 = f32[128,2048]{1,0:T(8,128)S(1)} custom-call(bf16[8,128,2048]{2,1,0:T(8,128)(2,1)S(1)} %bitcast.153), custom_call_target="tpu_custom_call" | custom-call | tf_op jit(solution)/shard_map/scatter_seq/pallas_call | solution.py:294
  229.0 0.9 copy.80
  230.2 1.0 copy-done.12
  232.2 268.4 %mixture.1 = (bf16[32,128,2048]{2,1,0:T(8,128)(2,1)}, bf16[4,8,256,2048]{3,2,1,0:T(8,128)(2,1)}, bf16[4,8,256,2048]{3,2,1,0:T(8,128)(2,1)}, bf16[4,8,3,256,256]{...) custom-call(s32[32,8,128]{2,1,0:T(8,128)} %slice.96.routes_ref, ...), custom_call_target="tpu_custom_call" | custom-call | tf_op jit(solution)/shard_map/mixture/pallas_call | solution.py:924
  500.6 0.9 fusion.41
  501.5 0.8 fusion.43
  502.3 1.3 fusion.60
  503.6 2.1 multiply_reduce_fusion.2
  505.7 0.9 copy-done.18
  507.0 63.5 %gather_seq.1 = bf16[8,128,2048]{2,1,0:T(8,128)(2,1)S(1)} custom-call(bf16[128,2048]{1,0:T(8,128)(2,1)S(1)} %fusion.56.h_ref), custom_call_target="tpu_custom_call" | custom-call | tf_op jit(solution)/shard_map/gather_seq/pallas_call | solution.py:247
  570.6 1.3 convolution_convert_fusion.2
  572.1 1.3 multiply_reduce_fusion.5
  573.4 0.4 copy-done.24
  573.8 2.7 fusion.14
  576.5 3.3 multiply_convert_fusion.1
  579.8 1.5 convolution_bitcast_fusion
  581.3 0.9 broadcast_multiply_fusion.1
  582.4 0.9 copy-done.29
  583.3 0.5 maximum_subtract_fusion
  583.8 0.5 copy-done.17
  584.3 0.6 fusion.29
  584.9 6.8 sum_seq.3
  591.7 0.4 multiply_convert_fusion.4
  592.2 6.9 multiply_reduce_fusion
  599.1 3.8 convolution_convert_fusion.1
  602.8 1.9 copy.86
  604.8 0.8 concatenate.53
  605.6 1.7 copy.66
  607.4 1.4 copy.67
  609.0 1.4 copy.68
  610.4 1.6 broadcast_select_fusion
  612.0 1.1 broadcast_in_dim.97
  613.1 4.2 concatenate.56
  617.3 78.3 %scatter_last.1 = (f32[128,2048]{1,0:T(8,128)S(1)}, f32[8,64,768]{2,1,0:T(8,128)S(1)}, f32[64,2048]{1,0:T(8,128)S(1)}, f32[64,128]{1,0:T(8,128)S(1)}) custom-call(bf16[8,128,2048]{2,1,0:T(8,128)(2,1)} %bitcast.180, bf16[2,2,8,64,768]{4,3,2,1,0:T(8,128)(2,1)} %bitcast.170, bf16[2,2,64,2048]{3,2,1,0:T(8,128)(2,1)S(1)} %bitcast.160, ...), custom_call_target="tpu_custom_call" | custom-call | tf_op jit(solution)/shard_map/scatter_last/pallas_call | solution.py:438
  695.6 0.9 copy-done.3
  697.1 3.7 reshape.368
  700.8 2.7 copy.69
  703.4 1.6 copy.82
  705.1 0.7 copy.70
  705.8 3.3 fusion.23
  709.1 50.2 %weights.1 = f32[8,3,2048,256]{3,2,1,0:T(8,128)} custom-call(bf16[4,8,256,2048]{3,2,1,0:T(8,128)(2,1)} %get-tuple-element.34.xs_ref, bf16[4,8,256,2048]{3,2,1,0:T(8,128)(2,1)} %get-tuple-element.35.gs_ref, bf16[4,8,3,256,256]{4,3,2,1,0:T(8,128)(2,1)} %get-tuple-element.36.st_ref), custom_call_target="tpu_custom_call" | custom-call | tf_op jit(solution)/shard_map/weights/pallas_call | solution.py:986
  759.3 0.8 copy.91
  760.1 0.6 copy.92
  (123 shorter events, 4.8 us)
Async XLA Ops:
  7.2 3.5 copy-start.36
  7.2 3.7 copy-start.37
  7.2 3.7 copy-start.35
  7.2 3.8 copy-start.34
  7.2 3.9 copy-start.2
  7.2 3.9 copy-start.9
  7.2 224.6 %all-gather.3.cloned.1.call-start = ((), (), s32[]{:S(2)}) async-start(), calls=%async_computation | async-start | bytes 17301504 | tf_op jit(solution)/shard_map/all_gather | solution.py:1356
  143.1 3.2 copy-start.6
  143.1 3.2 copy-start
  143.1 4.2 copy-start.10
  150.9 14.2 %copy-start.15 = (f32[1024,768]{0,1:T(8,128)}, f32[1024,768]{0,1:T(8,128)S(1)}, u32[]{:S(2)}) copy-start(f32[1024,768]{0,1:T(8,128)S(1)} %fusion.59) | copy-start | bytes 9437188
  151.0 25.3 %copy-start.32 = (bf16[1024,256]{0,1:T(8,128)(2,1)}, bf16[1024,256]{0,1:T(8,128)(2,1)S(1)}, u32[]{:S(2)}) copy-start(bf16[1024,256]{0,1:T(8,128)(2,1)S(1)} %slice.169) | copy-start | bytes 1572868
  165.9 4.7 copy-start.16
  171.7 2.6 copy-start.25
  171.7 2.6 copy-start.27
  172.4 4.0 copy-start.23
  174.3 3.4 copy-start.19
  177.7 3.6 copy-start.7
  181.3 47.7 %copy-start.30 = (bf16[1024,2,128]{0,2,1:T(8,128)(2,1)}, bf16[1024,2,128]{0,2,1:T(8,128)(2,1)S(1)}, u32[]{:S(2)}) copy-start(bf16[1024,2,128]{0,2,1:T(8,128)(2,1)S(1)} %get-tuple-element.114) | copy-start | bytes 1572868
  230.2 1.0 copy-start.12
  231.3 0.8 copy-start.20
  500.6 6.0 copy-start.13
  500.6 6.0 copy-start.22
  505.6 1.0 copy-start.18
  505.7 64.9 %copy-start.31 = (bf16[1024,2,128]{0,2,1:T(8,128)(2,1)S(1)}, bf16[1024,2,128]{0,2,1:T(8,128)(2,1)}, u32[]{:S(2)}) copy-start(bf16[1024,2,128]{0,2,1:T(8,128)(2,1)} %copy-done.30) | copy-start | bytes 1572868
  507.0 66.4 %slice-start = ((s8[8388608]{0:T(1024)(128)(4,1)}), s8[4194304]{0:T(1024)(128)(4,1)S(1)}, s32[]{:S(2)}) async-start(s8[8388608]{0:T(1024)(128)(4,1)} %bitcast.176), calls=%async_computation.1 | async-start | bytes 8388608
  570.5 1.3 copy-start.8
  570.5 1.5 copy-start.38
  570.5 2.8 slice-start.1
  571.8 2.0 copy-start.24
  573.8 2.7 copy-start.33
  576.5 3.3 copy-start.28
  579.8 1.6 copy-start.21
  579.8 1.5 copy-start.26
  582.2 1.0 copy-start.29
  582.3 2.0 copy-start.17
  584.3 7.9 %copy-start.1 = (bf16[8,128,2048]{2,1,0:T(8,128)(2,1)S(1)}, bf16[8,128,2048]{2,1,0:T(8,128)(2,1)}, u32[]{:S(2)}) copy-start(bf16[8,128,2048]{2,1,0:T(8,128)(2,1)} %copy-done) | copy-start | bytes 12582916
  584.3 7.9 %copy-start.11 = (bf16[8,4,64,768]{3,2,1,0:T(8,128)(2,1)S(1)}, bf16[8,4,64,768]{3,2,1,0:T(8,128)(2,1)}, u32[]{:S(2)}) copy-start(bf16[8,4,64,768]{3,2,1,0:T(8,128)(2,1)} %copy-done.10) | copy-start | bytes 9437188
  695.6 1.0 copy-start.3
  695.6 1.5 copy-start.5
  700.8 5.0 copy-start.4
  700.8 5.0 copy-start.14
Sparse Core Ops, SparseCore 0:
  10.9 169.1 all-gather.2

commit v4 on v3

--- a/solution.py
+++ b/solution.py
@@ -217,43 +217,14 @@
         ),
         [ANY, ANY, ANY, WHOLE, WHOLE],
         (ANY, ANY, ANY, WHOLE, WHOLE),
-        [pltpu.VMEM((32,) + ints.shape, ints.dtype), pltpu.VMEM((32,) + small.shape, small.dtype)],
-        2 + 3 + 1 + 7 + 1 + 1 + 2 + 2 + 2 + 6 + 3 + 14 + 1 + 8,
+        [
+            pltpu.VMEM((32,) + ints.shape, ints.dtype),
+            pltpu.VMEM((32,) + small.shape, small.dtype),
+        ],
+        2 + 3 + 1 + 7 + 1 + 1 + 1 + 1 + 2 + 2 + 6 + 3 + 7 + 7 + 1 + 8,
         3,
     )(hidden, parts, w_out, ints, small)
     return outs
-
-
-def gather_seq_kernel(h_ref, h_out, send_sem, recv_sem, own_sem):
-    p = Place()
-    seq, b = p.at()
-    barrier([p.at(1), p.at(2), p.at(3), p.at(y=1)])
-    sends = Sends(send_sem, recv_sem)
-    own = pltpu.make_async_copy(h_ref, h_out.at[seq], own_sem.at[0])
-    own.start()
-    h_z = {r: sends.start(h_ref, h_out.at[seq], p.at(r)) for r in Z_ORDER}
-    h_y = [sends.start(h_ref, h_out.at[seq], p.at(y=1))]
-    for r in Z_ORDER:
-        h_z[r].wait_recv()
-        s = p.at(-r % 4)[0]
-        h_y.append(sends.start(h_out.at[s], h_out.at[s], p.at(y=1)))
-    for copy in h_y:
-        copy.wait_recv()
-    sends.finish()
-    own.wait()
-
-
-def gather_seq(x, collective_id):
-    return call(
-        gather_seq_kernel,
-        "gather_seq",
-        collective_id,
-        jax.ShapeDtypeStruct((8,) + x.shape, x.dtype),
-        [ANY],
-        ANY,
-        [],
-        7,
-    )(x)
 
 
 def scatter_seq_kernel(p_ref, out_ref, acc, ry, rz, send_sem, recv_sem, own_sem):
@@ -356,16 +327,17 @@
     core, nbr_x, nbr_y = p.at(c=1), p.at(x=1), p.at(y=1)
     order = (2, 1, 3, 0)
     loads = [
-        pltpu.make_async_copy(wi_ref.at[c], wi_acc, own_sem.at[4]),
-        pltpu.make_async_copy(wo_ref.at[c], wo_acc, own_sem.at[5]),
-        pltpu.make_async_copy(sm_ref.at[c], sm_acc, own_sem.at[6]),
+        pltpu.make_async_copy(wi_ref.at[:, 1 - x, c], wi_acc.at[0], own_sem.at[4]),
+        pltpu.make_async_copy(wi_ref.at[:, x, c], wi_acc.at[1], own_sem.at[7]),
+        pltpu.make_async_copy(wo_ref.at[:, c], wo_acc, own_sem.at[5]),
+        pltpu.make_async_copy(sm_ref.at[:, :, :, c], sm_acc, own_sem.at[6]),
     ]
     for load in loads:
         load.start()
-    wi1 = sends.start(wi_ref.at[1 - c, 1 - x], wi_c.at[0], core)
-    sm1 = sends.start(sm_ref.at[1 - c], sm_c, core)
-    wo1 = sends.start(wo_ref.at[1 - c], wo_c, core)
-    wi2 = sends.start(wi_ref.at[1 - c, x], wi_c.at[1], core)
+    wi1 = sends.start(wi_ref.at[:, 1 - x, 1 - c], wi_c.at[0], core)
+    sm1 = sends.start(sm_ref.at[:, :, :, 1 - c], sm_c, core)
+    wo1 = sends.start(wo_ref.at[:, 1 - c], wo_c, core)
+    wi2 = sends.start(wi_ref.at[:, x, 1 - c], wi_c.at[1], core)
     fy, n_loads, fz = [], [], []
     for n, r in enumerate(order):
         fy.append(sends.start(n_ref.at[p.at(r, 1)[0]], n_y.at[n], nbr_y))
@@ -375,16 +347,16 @@
     for load in loads:
         load.wait()
     wi1.wait_recv()
-    add_blocks(wi_acc.at[1 - x], wi_c.at[0])
-    wi3 = sends.start(wi_acc.at[1 - x], wi_x, nbr_x)
+    add_blocks(wi_acc.at[0], wi_c.at[0])
+    wi3 = sends.start(wi_acc.at[0], wi_x, nbr_x)
     sm1.wait_recv()
     sm_acc[...] = sm_acc[...] + sm_c[...]
-    sm2 = sends.start(sm_acc.at[1 - x], sm_x, nbr_x)
+    sm2 = sends.start(sm_acc.at[:, :, 1 - x], sm_x, nbr_x)
     wo1.wait_recv()
     add_blocks(wo_acc, wo_c)
     wo2 = sends.start(wo_acc.at[1 - x], wo_x, nbr_x)
     wi2.wait_recv()
-    add_blocks(wi_acc.at[x], wi_c.at[1])
+    add_blocks(wi_acc.at[1], wi_c.at[1])
     rows = n_acc.shape[1]
     for n, r in enumerate(order):
         n_loads[n].wait()
@@ -393,29 +365,34 @@
         if r:
             fz.append(sends.start(n_acc.at[n], n_z.at[n], p.at(r)))
     wi3.wait_recv()
-    add_blocks(wi_acc.at[x], wi_x)
+    add_blocks(wi_acc.at[1], wi_x)
     me = p.at()[0]
     wi4 = []
     for r, yy in ((0, 1), (1, 0), (3, 0), (2, 0), (1, 1), (3, 1), (2, 1)):
         to = p.at(r, yy)
-        wi4.append(sends.start(wi_acc.at[x, to[0]], wi_got.at[me], to))
+        wi4.append(sends.start(wi_acc.at[1, to[0]], wi_got.at[me], to))
     sm2.wait_recv()
-    sm_acc[x] = sm_acc[x] + sm_x[...]
-    sm3 = sends.start(sm_acc.at[x, 1 - y], sm_y, nbr_y)
-    wi_got[me] = wi_acc[x, me]
+    sm_acc[:, :, x] = sm_acc[:, :, x] + sm_x[...]
+    sm3 = sends.start(sm_acc.at[:, 1 - y, x], sm_y, nbr_y)
+    wi_got[me] = wi_acc[1, me]
     wo2.wait_recv()
     wo_out[...] = wo_acc[x].astype(f32) + wo_x[...].astype(f32)
     sm3.wait_recv()
-    sm_acc[x, y] = sm_acc[x, y] + sm_y[...]
+    sm_acc[:, y, x] = sm_acc[:, y, x] + sm_y[...]
     sm4 = [
-        sends.start(sm_acc.at[x, y, lax.rem(z + r, 4)], sm_z.at[n], p.at(r)) for n, r in enumerate(Z_ORDER)
+        sends.start(sm_acc.at[lax.rem(z + r, 4), y, x], sm_z.at[n], p.at(r)) for n, r in enumerate(Z_ORDER)
     ]
     for copy in wi4:
         copy.wait_recv()
-    wi_out[...] = wi_got[...].astype(f32)
+    seq, _, columns = wi_got.shape
+    part = columns // 3
+    for s in range(seq):
+        for i in range(3):
+            value = wi_got[s, :, i * part : (i + 1) * part].astype(f32)
+            wi_out[:, (i * seq + s) * part : (i * seq + s + 1) * part] = value
     for copy in sm4:
         copy.wait_recv()
-    sm_out[...] = sm_acc[x, y, z] + sm_z[0] + sm_z[1] + sm_z[2]
+    sm_out[...] = sm_acc[z, y, x] + sm_z[0] + sm_z[1] + sm_z[2]
     for copy in fz:
         copy.wait_recv()
 
@@ -433,23 +410,24 @@
 
 def scatter_last(normed, w_in, w_out, small, collective_id):
     struct = jax.ShapeDtypeStruct
-    nb, ib, ob, sb = normed.shape[1:], w_in.shape[2:], w_out.shape[2:], small.shape[4:]
+    nb, ib, ob, sb = normed.shape[1:], w_in.shape[3:], w_out.shape[2:], small.shape[4:]
     V = pltpu.VMEM
+    seq = w_in.shape[0]
     return call(
         scatter_last_kernel,
         "scatter_last",
         collective_id,
-        (struct(nb, f32), struct(ib, f32), struct(ob, f32), struct(sb, f32)),
+        (struct(nb, f32), struct((ib[0], seq * ib[1]), f32), struct(ob, f32), struct(sb, f32)),
         [ANY] * 4,
         (WHOLE,) * 4,
         [
             V((4,) + nb, bf16), V((4,) + nb, bf16), V((3,) + nb, bf16),
-            V((2,) + ib, bf16), V((2,) + ib, bf16), V(ib, bf16), V(ib, bf16),
+            V((2, seq) + ib, bf16), V((2, seq) + ib, bf16), V((seq,) + ib, bf16), V((seq,) + ib, bf16),
             V((2,) + ob, bf16), V((2,) + ob, bf16), V(ob, bf16),
-            V((2, 2, 4) + sb, f32), V((2, 2, 4) + sb, f32), V((2, 4) + sb, f32), V((4,) + sb, f32), V((3,) + sb, f32),
+            V((4, 2, 2) + sb, f32), V((4, 2, 2) + sb, f32), V((4, 2) + sb, f32), V((4,) + sb, f32), V((3,) + sb, f32),
         ],
         4 + 4 + 3 + 1 + 1 + 1 + 7 + 1 + 3,
-        7,
+        8,
         48,
     )(normed, w_in, w_out, small)
 
@@ -521,13 +499,14 @@
 
     def start(self):
         self.own.start()
-        for copy in self.along:
-            copy.start()
+        self.along[0].start()
         self.own.wait()
 
     def spread(self, k):
         if BACK[k]:
             self.along[k].wait_recv()
+            if k < 2:
+                self.along[k + 1].start()
         self.to_x[k].start()
         self.to_y[k].start()
         self.to_core[k][0].start()
@@ -760,16 +739,13 @@
         gather.start()
         gather.spread(3)
         gather.spread(0)
-        gather.spread(1)
-        gather.cross(0)
-        gather.spread(2)
-        gather.close(0)
 
     at_step(0, 0, (begin,))
-    at_step(0, 1, (gather.cross, 1))
-    at_step(0, 4, (gather.close, 1), (gather.cross, 2))
-    at_step(0, 6, (gather.close, 2), (gather.cross, 3))
-    at_step(1, 1, (gather.close, 3))
+    at_step(0, 1, (gather.cross, 1), (gather.cross, 3))
+    at_step(0, 3, (gather.spread, 2))
+    at_step(0, 4, (gather.close, 1))
+    at_step(0, 7, (gather.close, 3), (gather.cross, 2))
+    at_step(1, 1, (gather.close, 2))
     for k in range(3):
         before = [(scatter.line, k - 1, 1)] if k else []
         at_step(k + 1, 0, *before, (scatter.diagonal, k, 0), (scatter.diagonal, k, 1))
@@ -827,18 +803,29 @@
             if j % 2:
                 for k in range(4):
                     pl.when(chunk == k)(gather.to_core[k][j // 2].wait_recv)
-
-        arrive(0)
-        for copy in loads(0):
-            copy.start()
+            elif j == 2:
+                pl.when(chunk == 0)(functools.partial(gather.cross, 0))
+            elif j == 6:
+
+                @pl.when(chunk == 0)
+                def _():
+                    gather.close(0)
+                    gather.spread(1)
+
+        def fetch(j):
+            arrive(j)
+            for copy in loads(j):
+                copy.start()
+
+        fetch(0)
         for j in range(8):
             if j < 7:
-                arrive(j + 1)
-                for copy in loads(j + 1):
-                    copy.start()
+                pl.when(chunk > 0)(functools.partial(fetch, j + 1))
             for copy in loads(j):
                 copy.wait()
             place_rows(j)
+            if j < 7:
+                pl.when(chunk == 0)(functools.partial(fetch, j + 1))
         for k in range(experts):
             save(k, 0).start()
             save(k, 1).start()
@@ -991,6 +978,10 @@
         in_specs=[row, row, pl.BlockSpec((chunks, 1, 3, slots, hidden), lambda e: (0, e, 0, 0, 0))],
         out_specs=pl.BlockSpec((1, 3, width, hidden), lambda e: (e, 0, 0, 0)),
         compiler_params=pltpu.CompilerParams(vmem_limit_bytes=60 << 20),
+        cost_estimate=pl.CostEstimate(
+            flops=6 * xs.size * hidden, bytes_accessed=4 * xs.size + 2 * st.size + 12 * experts * width * hidden,
+            transcendentals=0,
+        ),
     )(xs, gs, st)
 
 
@@ -1075,7 +1066,7 @@
         length, cols, width = self.length, self.cols, self.width
         scale = self.hs ** (-0.5)
         shape = (length, self.hl, self.hs)
-        grad_all = gather_seq(middle_low, 3).reshape(length, width)
+        grad_all = lax.all_gather(middle_low, "seq", axis=0, tiled=True)
         out_grad = dot(self.attn_low, grad_all, ((0,), (0,))).astype(bf16)
         attn_grad = dot(grad_all, self.w_rows, ((1,), (1,))).astype(bf16).reshape(shape)
         delta = jnp.sum(attn_grad.astype(f32) * self.attended, axis=-1)
@@ -1109,26 +1100,20 @@
         in_grad = dot(self.normed, projected_grad, ((0,), (0,))).astype(bf16)
         own = width // (seq * batch)
 
-        def by_batch(value, *shape):
-            return jnp.swapaxes(value.reshape(2, 2, *shape), 0, 1)
-
-        in_grad = jnp.transpose(in_grad.reshape(seq, 2, 2, own, 3 * cols), (2, 1, 0, 3, 4))
-        out_grad = by_batch(out_grad, own, width)
+        lane = jnp.arange(router_grad.shape[1])
         mine = jnp.arange(seq)[:, None] == lax.axis_index("seq")
-
-        def own_columns(value):
-            return jnp.where(mine, value[None], 0.0).reshape(width)
-
-        gains_grad = jnp.stack(
-            [attn_gain_grad, own_columns(query_gain_grad), own_columns(key_gain_grad), ffn_gain_grad], axis=1
+        total = self.router_all.shape[1]
+        small = router_grad.reshape(seq, cols, -1)
+        for n, value in enumerate((attn_gain_grad, query_gain_grad, key_gain_grad, ffn_gain_grad)):
+            value = jnp.where(mine, value[None], 0.0) if n in (1, 2) else value.reshape(seq, cols)
+            small = small + jnp.where(lane == total + n, value[:, :, None], 0.0)
+        normed_grad, in_shard, out_shard, small = scatter_last(
+            partial.astype(bf16).reshape(seq, self.rows, width),
+            in_grad.reshape(seq, 2, 2, own, 3 * cols),
+            out_grad.reshape(2, 2, own, width),
+            small.reshape(4, 2, 2, 2, own, -1),
+            5,
         )
-        total = router_grad.shape[1]
-        small = jnp.concatenate([router_grad, gains_grad, jnp.zeros((width, 128 - total - 4), f32)], axis=1)
-        small = jnp.transpose(small.reshape(4, 2, 2, 2, own, 128), (3, 2, 1, 0, 4, 5))
-        normed_grad, in_shard, out_shard, small = scatter_last(
-            partial.astype(bf16).reshape(seq, self.rows, width), in_grad, out_grad, small, 5
-        )
-        in_shard = jnp.transpose(in_shard.reshape(seq, own, 3, cols), (1, 2, 0, 3)).reshape(own, 3 * width)
         return normed_grad, in_shard, out_shard, small[:, :total], small[:, total : total + 4].T
 
 
@@ -1383,7 +1368,11 @@
     router = jax.nn.softmax(jnp.dot(ffn_in, router_all, preferred_element_type=f32), axis=-1)
     logit_grad = router * (prob_grad - jnp.sum(router * prob_grad, axis=-1, keepdims=True))
     logit_low = logit_grad.astype(bf16)
-    router_grad = dot(ffn_in, logit_low, ((0,), (0,)))
+    if by_heads:
+        wide = jnp.pad(logit_low, ((0, 0), (0, 128 - total_experts)))
+        router_grad = dot(ffn_in, wide, ((0,), (0,)))
+    else:
+        router_grad = dot(ffn_in, logit_low, ((0,), (0,)))
     ffn_in_grad = ffn_in_grad + dot(logit_low, router_all, ((1,), (1,)))
     ffn_gain_grad = jnp.sum(ffn_in_grad * second_normal, axis=0)
     middle_grad = grad_out + norm_back(ffn_in_grad, second_normal, second_scale, gains_all[3])

time: 776 us -> 718 us (0.925)
  Pallas kernels: 660 us -> 591 us
  waiting for transfers between devices: 0.7 us -> 22.5 us
  local copies, waits for them, and re-layouts: 36.7 us -> 16.6 us
  matrix products: 35.6 us -> 44 us
    pallas_call x1 -> x0, Pallas kernels: 63.5 us -> none  [gather_seq(): call(gather_seq_kernel, 'gather_seq', collective_id, jax.ShapeDtypeStruct...]
    all_gather x0 -> x1, waiting for transfers between devices: none -> 21.8 us  [back(): grad_all = lax.all_gather(middle_low, 'seq', axis=0, tiled=True)]
    concatenate x7 -> x0, local copies, waits for them, and re-layouts: 9.54 us -> none  [back(): jnp.concatenate([router_grad, gains_grad, jnp.zeros((width, 128 - total -...]
  transfers between devices with their start and end apart: 1 -> 2, of which waited for: 0 -> 1; matrix products, arithmetic and copies ran while one was open for 4% -> 4% of each run, Pallas kernels for 25% -> 34%
where the time goes in v4:
time: 718 us; the launch traced here: 710 us
  Pallas kernels  591 us (82%)
  matrix products  44 us (6%)
  waiting for transfers between devices  22.5 us (3%)
  other arithmetic  20.7 us (3%)
  local copies, waits for them, and re-layouts  16.6 us (2%)
  between operations  15.1 us (2%)
    pallas_call x1, Pallas kernels, mixture_all(): pl.pallas_call(mixture_kernel, name='mixture', grid=(4, experts), out_sha...  263 us
    pallas_call x1, Pallas kernels, gather_first(): call(gather_first_kernel, 'gather_first', collective_id, (struct((8,) + h...  132 us
    pallas_call x1, Pallas kernels, scatter_last(): call(scatter_last_kernel, 'scatter_last', collective_id, (struct(nb, f32)...  78.9 us
    pallas_call x1, Pallas kernels, weights_all(): pl.pallas_call(weights_kernel, name='weights', grid=(experts,), out_shape...  50.2 us
    pallas_call x1, Pallas kernels, scatter_seq(): call(scatter_seq_kernel, 'scatter_seq', collective_id, jax.ShapeDtypeStru...  46.2 us
    all_gather x1, waiting for transfers between devices, back(): grad_all = lax.all_gather(middle_low, 'seq', axis=0, tiled=True)  21.8 us
    dot_general x6, matrix products, dot(): return lax.dot_general(a, b, (dims, ((), ())), preferred_element_type=f32)  21.4 us
    pallas_call x2, Pallas kernels, sum_seq(): call(sum_seq_kernel, 'sum_seq', collective_id, jax.ShapeDtypeStruct(x.sha...  20.7 us
  transfers between devices with their start and end apart: 2, of which 1 were waited for; matrix products, arithmetic and copies ran while one was open for 4% of the time, Pallas kernels for 34%

profile of v4, /device:TPU:0, one launch (start us, length us, event | category | flops | bytes accessed | tf_op | source)
XLA Modules:
  0.0 709.6 jit_solution(7052268878197311564)
XLA Ops:
  7.3 0.7 all-gather.6.cloned.1.call-update
  8.0 1.3 copy.65
  9.3 0.4 copy.67
  9.7 0.9 reshape.358.wi_ref
  11.1 132.0 %gather_first.1 = (bf16[8,128,2048]{2,1,0:T(8,128)(2,1)S(1)}, bf16[8,4,64,768]{3,2,1,0:T(8,128)(2,1)S(1)}, bf16[4,64,2048]{2,1,0:T(8,128)(2,1)S(1)}, s32[32,16,128]{2,1,0:T(8,128)S(1)}, bf16[32,64,128]{2,1,0:T(8,128)(2,1)S(1)}) custom-call(bf16[128,2048]{1,0:T(8,128)(2,1)S(1)} %bitcast.140, bf16[8,64,768]{2,1,0:T(8,128)(2,1)S(1)} %reshape.358.wi_ref, ...), custom_call_target="tpu_custom_call" | custom-call | tf_op jit(solution)/shard_map/gather_first/pallas_call | solution.py:207
  143.2 1.3 slice_convert_fusion.1
  144.5 0.9 slice_reduce_fusion
  145.4 0.9 multiply_reduce_fusion.1
  146.4 1.0 multiply_convert_fusion.2
  147.4 3.6 fusion.62
  151.1 0.2 multiply_reduce_fusion.9
  151.3 13.9 %sum_seq.2 = f32[2,8,128]{2,1,0:T(8,128)S(1)} custom-call(f32[2,8,128]{2,1,0:T(8,128)S(1)} %pad_maximum_fusion.4.x_ref), custom_call_target="tpu_custom_call" | custom-call | tf_op jit(solution)/shard_map/sum_seq/pallas_call | solution.py:296
  165.2 0.7 slice.96.routes_ref
  165.9 1.1 dynamic-slice_bitcast_fusion
  167.0 0.3 slice_reduce_fusion.2
  167.4 3.1 broadcast_multiply_fusion.3
  170.5 0.2 fusion.35
  170.8 0.3 slice_negate_fusion.2
  171.1 0.6 fusion.28
  171.7 0.6 fusion.8
  172.3 1.9 fusion.3
  174.3 2.0 fusion
  176.3 1.2 copy-done.18
  177.5 3.6 fusion.60
  181.1 1.3 convolution_convert_fusion
  182.4 46.2 %scatter_seq.1 = f32[128,2048]{1,0:T(8,128)S(1)} custom-call(bf16[8,128,2048]{2,1,0:T(8,128)(2,1)S(1)} %bitcast.139), custom_call_target="tpu_custom_call" | custom-call | tf_op jit(solution)/shard_map/scatter_seq/pallas_call | solution.py:265
  228.6 0.9 copy.64
  229.5 0.3 multiply_reduce_fusion.7
  229.8 1.0 copy-done.11
  230.8 0.2 multiply_convert_fusion.5.x_ref
  231.0 0.4 fusion.61
  231.4 0.4 copy-done.19
  231.8 262.5 %mixture.1 = (bf16[32,128,2048]{2,1,0:T(8,128)(2,1)}, bf16[4,8,256,2048]{3,2,1,0:T(8,128)(2,1)}, bf16[4,8,256,2048]{3,2,1,0:T(8,128)(2,1)}, bf16[4,8,3,256,256]{...) custom-call(s32[32,8,128]{2,1,0:T(8,128)} %slice.96.routes_ref, ...), custom_call_target="tpu_custom_call" | custom-call | tf_op jit(solution)/shard_map/mixture/pallas_call | solution.py:911
  494.3 0.9 fusion.41
  495.3 0.8 fusion.43
  496.0 2.1 multiply_reduce_fusion.2
  498.1 1.0 copy-done.17
  499.1 1.2 fusion.59
  500.4 0.3 fusion.44
  500.8 50.2 %weights.1 = f32[8,3,2048,256]{3,2,1,0:T(8,128)} custom-call(bf16[4,8,256,2048]{3,2,1,0:T(8,128)(2,1)} %get-tuple-element.34.xs_ref, bf16[4,8,256,2048]{3,2,1,0:T(8,128)(2,1)} %get-tuple-element.35.gs_ref, bf16[4,8,3,256,256]{4,3,2,1,0:T(8,128)(2,1)} %get-tuple-element.36.st_ref), custom_call_target="tpu_custom_call" | custom-call | flops 25769803776 | bytes 130023424 | tf_op jit(solution)/shard_map/weights/pallas_call | solution.py:973
  551.0 21.8 %all-gather.4.cloned.1.call-done = bf16[1024,2048]{1,0:T(8,128)(2,1)} async-done(((bf16[128,2048]{1,0:T(8,128)(2,1)}), bf16[1024,2048]{1,0:T(8,128)(2,1)}) %all-gather.4.cloned.1.call-update) | async-done | bytes 4194320 | tf_op jit(solution)/shard_map/all_gather | solution.py:1069
  572.7 3.9 multiply_reduce_fusion.5
  576.7 6.1 fusion.14
  582.9 3.4 multiply_convert_fusion.1
  586.3 1.5 convolution_bitcast_fusion
  587.9 0.9 broadcast_multiply_fusion.1
  588.9 0.9 copy-done.29
  589.8 0.5 maximum_subtract_fusion
  590.3 0.5 copy-done.16
  590.8 0.6 fusion.30
  591.4 6.8 sum_seq.3
  598.3 0.4 multiply_convert_fusion.4
  598.7 6.7 multiply_reduce_fusion
  605.5 4.9 convolution_convert_fusion.1
  610.7 1.2 select_add_fusion.sm_ref
  612.0 3.4 convolution_convert_fusion.2
  615.4 78.9 %scatter_last.1 = (f32[128,2048]{1,0:T(8,128)S(1)}, f32[64,6144]{1,0:T(8,128)S(1)}, f32[64,2048]{1,0:T(8,128)S(1)}, f32[64,128]{1,0:T(8,128)S(1)}) custom-call(bf16[8,128,2048]{2,1,0:T(8,128)(2,1)} %bitcast.161, bf16[8,2,2,64,768]{4,3,2,1,0:T(8,128)(2,1)} %bitcast.164, bf16[2,2,64,2048]{3,2,1,0:T(8,128)(2,1)S(1)} %bitcast.145, ...), custom_call_target="tpu_custom_call" | custom-call | tf_op jit(solution)/shard_map/scatter_last/pallas_call | solution.py:416
  694.4 1.1 copy-done.3
  695.5 0.3 fusion.19
  695.9 0.7 copy.54
  696.6 3.4 fusion.23
  700.0 1.1 copy.71
  701.1 0.8 copy.72
  701.9 0.6 copy.73
  (114 shorter events, 1.6 us)
Async XLA Ops:
  7.2 3.6 copy-start.36
  7.2 3.8 copy-start.37
  7.2 3.8 copy-start.35
  7.2 3.8 copy-start.34
  7.2 3.9 copy-start.2
  7.2 3.9 copy-start.8
  7.2 224.2 %all-gather.6.cloned.1.call-start = ((), (), s32[]{:S(2)}) async-start(), calls=%async_computation.1 | async-start | bytes 17301504 | tf_op jit(solution)/shard_map/all_gather | solution.py:1341
  8.0 564.8 %all-gather.4.cloned.1.call-start = ((), (), s32[]{:S(2)}) async-start(), calls=%async_computation | async-start | bytes 4718592 | tf_op jit(solution)/shard_map/all_gather | solution.py:1069
  143.2 3.2 copy-start.5
  143.2 3.2 copy-start
  143.2 4.2 copy-start.9
  151.0 14.2 %copy-start.14 = (f32[1024,768]{0,1:T(8,128)}, f32[1024,768]{0,1:T(8,128)S(1)}, u32[]{:S(2)}) copy-start(f32[1024,768]{0,1:T(8,128)S(1)} %fusion.62) | copy-start | bytes 9437188
  151.1 25.2 %copy-start.32 = (bf16[1024,256]{0,1:T(8,128)(2,1)}, bf16[1024,256]{0,1:T(8,128)(2,1)S(1)}, u32[]{:S(2)}) copy-start(bf16[1024,256]{0,1:T(8,128)(2,1)S(1)} %slice.169) | copy-start | bytes 1572868
  165.9 4.6 copy-start.15
  171.7 2.6 copy-start.25
  171.7 2.6 copy-start.27
  172.3 4.0 copy-start.23
  174.3 3.2 copy-start.18
  177.5 3.6 copy-start.6
  181.1 47.5 %copy-start.30 = (bf16[1024,2,128]{0,2,1:T(8,128)(2,1)}, bf16[1024,2,128]{0,2,1:T(8,128)(2,1)S(1)}, u32[]{:S(2)}) copy-start(bf16[1024,2,128]{0,2,1:T(8,128)(2,1)S(1)} %get-tuple-element.114) | copy-start | bytes 1572868
  229.8 1.0 copy-start.11
  231.0 0.8 copy-start.19
  494.3 4.8 copy-start.12
  494.3 4.8 copy-start.22
  494.3 6.1 copy-start.20
  498.1 1.0 copy-start.17
  500.8 72.0 %copy-start.7 = (bf16[4,64,2048]{2,1,0:T(8,128)(2,1)S(1)}, bf16[4,64,2048]{2,1,0:T(8,128)(2,1)}, u32[]{:S(2)}) copy-start(bf16[4,64,2048]{2,1,0:T(8,128)(2,1)} %copy-done.5) | copy-start | bytes 3145732
  572.7 4.0 copy-start.24
  572.7 10.1 %slice-start = ((s8[8388608]{0:T(1024)(128)(4,1)}), s8[4194304]{0:T(1024)(128)(4,1)S(1)}, s32[]{:S(2)}) async-start(s8[8388608]{0:T(1024)(128)(4,1)} %bitcast.157), calls=%async_computation.2 | async-start | bytes 8388608
  576.7 6.1 slice-start.1
  576.7 6.1 copy-start.33
  582.8 3.4 copy-start.28
  586.3 1.6 copy-start.21
  586.3 1.6 copy-start.26
  588.7 1.0 copy-start.29
  588.8 2.0 copy-start.16
  590.8 7.9 %copy-start.1 = (bf16[8,128,2048]{2,1,0:T(8,128)(2,1)S(1)}, bf16[8,128,2048]{2,1,0:T(8,128)(2,1)}, u32[]{:S(2)}) copy-start(bf16[8,128,2048]{2,1,0:T(8,128)(2,1)} %copy-done) | copy-start | bytes 12582916
  590.8 7.9 %copy-start.10 = (bf16[8,4,64,768]{3,2,1,0:T(8,128)(2,1)S(1)}, bf16[8,4,64,768]{3,2,1,0:T(8,128)(2,1)}, u32[]{:S(2)}) copy-start(bf16[8,4,64,768]{3,2,1,0:T(8,128)(2,1)} %copy-done.9) | copy-start | bytes 9437188
  605.5 6.5 copy-start.31
  615.4 81.2 %copy-start.13 = (f32[128,2048]{1,0:T(8,128)S(1)}, f32[128,2048]{1,0:T(8,128)}, u32[]{:S(2)}) copy-start(f32[128,2048]{1,0:T(8,128)} %copy-done.11) | copy-start | bytes 3145732
  694.4 1.1 copy-start.3
  696.6 3.4 copy-start.4
Sparse Core Ops, SparseCore 0:
  10.9 169.1 all-gather.5
  500.4 72.2 all-gather.3

commit v5 on v4

--- a/solution.py
+++ b/solution.py
@@ -443,7 +443,7 @@
     return jnp.where(hot, 1.0, 0.0).reshape(experts * CAP, rows).astype(bf16)
 
 
-BACK = (1, 3, 2, 0)
+BACK = (1, 2, 3, 0)
 
 
 class Flip(Place):
@@ -463,7 +463,7 @@
     @staticmethod
     def scratch():
         S = pltpu.SemaphoreType.DMA
-        return [S((35,)), S((35,)), S]
+        return [S((34,)), S((34,)), S]
 
     def __init__(self, p, x_ref, x_all, refs):
         send, recv, own_sem = refs
@@ -480,21 +480,23 @@
             count[0] += 1
             return remote(src, dst, send.at[i], recv.at[i], peer)
 
-        self.along, self.to_x, self.to_y, self.to_core, self.by_y, self.by_x = [], [], [], [], [], []
+        self.along, self.to_x, self.to_y, self.by_y, self.by_x, self.to_core = {}, {}, {}, {}, {}, []
         for k, r in enumerate(BACK):
             at, ix, iy, far = p.block(r), p.block(r, x=1), p.block(r, y=1), p.block(r, y=1, x=1)
-            src = x_all.at[at]
-            if r:
-                self.along.append(copy(x_ref, x_all.at[mine], p.at(r)))
+            src = x_all.at[at] if r else x_ref
+            if k < 2:
+                self.along[k] = copy(x_ref, x_all.at[mine], p.at(r))
+            if k == 2:
+                plane = [p.block(0, x=1), p.block(0, y=1), p.block(0, y=1, x=1)]
+                self.shift = [copy(x_ref, x_all.at[mine], p.at(r))]
+                self.shift += [copy(x_all.at[i], x_all.at[i], p.at(r)) for i in plane]
             else:
-                src = x_ref
-            self.to_x.append(copy(src, x_all.at[at], nx))
-            self.to_y.append(copy(src, x_all.at[at], ny))
-            self.by_y.append(copy(x_all.at[ix, A], x_all.at[ix, A], ny))
-            self.by_x.append(copy(x_all.at[iy, B], x_all.at[iy, B], nx))
+                self.to_x[k] = copy(src, x_all.at[at], nx)
+                self.to_y[k] = copy(src, x_all.at[at], ny)
+                self.by_y[k] = copy(x_all.at[ix, A], x_all.at[ix, A], ny)
+                self.by_x[k] = copy(x_all.at[iy, B], x_all.at[iy, B], nx)
             self.to_core.append(
-                [copy(src, x_all.at[at], core)]
-                + [copy(x_all.at[i], x_all.at[i], core) for i in (ix, iy, far)]
+                [copy(src, x_all.at[at], core)] + [copy(x_all.at[i], x_all.at[i], core) for i in (ix, iy, far)]
             )
 
     def start(self):
@@ -503,33 +505,54 @@
         self.own.wait()
 
     def spread(self, k):
-        if BACK[k]:
-            self.along[k].wait_recv()
-            if k < 2:
-                self.along[k + 1].start()
+        if k == 2:
+            self.shift[0].wait_recv()
+            self.to_core[k][0].start()
+            return
+        if k == 0:
+            self.along[0].wait_recv()
+            self.along[1].start()
+        elif k == 1:
+            self.along[1].wait_recv()
+            self.shift[0].start()
         self.to_x[k].start()
         self.to_y[k].start()
         self.to_core[k][0].start()
 
     def cross(self, k):
+        if k == 2:
+            for n in (1, 2):
+                self.shift[n].wait_recv()
+                self.to_core[k][n].start()
+            return
         self.to_x[k].wait_recv()
         self.by_y[k].start()
         self.to_core[k][1].start()
         self.to_y[k].wait_recv()
         self.by_x[k].start()
         self.to_core[k][2].start()
+        if k == 3:
+            self.shift[1].start()
+            self.shift[2].start()
 
     def close(self, k):
-        self.by_y[k].wait_recv()
-        self.by_x[k].wait_recv()
+        if k == 2:
+            self.shift[3].wait_recv()
+        else:
+            self.by_y[k].wait_recv()
+            self.by_x[k].wait_recv()
+            if k == 3:
+                self.shift[3].start()
         self.to_core[k][3].start()
 
     def finish(self):
-        for copy in self.along:
+        copies = list(self.shift)
+        for group in (self.along, self.to_x, self.to_y, self.by_y, self.by_x):
+            copies += group.values()
+        for group in self.to_core:
+            copies += group
+        for copy in copies:
             copy.wait_send()
-        for k in range(4):
-            for copy in [self.to_x[k], self.to_y[k], self.by_y[k], self.by_x[k]] + self.to_core[k]:
-                copy.wait_send()
 
 
 class Scatter:
@@ -741,17 +764,20 @@
         gather.spread(0)
 
     at_step(0, 0, (begin,))
-    at_step(0, 1, (gather.cross, 1), (gather.cross, 3))
-    at_step(0, 3, (gather.spread, 2))
-    at_step(0, 4, (gather.close, 1))
-    at_step(0, 7, (gather.close, 3), (gather.cross, 2))
-    at_step(1, 1, (gather.close, 2))
+    at_step(0, 1, (gather.cross, 3))
+    at_step(0, 3, (gather.cross, 1))
+    at_step(0, 4, (gather.close, 3))
+    at_step(0, 6, (gather.close, 1))
+    at_step(1, 1, (gather.spread, 2))
+    at_step(1, 4, (gather.cross, 2))
+    at_step(1, 7, (gather.close, 2))
     for k in range(3):
         before = [(scatter.line, k - 1, 1)] if k else []
         at_step(k + 1, 0, *before, (scatter.diagonal, k, 0), (scatter.diagonal, k, 1))
         at_step(k + 1, 1, (scatter.across, k, 0))
-        at_step(k + 1, 2, (scatter.across, k, 1))
+        at_step(k + 1, 4, (scatter.across, k, 1))
         at_step(k + 1, 6, (scatter.line, k, 0))
+    at_step(3, last, (scatter.line, 2, 1))
 
     back = jnp.where(chunk == 0, BACK[0], jnp.where(chunk == 1, BACK[1], jnp.where(chunk == 2, BACK[2], BACK[3])))
     first = p.at()[0] * experts
@@ -884,7 +910,6 @@
     @pl.when((chunk == 3) & (e == last))
     def _():
         probs.start()
-        scatter.line(2, 1)
         scatter.diagonal(3, 0)
         scatter.diagonal(3, 1)
         probs.over_x()
@@ -1096,8 +1121,9 @@
             [query_raw_grad, key_raw_grad, value_grad.reshape(length, cols)], axis=1
         ).astype(bf16)
         partial = dot(projected_grad, self.w_cols, ((1,), (1,)))
-        attn_gain_grad = jnp.sum(partial * self.first_normal, axis=0)
-        in_grad = dot(self.normed, projected_grad, ((0,), (0,))).astype(bf16)
+        in_grad = lax.optimization_barrier(dot(self.normed, projected_grad, ((0,), (0,))).astype(bf16))
+        terms = in_grad.astype(f32) * self.w_cols.astype(f32)
+        attn_gain_grad = jnp.sum(terms, axis=1) / self.gains_all[0]
         own = width // (seq * batch)
 
         lane = jnp.arange(router_grad.shape[1])

time: 718 us -> 713 us (level)
  other arithmetic: 20.7 us -> 30 us
    pallas_call x1, Pallas kernels: 263 us -> 255 us  [mixture_all(): pl.pallas_call(mixture_kernel, name='mixture', grid=(4, experts), out_sha...]
  transfers between devices with their start and end apart: 2 -> 2, of which waited for: 1 -> 1; matrix products, arithmetic and copies ran while one was open for 4% -> 5% of each run, Pallas kernels for 34% -> 34%
where the time goes in v5:
time: 713 us; the launch traced here: 705 us
  Pallas kernels  584 us (82%)
  matrix products  42.3 us (6%)
  other arithmetic  30 us (4%)
  waiting for transfers between devices  16.9 us (2%)
  local copies, waits for them, and re-layouts  16.4 us (2%)
  between operations  15.1 us (2%)
    pallas_call x1, Pallas kernels, mixture_all(): pl.pallas_call(mixture_kernel, name='mixture', grid=(4, experts), out_sha...  255 us
    pallas_call x1, Pallas kernels, gather_first(): call(gather_first_kernel, 'gather_first', collective_id, (struct((8,) + h...  132 us
    pallas_call x1, Pallas kernels, scatter_last(): call(scatter_last_kernel, 'scatter_last', collective_id, (struct(nb, f32)...  79 us
    pallas_call x1, Pallas kernels, weights_all(): pl.pallas_call(weights_kernel, name='weights', grid=(experts,), out_shape...  50.9 us
    pallas_call x1, Pallas kernels, scatter_seq(): call(scatter_seq_kernel, 'scatter_seq', collective_id, jax.ShapeDtypeStru...  46.4 us
    pallas_call x2, Pallas kernels, sum_seq(): call(sum_seq_kernel, 'sum_seq', collective_id, jax.ShapeDtypeStruct(x.sha...  20.7 us
    dot_general x6, matrix products, dot(): return lax.dot_general(a, b, (dims, ((), ())), preferred_element_type=f32)  19.7 us
    all_gather x1, waiting for transfers between devices, back(): grad_all = lax.all_gather(middle_low, 'seq', axis=0, tiled=True)  16.2 us
  transfers between devices with their start and end apart: 2, of which 1 were waited for; matrix products, arithmetic and copies ran while one was open for 5% of the time, Pallas kernels for 34%

profile of v5, /device:TPU:0, one launch (start us, length us, event | category | flops | bytes accessed | tf_op | source)
XLA Modules:
  0.0 705.0 jit_solution(12793754749320284761)
XLA Ops:
  7.3 0.7 all-gather.6.cloned.1.call-update
  8.0 1.3 copy.65
  9.3 0.4 copy.67
  9.7 0.9 reshape.366.wi_ref
  11.1 132.0 %gather_first.1 = (bf16[8,128,2048]{2,1,0:T(8,128)(2,1)S(1)}, bf16[8,4,64,768]{3,2,1,0:T(8,128)(2,1)S(1)}, bf16[4,64,2048]{2,1,0:T(8,128)(2,1)S(1)}, s32[32,16,128]{2,1,0:T(8,128)S(1)}, bf16[32,64,128]{2,1,0:T(8,128)(2,1)S(1)}) custom-call(bf16[128,2048]{1,0:T(8,128)(2,1)S(1)} %bitcast.141, bf16[8,64,768]{2,1,0:T(8,128)(2,1)S(1)} %reshape.366.wi_ref, ...), custom_call_target="tpu_custom_call" | custom-call | tf_op jit(solution)/shard_map/gather_first/pallas_call | solution.py:207
  143.2 1.4 slice_convert_fusion.1
  144.6 0.9 slice_reduce_fusion
  145.5 0.9 multiply_reduce_fusion
  146.4 1.0 multiply_convert_fusion.1
  147.5 3.6 fusion.63
  151.4 13.9 %sum_seq.2 = f32[2,8,128]{2,1,0:T(8,128)S(1)} custom-call(f32[2,8,128]{2,1,0:T(8,128)S(1)} %pad_maximum_fusion.4.x_ref), custom_call_target="tpu_custom_call" | custom-call | tf_op jit(solution)/shard_map/sum_seq/pallas_call | solution.py:296
  165.3 0.7 slice.97.routes_ref
  166.0 1.1 dynamic-slice_bitcast_fusion
  167.0 0.3 slice_reduce_fusion.2
  167.4 3.1 broadcast_multiply_fusion.3
  170.6 0.2 fusion.37
  170.8 0.3 slice_negate_fusion.2
  171.1 0.6 fusion.30
  171.7 0.6 fusion.10
  172.4 1.9 fusion.5
  174.3 2.0 fusion.2
  176.3 1.2 copy-done.16
  177.5 3.6 fusion.61
  181.1 1.3 convolution_convert_fusion
  182.4 46.4 %scatter_seq.1 = f32[128,2048]{1,0:T(8,128)S(1)} custom-call(bf16[8,128,2048]{2,1,0:T(8,128)(2,1)S(1)} %bitcast.140), custom_call_target="tpu_custom_call" | custom-call | tf_op jit(solution)/shard_map/scatter_seq/pallas_call | solution.py:265
  228.8 0.9 copy.64
  229.7 0.3 multiply_reduce_fusion.7
  230.0 1.0 copy-done.10
  231.2 0.4 fusion.62
  231.6 0.4 copy-done.17
  232.0 255.3 %mixture.1 = (bf16[32,128,2048]{2,1,0:T(8,128)(2,1)}, bf16[4,8,256,2048]{3,2,1,0:T(8,128)(2,1)}, bf16[4,8,256,2048]{3,2,1,0:T(8,128)(2,1)}, bf16[4,8,3,256,256]{...) custom-call(s32[32,8,128]{2,1,0:T(8,128)} %slice.97.routes_ref, ...), custom_call_target="tpu_custom_call" | custom-call | tf_op jit(solution)/shard_map/mixture/pallas_call | solution.py:936
  487.3 0.9 fusion.42
  488.2 0.8 fusion.44
  489.0 2.1 multiply_reduce_fusion.2
  491.1 1.0 copy-done.15
  492.1 1.2 fusion.60
  493.4 5.2 fusion.1
  498.8 0.3 fusion.45
  499.1 50.9 %weights.1 = f32[8,3,2048,256]{3,2,1,0:T(8,128)} custom-call(bf16[4,8,256,2048]{3,2,1,0:T(8,128)(2,1)} %get-tuple-element.34.xs_ref, bf16[4,8,256,2048]{3,2,1,0:T(8,128)(2,1)} %get-tuple-element.35.gs_ref, bf16[4,8,3,256,256]{4,3,2,1,0:T(8,128)(2,1)} %get-tuple-element.36.st_ref), custom_call_target="tpu_custom_call" | custom-call | flops 25769803776 | bytes 130023424 | tf_op jit(solution)/shard_map/weights/pallas_call | solution.py:998
  550.1 16.2 %all-gather.4.cloned.1.call-done = bf16[1024,2048]{1,0:T(8,128)(2,1)} async-done(((bf16[128,2048]{1,0:T(8,128)(2,1)}), bf16[1024,2048]{1,0:T(8,128)(2,1)}) %all-gather.4.cloned.1.call-update) | async-done | bytes 4194320 | tf_op jit(solution)/shard_map/all_gather | solution.py:1094
  566.2 3.9 multiply_reduce_fusion.5
  570.2 6.1 fusion.16
  576.3 3.4 multiply_convert_fusion
  579.8 1.5 convolution_bitcast_fusion
  581.3 0.9 broadcast_multiply_fusion.1
  582.4 0.9 copy-done.28
  583.2 0.5 maximum_subtract_fusion
  583.8 0.5 copy-done.14
  584.3 0.6 fusion.32
  584.9 6.8 sum_seq.3
  591.7 0.4 multiply_convert_fusion.3
  592.2 5.1 convolution_convert_fusion.1
  597.2 4.9 convolution_convert_fusion.2
  602.3 3.8 multiply_reduce_fusion.1
  606.2 1.2 select_add_fusion.sm_ref
  607.5 3.4 convolution_convert_fusion.3
  611.0 79.0 %scatter_last.1 = (f32[128,2048]{1,0:T(8,128)S(1)}, f32[64,6144]{1,0:T(8,128)S(1)}, f32[64,2048]{1,0:T(8,128)S(1)}, f32[64,128]{1,0:T(8,128)S(1)}) custom-call(bf16[8,128,2048]{2,1,0:T(8,128)(2,1)} %bitcast.163, bf16[8,2,2,64,768]{4,3,2,1,0:T(8,128)(2,1)} %bitcast.154, bf16[2,2,64,2048]{3,2,1,0:T(8,128)(2,1)S(1)} %bitcast.148, ...), custom_call_target="tpu_custom_call" | custom-call | tf_op jit(solution)/shard_map/scatter_last/pallas_call | solution.py:416
  689.9 0.8 copy-done.7
  690.7 0.3 fusion.21
  691.1 0.7 copy.54
  691.8 3.7 fusion.25
  695.4 1.1 copy.71
  696.6 0.8 copy.72
  697.4 0.6 copy.73
  (116 shorter events, 2.1 us)
Async XLA Ops:
  7.2 3.6 copy-start.35
  7.2 3.8 copy-start.36
  7.2 3.8 copy-start.34
  7.2 3.8 copy-start.33
  7.2 3.9 copy-start.1
  7.2 3.9 copy-start.9
  7.2 224.4 %all-gather.6.cloned.1.call-start = ((), (), s32[]{:S(2)}) async-start(), calls=%async_computation.1 | async-start | bytes 17301504 | tf_op jit(solution)/shard_map/all_gather | solution.py:1367
  8.0 558.3 %all-gather.4.cloned.1.call-start = ((), (), s32[]{:S(2)}) async-start(), calls=%async_computation | async-start | bytes 4718592 | tf_op jit(solution)/shard_map/all_gather | solution.py:1094
  143.2 3.2 copy-start.4
  143.2 3.2 copy-start
  143.2 4.3 copy-start.2
  151.1 14.2 %copy-start.12 = (f32[1024,768]{0,1:T(8,128)}, f32[1024,768]{0,1:T(8,128)S(1)}, u32[]{:S(2)}) copy-start(f32[1024,768]{0,1:T(8,128)S(1)} %fusion.63) | copy-start | bytes 9437188
  151.1 25.2 %copy-start.31 = (bf16[1024,256]{0,1:T(8,128)(2,1)}, bf16[1024,256]{0,1:T(8,128)(2,1)S(1)}, u32[]{:S(2)}) copy-start(bf16[1024,256]{0,1:T(8,128)(2,1)S(1)} %slice.170) | copy-start | bytes 1572868
  165.9 4.6 copy-start.13
  171.7 2.6 copy-start.24
  171.7 2.6 copy-start.26
  172.3 4.0 copy-start.21
  174.3 3.2 copy-start.16
  177.5 3.6 copy-start.5
  181.1 47.7 %copy-start.29 = (bf16[1024,2,128]{0,2,1:T(8,128)(2,1)}, bf16[1024,2,128]{0,2,1:T(8,128)(2,1)S(1)}, u32[]{:S(2)}) copy-start(bf16[1024,2,128]{0,2,1:T(8,128)(2,1)S(1)} %get-tuple-element.111) | copy-start | bytes 1572868
  230.0 1.0 copy-start.10
  231.2 0.8 copy-start.17
  487.3 4.8 copy-start.11
  487.3 4.8 copy-start.20
  491.1 1.0 copy-start.15
  493.4 5.3 copy-start.18
  499.1 67.1 %copy-start.6 = (bf16[4,64,2048]{2,1,0:T(8,128)(2,1)S(1)}, bf16[4,64,2048]{2,1,0:T(8,128)(2,1)}, u32[]{:S(2)}) copy-start(bf16[4,64,2048]{2,1,0:T(8,128)(2,1)} %copy-done.4) | copy-start | bytes 3145732
  566.2 3.9 copy-start.22
  566.2 10.1 %slice-start = ((s8[8388608]{0:T(1024)(128)(4,1)}), s8[4194304]{0:T(1024)(128)(4,1)S(1)}, s32[]{:S(2)}) async-start(s8[8388608]{0:T(1024)(128)(4,1)} %bitcast.159), calls=%async_computation.2 | async-start | bytes 8388608
  570.2 6.1 slice-start.1
  570.2 6.1 copy-start.32
  576.3 3.4 copy-start.27
  579.8 1.6 copy-start.19
  579.8 1.6 copy-start.25
  582.2 1.0 copy-start.28
  582.3 2.0 copy-start.14
  584.3 7.9 %copy-start.3 = (bf16[8,4,64,768]{3,2,1,0:T(8,128)(2,1)S(1)}, bf16[8,4,64,768]{3,2,1,0:T(8,128)(2,1)}, u32[]{:S(2)}) copy-start(bf16[8,4,64,768]{3,2,1,0:T(8,128)(2,1)} %copy-done.2) | copy-start | bytes 9437188
  592.2 5.1 copy-start.23
  602.3 5.2 copy-start.30
  689.9 0.8 copy-start.7
  691.8 4.8 copy-start.8
Sparse Core Ops, SparseCore 0:
  10.9 169.1 all-gather.5
  493.4 72.7 all-gather.3
